TPU v7x, 32 devices: a whole 2x2x4 slice. The times are simulated.
32 devices in a mesh: wide: 16 (over z, y, x), narrow: 2 (over core).
Axes of the slice: x: 2, y: 2, z: 4, core: 2. Of those that a mesh axis runs over, the one named last changes fastest.
Arguments:
- rhs: float32 [256, 32, 128], P('wide', 'narrow'), may hold values from -4 to 4
- alpha: float32 [256, 32, 128], P('wide', 'narrow'), may hold values from 0.05 to 0.5
- beta: float32 [256, 32, 128], P('wide', 'narrow'), may hold values from 0.5 to 4
Outputs:
- solution: float32 [256, 32, 128], P('wide', 'narrow')
All inputs are finite; a program needn't handle non-finite values.
Results may differ from a plain program's by a relative error of at most 0.00002.
Values sent between devices are 32-bit elements; how exact they have to be, the bound alone decides.
No kernel may reach another device: no remote copies, remote signals or barrier semaphores. Data moves between devices by JAX's collectives and lax.ppermute only.
A program may use at most 64 MiB of HBM per device.

v0:
```python
import jax
import jax.numpy as jnp
from jax import lax
from jax.sharding import PartitionSpec as P

LEVELS = 6
SWEEPS = 2
BOTTOM = 6
AGG = 4096


OMEGA = 2.0 / 3.0


def from_behind(array, axis, by):
    peers = lax.axis_size(axis)
    pairs = [(i, i + by) for i in range(peers) if 0 <= i + by < peers]
    return lax.ppermute(array, axis, pairs)


def partner_2(value, axis, bit):
    mask = 2**bit
    pairs = [(source, source ^ mask) for source in range(lax.axis_size(axis))]
    return lax.ppermute(value, axis, pairs)


def neighbours(extended):
    centre = extended[1:-1, 1:-1]
    padded_y = jnp.pad(centre, ((0, 0), (0, 0), (1, 1)))
    return (
        extended[:-2, 1:-1],
        extended[2:, 1:-1],
        extended[1:-1, :-2],
        extended[1:-1, 2:],
        padded_y[:, :, :-2],
        padded_y[:, :, 2:],
    )


def level_setup(alpha_grid, beta_ext, factor):
    beta_grid = beta_ext[1:-1, 1:-1]
    couple = tuple((0.5 * (beta_grid + other_cell) for other_cell in neighbours(beta_ext)))
    diagonal = alpha_grid + factor * (
        couple[0] + couple[1] + couple[2] + couple[3] + couple[4] + couple[5]
    )
    return (couple, diagonal)


def apply_operator(extended, couple, diagonal, factor):
    nearby = neighbours(extended)
    total = couple[0] * nearby[0] + couple[1] * nearby[1] + couple[2] * nearby[2]
    total = total + couple[3] * nearby[3] + couple[4] * nearby[4] + couple[5] * nearby[5]
    return diagonal * extended[1:-1, 1:-1] - factor * total


def relax_once(iterate, extended, source, couple, diagonal, factor):
    return (
        iterate + OMEGA * (source - apply_operator(extended, couple, diagonal, factor)) / diagonal
    )


def restrict(grid_field):
    half_x = grid_field.shape[0] // 2
    half_z = grid_field.shape[1] // 2
    half_y = grid_field.shape[2] // 2
    return grid_field.reshape(half_x, 2, half_z, 2, half_y, 2).sum(axis=(1, 3, 5)) * 0.125


def prolong(grid_field):
    return jnp.repeat(jnp.repeat(jnp.repeat(grid_field, 2, axis=0), 2, axis=1), 2, axis=2)


def border(grid_field, span_x, span_z):
    if span_z < lax.axis_size("narrow"):
        south_face = from_behind(grid_field[:, -1:], "narrow", span_z)
        north_face = from_behind(grid_field[:, :1], "narrow", -span_z)
    else:
        south_face = jnp.zeros_like(grid_field[:, :1])
        north_face = jnp.zeros_like(grid_field[:, :1])
    widened = jnp.concatenate([south_face, grid_field, north_face], 1)
    if span_x < lax.axis_size("wide"):
        below_face = from_behind(grid_field[-1:], "wide", span_x)
        above_face = from_behind(grid_field[:1], "wide", -span_x)
    else:
        below_face = jnp.zeros_like(grid_field[:1])
        above_face = jnp.zeros_like(grid_field[:1])
    below_face = jnp.pad(below_face, ((0, 0), (1, 1), (0, 0)))
    above_face = jnp.pad(above_face, ((0, 0), (1, 1), (0, 0)))
    return jnp.concatenate([below_face, widened, above_face], 0)


def arrive(bundle, span_x, span_z, bottom):
    n_wide = lax.axis_size("wide")
    n_narrow = lax.axis_size("narrow")
    history = []
    while span_x < n_wide or span_z < n_narrow:
        cell_count = bundle.shape[1] * bundle.shape[2] * bundle.shape[3]
        uneven_x = not bottom and bundle.shape[1] % 2 == 1
        uneven_z = not bottom and bundle.shape[2] % 2 == 1
        if not (uneven_x or uneven_z or cell_count < AGG):
            break
        along_x = span_x < n_wide and (
            uneven_x
            or (not uneven_z and (bundle.shape[1] <= bundle.shape[2] or span_z == n_narrow))
        )
        if along_x:
            bit_index = span_x.bit_length() - 1
            partner = partner_2(bundle, "wide", bit_index)
            upper_half = lax.axis_index("wide") // span_x % 2
            leading = jnp.where(upper_half == 1, partner, bundle)
            trailing = jnp.where(upper_half == 1, bundle, partner)
            bundle = jnp.concatenate([leading, trailing], 1)
            history.append(("along_x", span_x, 0))
            span_x = span_x * 2
        else:
            bit_index = span_z.bit_length() - 1
            partner = partner_2(bundle, "narrow", bit_index)
            upper_half = lax.axis_index("narrow") // span_z % 2
            leading = jnp.where(upper_half == 1, partner, bundle)
            trailing = jnp.where(upper_half == 1, bundle, partner)
            bundle = jnp.concatenate([leading, trailing], 2)
            history.append(("along_z", span_z, 0))
            span_z = span_z * 2
    return (bundle, span_x, span_z, history)


def depart(grid_field, history):
    for move_kind, lead_size, tail_size in reversed(history):
        if move_kind == "along_x":
            half_size = grid_field.shape[0] // 2
            offset = lax.axis_index("wide") // lead_size % 2 * half_size
            grid_field = lax.dynamic_slice_in_dim(grid_field, offset, half_size, 0)
        else:
            half_size = grid_field.shape[1] // 2
            offset = lax.axis_index("narrow") // lead_size % 2 * half_size
            grid_field = lax.dynamic_slice_in_dim(grid_field, offset, half_size, 1)
    return grid_field


def coarse_cycle(level_index, bundle, span_x, span_z):
    bottom = level_index == LEVELS - 1
    bundle, span_x, span_z, history = arrive(bundle, span_x, span_z, bottom)
    source = bundle[0]
    alpha_grid = bundle[1]
    beta_grid = bundle[2]
    factor = 0.25**level_index
    couple, diagonal = level_setup(alpha_grid, border(beta_grid, span_x, span_z), factor)
    iterate = OMEGA * source / diagonal
    if bottom:
        for sweep_index in range(BOTTOM - 1):
            iterate = relax_once(
                iterate, border(iterate, span_x, span_z), source, couple, diagonal, factor
            )
        return depart(iterate, history)
    iterate = relax_once(iterate, border(iterate, span_x, span_z), source, couple, diagonal, factor)
    extended = border(iterate, span_x, span_z)
    leftover = source - apply_operator(extended, couple, diagonal, factor)
    coarser = jnp.stack([restrict(leftover), restrict(alpha_grid), restrict(beta_grid)])
    correct = coarse_cycle(level_index + 1, coarser, span_x, span_z)
    iterate = iterate + prolong(correct)
    for sweep_index in range(SWEEPS):
        iterate = relax_once(
            iterate, border(iterate, span_x, span_z), source, couple, diagonal, factor
        )
    return depart(iterate, history)


def shards(rhs, alpha, beta):
    bundle = jnp.stack([rhs, alpha, beta])
    return coarse_cycle(0, bundle, 1, 1)


def solution(mesh):
    placed = (P("wide", "narrow", None), P("wide", "narrow", None), P("wide", "narrow", None))
    return jax.shard_map(
        shards, mesh=mesh, in_specs=placed, out_specs=P("wide", "narrow", None), check_vma=False
    )
```

profile of v0, /device:TPU:0, one launch (start us, length us, event | category | flops | bytes accessed | tf_op | source)
XLA Modules:
  0.0 241.4 jit_solution(3980276786655374151)
XLA Ops:
  0.9 2.4 collective-permute-start.1
  5.3 4.2 %collective-permute-start = (f32[1,16,128]{2,1,0:T(8,128)S(1)}, f32[1,16,128]{2,1,0:T(8,128)S(1)}, u32[]{:S(2)}, u32[]{:S(2)}) collective-permute-start(f32[1,16,128]{2,1,0:T(8,128)S(1)} %get-tuple-element.51), channel_id=1, source_target_pairs={{0,2},{2,4},{4,6},{6,8},{8,10},{10,12},{12,14},{14,16},{16,18},{18... | collective-permute-start | bytes 24584 | tf_op jit(solution)/shard_map/ppermute | solution.py:18
  9.5 1.4 collective-permute-start.3
  11.0 10.5 %reshape_squeeze_stack.5 = f32[8,2,8,2,64,2]{5,4,3,2,1,0:T(8,128)} reshape(f32[16,16,128]{2,1,0:T(8,128)} %param.5) | data formatting | bytes 262144 | tf_op jit(solution)/shard_map/reshape;squeeze;stack | solution.py:66
  21.5 4.0 %reduce_sum.158 = f32[8,8,64]{2,1,0:T(8,128)S(1)} reduce(f32[8,2,8,2,64,2]{5,4,3,2,1,0:T(8,128)} %reshape_squeeze_stack.5, f32[]{:T(128)} %constant.180.clone.1), dimensions={1,3,5}, to_apply=%region_2.3 | reduce | flops 28672 | bytes 147460 | tf_op jit(solution)/shard_map/reduce_sum | solution.py:66
  25.8 2.7 %collective-permute-start.5 = (f32[16,1,128]{2,0,1:T(8,128)S(1)}, f32[16,1,128]{2,0,1:T(8,128)S(1)}, u32[]{:S(2)}, u32[]{:S(2)}) collective-permute-start(f32[16,1,128]{2,0,1:T(8,128)S(1)} %bitcast.219), channel_id=1, source_target_pairs={{0,1},{2,3},{4,5},{6,7},{8,9},{10,11},{12,13},{14,15},{16,17},{18,... | collective-permute-start | bytes 24584 | tf_op jit(solution)/shard_map/ppermute | solution.py:18
  29.9 4.3 %collective-permute-start.4 = (f32[1,16,128]{2,1,0:T(8,128)S(1)}, f32[1,16,128]{2,1,0:T(8,128)S(1)}, u32[]{:S(2)}, u32[]{:S(2)}) collective-permute-start(f32[1,16,128]{2,1,0:T(8,128)S(1)} %get-tuple-element.46), channel_id=1, source_target_pairs={{0,2},{2,4},{4,6},{6,8},{8,10},{10,12},{12,14},{14,16},{16,18},{18... | collective-permute-start | bytes 24584 | tf_op jit(solution)/shard_map/ppermute | solution.py:18
  35.4 4.9 %collective-permute-start.12 = (f32[1,8,64]{2,1,0:T(8,128)S(1)}, f32[1,8,64]{2,1,0:T(8,128)S(1)}, u32[]{:S(2)}, u32[]{:S(2)}) collective-permute-start(f32[1,8,64]{2,1,0:T(8,128)S(1)} %get-tuple-element.84), channel_id=1, source_target_pairs={{0,2},{2,4},{4,6},{6,8},{8,10},{10,12},{12,14},{14,16},{16,18},{18... | collective-permute-start | bytes 6152 | tf_op jit(solution)/shard_map/ppermute | solution.py:18
  40.7 2.5 %collective-permute-start.9 = (f32[16,1,128]{2,0,1:T(8,128)S(1)}, f32[16,1,128]{2,0,1:T(8,128)S(1)}, u32[]{:S(2)}, u32[]{:S(2)}) collective-permute-start(f32[16,1,128]{2,0,1:T(8,128)S(1)} %bitcast.220), channel_id=1, source_target_pairs={{0,1},{2,3},{4,5},{6,7},{8,9},{10,11},{12,13},{14,15},{16,17},{18,... | collective-permute-start | bytes 24584 | tf_op jit(solution)/shard_map/ppermute | solution.py:18
  45.8 5.2 %collective-permute-start.8 = (f32[1,16,128]{2,1,0:T(8,128)S(1)}, f32[1,16,128]{2,1,0:T(8,128)S(1)}, u32[]{:S(2)}, u32[]{:S(2)}) collective-permute-start(f32[1,16,128]{2,1,0:T(8,128)S(1)} %get-tuple-element.42), channel_id=1, source_target_pairs={{0,2},{2,4},{4,6},{6,8},{8,10},{10,12},{12,14},{14,16},{16,18},{18... | collective-permute-start | bytes 24584 | tf_op jit(solution)/shard_map/ppermute | solution.py:18
  51.0 9.8 %reshape_squeeze_stack.4 = f32[8,2,8,2,64,2]{5,4,3,2,1,0:T(8,128)} reshape(f32[16,16,128]{2,1,0:T(8,128)S(1)} %copy-done.1) | data formatting | bytes 262144 | tf_op jit(solution)/shard_map/reshape;squeeze;stack | solution.py:66
  60.8 4.0 %reduce_sum.157 = f32[8,8,64]{2,1,0:T(8,128)S(1)} reduce(f32[8,2,8,2,64,2]{5,4,3,2,1,0:T(8,128)} %reshape_squeeze_stack.4, f32[]{:T(128)} %constant.180.clone.1), dimensions={1,3,5}, to_apply=%region_1.2 | reduce | flops 28672 | bytes 147460 | tf_op jit(solution)/shard_map/reduce_sum | solution.py:66
  64.8 2.7 %collective-permute-start.13 = (f32[8,1,64]{2,1,0:T(1,128)S(1)}, f32[8,1,64]{2,1,0:T(1,128)S(1)}, u32[]{:S(2)}, u32[]{:S(2)}) collective-permute-start(f32[8,1,64]{2,1,0:T(1,128)S(1)} %get-tuple-element.86), channel_id=1, source_target_pairs={{0,1},{2,3},{4,5},{6,7},{8,9},{10,11},{12,13},{14,15},{16,17},{18,... | collective-permute-start | bytes 6152 | tf_op jit(solution)/shard_map/ppermute | solution.py:18
  70.4 9.8 %reshape.187 = f32[8,2,8,2,64,2]{5,4,3,2,1,0:T(8,128)} reshape(f32[16,16,128]{2,1,0:T(8,128)S(1)} %fusion.17) | data formatting | bytes 262144 | tf_op jit(solution)/shard_map/reshape | solution.py:66
  80.2 4.0 %reduce_sum.156 = f32[8,8,64]{2,1,0:T(8,128)S(1)} reduce(f32[8,2,8,2,64,2]{5,4,3,2,1,0:T(8,128)} %reshape.187, f32[]{:T(128)} %constant.180.clone.1), dimensions={1,3,5}, to_apply=%region_0.1 | reduce | flops 28672 | bytes 147460 | tf_op jit(solution)/shard_map/reduce_sum | solution.py:66
  84.4 5.2 %collective-permute-start.16 = (f32[1,8,64]{2,1,0:T(8,128)S(1)}, f32[1,8,64]{2,1,0:T(8,128)S(1)}, u32[]{:S(2)}, u32[]{:S(2)}) collective-permute-start(f32[1,8,64]{2,1,0:T(8,128)S(1)} %get-tuple-element.79), channel_id=1, source_target_pairs={{0,2},{2,4},{4,6},{6,8},{8,10},{10,12},{12,14},{14,16},{16,18},{18... | collective-permute-start | bytes 6152 | tf_op jit(solution)/shard_map/ppermute | solution.py:18
  89.6 2.7 %collective-permute-start.17 = (f32[8,1,64]{2,1,0:T(1,128)S(1)}, f32[8,1,64]{2,1,0:T(1,128)S(1)}, u32[]{:S(2)}, u32[]{:S(2)}) collective-permute-start(f32[8,1,64]{2,1,0:T(1,128)S(1)} %get-tuple-element.81), channel_id=1, source_target_pairs={{0,1},{2,3},{4,5},{6,7},{8,9},{10,11},{12,13},{14,15},{16,17},{18,... | collective-permute-start | bytes 6152 | tf_op jit(solution)/shard_map/ppermute | solution.py:18
  97.4 2.3 collective-permute-done.19
  99.9 5.0 %collective-permute-start.20 = (f32[1,8,64]{2,1,0:T(8,128)S(1)}, f32[1,8,64]{2,1,0:T(8,128)S(1)}, u32[]{:S(2)}, u32[]{:S(2)}) collective-permute-start(f32[1,8,64]{2,1,0:T(8,128)S(1)} %get-tuple-element.74), channel_id=1, source_target_pairs={{0,2},{2,4},{4,6},{6,8},{8,10},{10,12},{12,14},{14,16},{16,18},{18... | collective-permute-start | bytes 6152 | tf_op jit(solution)/shard_map/ppermute | solution.py:18
  104.8 1.9 collective-permute-start.21
  109.8 5.3 %collective-permute-done.23 = f32[1,8,64]{2,1,0:T(8,128)S(1)} collective-permute-done((f32[1,8,64]{2,1,0:T(8,128)S(1)}, f32[1,8,64]{2,1,0:T(8,128)S(1)}, u32[]{:S(2)}, u32[]{:S(2)}) %collective-permute-start.23) | collective-permute-done | bytes 2080 | tf_op jit(solution)/shard_map/ppermute | solution.py:18
  116.4 3.7 %collective-permute-start.24 = (f32[3,4,4,32]{3,2,1,0:T(4,128)S(1)}, f32[3,4,4,32]{3,2,1,0:T(4,128)S(1)}, u32[]{:S(2)}, u32[]{:S(2)}) collective-permute-start(f32[3,4,4,32]{3,2,1,0:T(4,128)S(1)} %pad_maximum_fusion.116), channel_id=1, source_target_pairs={{0,2},{2,0},{4,6},{6,4},{8,10},{10,8},{12,14},{14,12},{16,18},{18,... | collective-permute-start | bytes 18440 | tf_op jit(solution)/shard_map/ppermute | solution.py:24
  120.1 1.8 collective-permute-done.24
  123.4 4.1 %collective-permute-start.26 = (f32[3,8,8,32]{3,2,1,0:T(8,128)S(1)}, f32[3,8,8,32]{3,2,1,0:T(8,128)S(1)}, u32[]{:S(2)}, u32[]{:S(2)}) collective-permute-start(f32[3,8,8,32]{3,2,1,0:T(8,128)S(1)} %pad_maximum_fusion.50), channel_id=1, source_target_pairs={{0,4},{2,6},{4,0},{6,2},{8,12},{10,14},{12,8},{14,10},{16,20},{18,... | collective-permute-start | bytes 73736 | tf_op jit(solution)/shard_map/ppermute | solution.py:24
  127.5 3.1 %collective-permute-done.26 = f32[3,8,8,32]{3,2,1,0:T(8,128)S(1)} collective-permute-done((f32[3,8,8,32]{3,2,1,0:T(8,128)S(1)}, f32[3,8,8,32]{3,2,1,0:T(8,128)S(1)}, u32[]{:S(2)}, u32[]{:S(2)}) %collective-permute-start.26) | collective-permute-done | bytes 24608 | tf_op jit(solution)/shard_map/ppermute | solution.py:24
  130.6 3.5 %collective-permute-start.27 = (f32[1,8,32]{2,1,0:T(8,128)S(1)}, f32[1,8,32]{2,1,0:T(8,128)S(1)}, u32[]{:S(2)}, u32[]{:S(2)}) collective-permute-start(f32[1,8,32]{2,1,0:T(8,128)S(1)} %slice_bitcast_fusion.1), channel_id=1, source_target_pairs={{0,8},{2,10},{4,12},{6,14},{8,16},{10,18},{12,20},{14,22},{16,24},... | collective-permute-start | bytes 3080 | tf_op jit(solution)/shard_map/ppermute | solution.py:18
  136.3 3.4 %collective-permute-done.28 = f32[1,8,32]{2,1,0:T(8,128)S(1)} collective-permute-done((f32[1,8,32]{2,1,0:T(8,128)S(1)}, f32[1,8,32]{2,1,0:T(8,128)S(1)}, u32[]{:S(2)}, u32[]{:S(2)}) %collective-permute-start.28) | collective-permute-done | bytes 1056 | tf_op jit(solution)/shard_map/ppermute | solution.py:18
  139.9 3.5 %collective-permute-start.29 = (f32[1,8,32]{2,1,0:T(8,128)S(1)}, f32[1,8,32]{2,1,0:T(8,128)S(1)}, u32[]{:S(2)}, u32[]{:S(2)}) collective-permute-start(f32[1,8,32]{2,1,0:T(8,128)S(1)} %get-tuple-element.62), channel_id=1, source_target_pairs={{0,8},{2,10},{4,12},{6,14},{8,16},{10,18},{12,20},{14,22},{16,24},... | collective-permute-start | bytes 3080 | tf_op jit(solution)/shard_map/ppermute | solution.py:18
  143.4 1.5 collective-permute-start.30
  145.7 3.2 %collective-permute-done.30 = f32[1,8,32]{2,1,0:T(8,128)S(1)} collective-permute-done((f32[1,8,32]{2,1,0:T(8,128)S(1)}, f32[1,8,32]{2,1,0:T(8,128)S(1)}, u32[]{:S(2)}, u32[]{:S(2)}) %collective-permute-start.30) | collective-permute-done | bytes 1056 | tf_op jit(solution)/shard_map/ppermute | solution.py:18
  149.1 2.5 %collective-permute-start.31 = (f32[1,8,32]{2,1,0:T(8,128)S(1)}, f32[1,8,32]{2,1,0:T(8,128)S(1)}, u32[]{:S(2)}, u32[]{:S(2)}) collective-permute-start(f32[1,8,32]{2,1,0:T(8,128)S(1)} %get-tuple-element.60), channel_id=1, source_target_pairs={{0,8},{2,10},{4,12},{6,14},{8,16},{10,18},{12,20},{14,22},{16,24},... | collective-permute-start | bytes 3080 | tf_op jit(solution)/shard_map/ppermute | solution.py:18
  152.9 4.2 %collective-permute-done.32 = f32[1,8,32]{2,1,0:T(8,128)S(1)} collective-permute-done((f32[1,8,32]{2,1,0:T(8,128)S(1)}, f32[1,8,32]{2,1,0:T(8,128)S(1)}, u32[]{:S(2)}, u32[]{:S(2)}) %collective-permute-start.32) | collective-permute-done | bytes 1056 | tf_op jit(solution)/shard_map/ppermute | solution.py:18
  158.2 5.1 %collective-permute-done.33 = f32[3,8,4,16]{1,3,2,0:T(8,128)S(1)} collective-permute-done((f32[3,8,4,16]{1,3,2,0:T(8,128)S(1)}, f32[3,8,4,16]{1,3,2,0:T(8,128)S(1)}, u32[]{:S(2)}, u32[]{:S(2)}) %collective-permute-start.33) | collective-permute-done | bytes 6176 | tf_op jit(solution)/shard_map/ppermute | solution.py:24
  163.7 5.3 %collective-permute-done.34 = f32[3,16,4,16]{1,3,2,0:T(8,128)S(1)} collective-permute-done((f32[3,16,4,16]{1,3,2,0:T(8,128)S(1)}, f32[3,16,4,16]{1,3,2,0:T(8,128)S(1)}, u32[]{:S(2)}, u32[]{:S(2)}) %collective-permute-start.34) | collective-permute-done | bytes 12320 | tf_op jit(solution)/shard_map/ppermute | solution.py:24
  176.7 4.2 %collective-permute-done.36 = f32[1,8,32]{2,1,0:T(8,128)S(1)} collective-permute-done((f32[1,8,32]{2,1,0:T(8,128)S(1)}, f32[1,8,32]{2,1,0:T(8,128)S(1)}, u32[]{:S(2)}, u32[]{:S(2)}) %collective-permute-start.36) | collective-permute-done | bytes 1056 | tf_op jit(solution)/shard_map/ppermute | solution.py:18
  181.0 2.9 %collective-permute-start.37 = (f32[1,8,32]{2,1,0:T(8,128)S(1)}, f32[1,8,32]{2,1,0:T(8,128)S(1)}, u32[]{:S(2)}, u32[]{:S(2)}) collective-permute-start(f32[1,8,32]{2,1,0:T(8,128)S(1)} %get-tuple-element.56), channel_id=1, source_target_pairs={{0,8},{2,10},{4,12},{6,14},{8,16},{10,18},{12,20},{14,22},{16,24},... | collective-permute-start | bytes 3080 | tf_op jit(solution)/shard_map/ppermute | solution.py:18
  185.3 4.2 %collective-permute-done.38 = f32[1,8,32]{2,1,0:T(8,128)S(1)} collective-permute-done((f32[1,8,32]{2,1,0:T(8,128)S(1)}, f32[1,8,32]{2,1,0:T(8,128)S(1)}, u32[]{:S(2)}, u32[]{:S(2)}) %collective-permute-start.38) | collective-permute-done | bytes 1056 | tf_op jit(solution)/shard_map/ppermute | solution.py:18
  190.0 3.6 %collective-permute-start.39 = (f32[1,8,64]{2,1,0:T(8,128)S(1)}, f32[1,8,64]{2,1,0:T(8,128)S(1)}, u32[]{:S(2)}, u32[]{:S(2)}) collective-permute-start(f32[1,8,64]{2,1,0:T(8,128)S(1)} %get-tuple-element.70), channel_id=1, source_target_pairs={{0,2},{2,4},{4,6},{6,8},{8,10},{10,12},{12,14},{14,16},{16,18},{18... | collective-permute-start | bytes 6152 | tf_op jit(solution)/shard_map/ppermute | solution.py:18
  197.9 3.7 %collective-permute-done.42 = f32[1,8,64]{2,1,0:T(8,128)S(1)} collective-permute-done((f32[1,8,64]{2,1,0:T(8,128)S(1)}, f32[1,8,64]{2,1,0:T(8,128)S(1)}, u32[]{:S(2)}, u32[]{:S(2)}) %collective-permute-start.42) | collective-permute-done | bytes 2080 | tf_op jit(solution)/shard_map/ppermute | solution.py:18
  201.8 3.9 %collective-permute-start.43 = (f32[1,8,64]{2,1,0:T(8,128)S(1)}, f32[1,8,64]{2,1,0:T(8,128)S(1)}, u32[]{:S(2)}, u32[]{:S(2)}) collective-permute-start(f32[1,8,64]{2,1,0:T(8,128)S(1)} %get-tuple-element.66), channel_id=1, source_target_pairs={{0,2},{2,4},{4,6},{6,8},{8,10},{10,12},{12,14},{14,16},{16,18},{18... | collective-permute-start | bytes 6152 | tf_op jit(solution)/shard_map/ppermute | solution.py:18
  205.7 1.7 collective-permute-start.44
  210.5 3.7 %collective-permute-done.46 = f32[1,8,64]{2,1,0:T(8,128)S(1)} collective-permute-done((f32[1,8,64]{2,1,0:T(8,128)S(1)}, f32[1,8,64]{2,1,0:T(8,128)S(1)}, u32[]{:S(2)}, u32[]{:S(2)}) %collective-permute-start.46) | collective-permute-done | bytes 2080 | tf_op jit(solution)/shard_map/ppermute | solution.py:18
  215.3 2.0 collective-permute-start.48
  218.6 3.9 %collective-permute-start.47 = (f32[1,16,128]{2,1,0:T(8,128)S(1)}, f32[1,16,128]{2,1,0:T(8,128)S(1)}, u32[]{:S(2)}, u32[]{:S(2)}) collective-permute-start(f32[1,16,128]{2,1,0:T(8,128)S(1)} %get-tuple-element.38), channel_id=1, source_target_pairs={{0,2},{2,4},{4,6},{6,8},{8,10},{10,12},{12,14},{14,16},{16,18},{18... | collective-permute-start | bytes 24584 | tf_op jit(solution)/shard_map/ppermute | solution.py:18
  223.9 4.2 %collective-permute-done.50 = f32[1,16,128]{2,1,0:T(8,128)S(1)} collective-permute-done((f32[1,16,128]{2,1,0:T(8,128)S(1)}, f32[1,16,128]{2,1,0:T(8,128)S(1)}, u32[]{:S(2)}, u32[]{:S(2)}) %collective-permute-start.50) | collective-permute-done | bytes 8224 | tf_op jit(solution)/shard_map/ppermute | solution.py:18
  228.4 1.6 collective-permute-start.52
  231.3 3.7 %collective-permute-start.51 = (f32[1,16,128]{2,1,0:T(8,128)S(1)}, f32[1,16,128]{2,1,0:T(8,128)S(1)}, u32[]{:S(2)}, u32[]{:S(2)}) collective-permute-start(f32[1,16,128]{2,1,0:T(8,128)S(1)} %get-tuple-element.34), channel_id=1, source_target_pairs={{0,2},{2,4},{4,6},{6,8},{8,10},{10,12},{12,14},{14,16},{16,18},{18... | collective-permute-start | bytes 24584 | tf_op jit(solution)/shard_map/ppermute | solution.py:18
  236.4 4.2 %collective-permute-done.54 = f32[1,16,128]{2,1,0:T(8,128)S(1)} collective-permute-done((f32[1,16,128]{2,1,0:T(8,128)S(1)}, f32[1,16,128]{2,1,0:T(8,128)S(1)}, u32[]{:S(2)}, u32[]{:S(2)}) %collective-permute-start.54) | collective-permute-done | bytes 8224 | tf_op jit(solution)/shard_map/ppermute | solution.py:18
  (230 shorter events, 52.6 us)
Async XLA Ops:
  0.9 24.6 %collective-permute-start.1 = (f32[16,1,128]{2,0,1:T(8,128)S(1)}, f32[16,1,128]{2,0,1:T(8,128)S(1)}, u32[]{:S(2)}, u32[]{:S(2)}) collective-permute-start(f32[16,1,128]{2,0,1:T(8,128)S(1)} %bitcast.221), channel_id=1, source_target_pairs={{0,1},{2,3},{4,5},{6,7},{8,9},{10,11},{12,13},{14,15},{16,17},{18,... | collective-permute-start | bytes 24584 | tf_op jit(solution)/shard_map/ppermute | solution.py:18
  3.3 22.3 %collective-permute-start.2 = (f32[16,1,128]{2,0,1:T(8,128)S(1)}, f32[16,1,128]{2,0,1:T(8,128)S(1)}, u32[]{:S(2)}, u32[]{:S(2)}) collective-permute-start(f32[16,1,128]{2,0,1:T(8,128)S(1)} %bitcast.218), channel_id=1, source_target_pairs={{1,0},{3,2},{5,4},{7,6},{9,8},{11,10},{13,12},{15,14},{17,16},{19,... | collective-permute-start | bytes 24584 | tf_op jit(solution)/shard_map/ppermute | solution.py:18
  5.3 20.3 %collective-permute-start = (f32[1,16,128]{2,1,0:T(8,128)S(1)}, f32[1,16,128]{2,1,0:T(8,128)S(1)}, u32[]{:S(2)}, u32[]{:S(2)}) collective-permute-start(f32[1,16,128]{2,1,0:T(8,128)S(1)} %get-tuple-element.51), channel_id=1, source_target_pairs={{0,2},{2,4},{4,6},{6,8},{8,10},{10,12},{12,14},{14,16},{16,18},{18... | collective-permute-start | bytes 24584 | tf_op jit(solution)/shard_map/ppermute | solution.py:18
  9.5 16.0 %collective-permute-start.3 = (f32[1,16,128]{2,1,0:T(8,128)S(1)}, f32[1,16,128]{2,1,0:T(8,128)S(1)}, u32[]{:S(2)}, u32[]{:S(2)}) collective-permute-start(f32[1,16,128]{2,1,0:T(8,128)S(1)} %get-tuple-element.50), channel_id=1, source_target_pairs={{2,0},{4,2},{6,4},{8,6},{10,8},{12,10},{14,12},{16,14},{18,16},{20... | collective-permute-start | bytes 24584 | tf_op jit(solution)/shard_map/ppermute | solution.py:18
  25.8 14.6 %collective-permute-start.5 = (f32[16,1,128]{2,0,1:T(8,128)S(1)}, f32[16,1,128]{2,0,1:T(8,128)S(1)}, u32[]{:S(2)}, u32[]{:S(2)}) collective-permute-start(f32[16,1,128]{2,0,1:T(8,128)S(1)} %bitcast.219), channel_id=1, source_target_pairs={{0,1},{2,3},{4,5},{6,7},{8,9},{10,11},{12,13},{14,15},{16,17},{18,... | collective-permute-start | bytes 24584 | tf_op jit(solution)/shard_map/ppermute | solution.py:18
  28.6 11.8 %collective-permute-start.6 = (f32[16,1,128]{2,0,1:T(8,128)S(1)}, f32[16,1,128]{2,0,1:T(8,128)S(1)}, u32[]{:S(2)}, u32[]{:S(2)}) collective-permute-start(f32[16,1,128]{2,0,1:T(8,128)S(1)} %bitcast.217), channel_id=1, source_target_pairs={{1,0},{3,2},{5,4},{7,6},{9,8},{11,10},{13,12},{15,14},{17,16},{19,... | collective-permute-start | bytes 24584 | tf_op jit(solution)/shard_map/ppermute | solution.py:18
  29.9 10.5 %collective-permute-start.4 = (f32[1,16,128]{2,1,0:T(8,128)S(1)}, f32[1,16,128]{2,1,0:T(8,128)S(1)}, u32[]{:S(2)}, u32[]{:S(2)}) collective-permute-start(f32[1,16,128]{2,1,0:T(8,128)S(1)} %get-tuple-element.46), channel_id=1, source_target_pairs={{0,2},{2,4},{4,6},{6,8},{8,10},{10,12},{12,14},{14,16},{16,18},{18... | collective-permute-start | bytes 24584 | tf_op jit(solution)/shard_map/ppermute | solution.py:18
  34.1 6.3 %collective-permute-start.7 = (f32[1,16,128]{2,1,0:T(8,128)S(1)}, f32[1,16,128]{2,1,0:T(8,128)S(1)}, u32[]{:S(2)}, u32[]{:S(2)}) collective-permute-start(f32[1,16,128]{2,1,0:T(8,128)S(1)} %get-tuple-element.47), channel_id=1, source_target_pairs={{2,0},{4,2},{6,4},{8,6},{10,8},{12,10},{14,12},{16,14},{18,16},{20... | collective-permute-start | bytes 24584 | tf_op jit(solution)/shard_map/ppermute | solution.py:18
  35.4 48.8 %collective-permute-start.12 = (f32[1,8,64]{2,1,0:T(8,128)S(1)}, f32[1,8,64]{2,1,0:T(8,128)S(1)}, u32[]{:S(2)}, u32[]{:S(2)}) collective-permute-start(f32[1,8,64]{2,1,0:T(8,128)S(1)} %get-tuple-element.84), channel_id=1, source_target_pairs={{0,2},{2,4},{4,6},{6,8},{8,10},{10,12},{12,14},{14,16},{16,18},{18... | collective-permute-start | bytes 6152 | tf_op jit(solution)/shard_map/ppermute | solution.py:18
  40.7 24.1 %collective-permute-start.9 = (f32[16,1,128]{2,0,1:T(8,128)S(1)}, f32[16,1,128]{2,0,1:T(8,128)S(1)}, u32[]{:S(2)}, u32[]{:S(2)}) collective-permute-start(f32[16,1,128]{2,0,1:T(8,128)S(1)} %bitcast.220), channel_id=1, source_target_pairs={{0,1},{2,3},{4,5},{6,7},{8,9},{10,11},{12,13},{14,15},{16,17},{18,... | collective-permute-start | bytes 24584 | tf_op jit(solution)/shard_map/ppermute | solution.py:18
  43.2 24.4 %collective-permute-start.10 = (f32[16,1,128]{2,0,1:T(8,128)S(1)}, f32[16,1,128]{2,0,1:T(8,128)S(1)}, u32[]{:S(2)}, u32[]{:S(2)}) collective-permute-start(f32[16,1,128]{2,0,1:T(8,128)S(1)} %bitcast.216), channel_id=1, source_target_pairs={{1,0},{3,2},{5,4},{7,6},{9,8},{11,10},{13,12},{15,14},{17,16},{19,... | collective-permute-start | bytes 24584 | tf_op jit(solution)/shard_map/ppermute | solution.py:18
  44.5 24.4 %collective-permute-start.11 = (f32[1,16,128]{2,1,0:T(8,128)S(1)}, f32[1,16,128]{2,1,0:T(8,128)S(1)}, u32[]{:S(2)}, u32[]{:S(2)}) collective-permute-start(f32[1,16,128]{2,1,0:T(8,128)S(1)} %get-tuple-element.43), channel_id=1, source_target_pairs={{2,0},{4,2},{6,4},{8,6},{10,8},{12,10},{14,12},{16,14},{18,16},{20... | collective-permute-start | bytes 24584 | tf_op jit(solution)/shard_map/ppermute | solution.py:18
  45.8 24.4 %collective-permute-start.8 = (f32[1,16,128]{2,1,0:T(8,128)S(1)}, f32[1,16,128]{2,1,0:T(8,128)S(1)}, u32[]{:S(2)}, u32[]{:S(2)}) collective-permute-start(f32[1,16,128]{2,1,0:T(8,128)S(1)} %get-tuple-element.42), channel_id=1, source_target_pairs={{0,2},{2,4},{4,6},{6,8},{8,10},{10,12},{12,14},{14,16},{16,18},{18... | collective-permute-start | bytes 24584 | tf_op jit(solution)/shard_map/ppermute | solution.py:18
  64.8 19.4 %collective-permute-start.13 = (f32[8,1,64]{2,1,0:T(1,128)S(1)}, f32[8,1,64]{2,1,0:T(1,128)S(1)}, u32[]{:S(2)}, u32[]{:S(2)}) collective-permute-start(f32[8,1,64]{2,1,0:T(1,128)S(1)} %get-tuple-element.86), channel_id=1, source_target_pairs={{0,1},{2,3},{4,5},{6,7},{8,9},{10,11},{12,13},{14,15},{16,17},{18,... | collective-permute-start | bytes 6152 | tf_op jit(solution)/shard_map/ppermute | solution.py:18
  67.6 16.7 %collective-permute-start.14 = (f32[8,1,64]{2,1,0:T(1,128)S(1)}, f32[8,1,64]{2,1,0:T(1,128)S(1)}, u32[]{:S(2)}, u32[]{:S(2)}) collective-permute-start(f32[8,1,64]{2,1,0:T(1,128)S(1)} %get-tuple-element.85), channel_id=1, source_target_pairs={{1,0},{3,2},{5,4},{7,6},{9,8},{11,10},{13,12},{15,14},{17,16},{19,... | collective-permute-start | bytes 6152 | tf_op jit(solution)/shard_map/ppermute | solution.py:18
  68.9 15.4 %collective-permute-start.15 = (f32[1,8,64]{2,1,0:T(8,128)S(1)}, f32[1,8,64]{2,1,0:T(8,128)S(1)}, u32[]{:S(2)}, u32[]{:S(2)}) collective-permute-start(f32[1,8,64]{2,1,0:T(8,128)S(1)} %get-tuple-element.83), channel_id=1, source_target_pairs={{2,0},{4,2},{6,4},{8,6},{10,8},{12,10},{14,12},{16,14},{18,16},{20... | collective-permute-start | bytes 6152 | tf_op jit(solution)/shard_map/ppermute | solution.py:18
  84.4 13.0 %collective-permute-start.16 = (f32[1,8,64]{2,1,0:T(8,128)S(1)}, f32[1,8,64]{2,1,0:T(8,128)S(1)}, u32[]{:S(2)}, u32[]{:S(2)}) collective-permute-start(f32[1,8,64]{2,1,0:T(8,128)S(1)} %get-tuple-element.79), channel_id=1, source_target_pairs={{0,2},{2,4},{4,6},{6,8},{8,10},{10,12},{12,14},{14,16},{16,18},{18... | collective-permute-start | bytes 6152 | tf_op jit(solution)/shard_map/ppermute | solution.py:18
  89.6 7.9 %collective-permute-start.17 = (f32[8,1,64]{2,1,0:T(1,128)S(1)}, f32[8,1,64]{2,1,0:T(1,128)S(1)}, u32[]{:S(2)}, u32[]{:S(2)}) collective-permute-start(f32[8,1,64]{2,1,0:T(1,128)S(1)} %get-tuple-element.81), channel_id=1, source_target_pairs={{0,1},{2,3},{4,5},{6,7},{8,9},{10,11},{12,13},{14,15},{16,17},{18,... | collective-permute-start | bytes 6152 | tf_op jit(solution)/shard_map/ppermute | solution.py:18
  92.3 5.1 %collective-permute-start.18 = (f32[8,1,64]{2,1,0:T(1,128)S(1)}, f32[8,1,64]{2,1,0:T(1,128)S(1)}, u32[]{:S(2)}, u32[]{:S(2)}) collective-permute-start(f32[8,1,64]{2,1,0:T(1,128)S(1)} %get-tuple-element.82), channel_id=1, source_target_pairs={{1,0},{3,2},{5,4},{7,6},{9,8},{11,10},{13,12},{15,14},{17,16},{19,... | collective-permute-start | bytes 6152 | tf_op jit(solution)/shard_map/ppermute | solution.py:18
  93.6 6.1 %collective-permute-start.19 = (f32[1,8,64]{2,1,0:T(8,128)S(1)}, f32[1,8,64]{2,1,0:T(8,128)S(1)}, u32[]{:S(2)}, u32[]{:S(2)}) collective-permute-start(f32[1,8,64]{2,1,0:T(8,128)S(1)} %get-tuple-element.80), channel_id=1, source_target_pairs={{2,0},{4,2},{6,4},{8,6},{10,8},{12,10},{14,12},{16,14},{18,16},{20... | collective-permute-start | bytes 6152 | tf_op jit(solution)/shard_map/ppermute | solution.py:18
  99.9 9.5 %collective-permute-start.20 = (f32[1,8,64]{2,1,0:T(8,128)S(1)}, f32[1,8,64]{2,1,0:T(8,128)S(1)}, u32[]{:S(2)}, u32[]{:S(2)}) collective-permute-start(f32[1,8,64]{2,1,0:T(8,128)S(1)} %get-tuple-element.74), channel_id=1, source_target_pairs={{0,2},{2,4},{4,6},{6,8},{8,10},{10,12},{12,14},{14,16},{16,18},{18... | collective-permute-start | bytes 6152 | tf_op jit(solution)/shard_map/ppermute | solution.py:18
  104.8 4.5 %collective-permute-start.21 = (f32[8,1,64]{2,1,0:T(1,128)S(1)}, f32[8,1,64]{2,1,0:T(1,128)S(1)}, u32[]{:S(2)}, u32[]{:S(2)}) collective-permute-start(f32[8,1,64]{2,1,0:T(1,128)S(1)} %get-tuple-element.76), channel_id=1, source_target_pairs={{0,1},{2,3},{4,5},{6,7},{8,9},{10,11},{12,13},{14,15},{16,17},{18,... | collective-permute-start | bytes 6152 | tf_op jit(solution)/shard_map/ppermute | solution.py:18
  108.0 7.0 %collective-permute-start.23 = (f32[1,8,64]{2,1,0:T(8,128)S(1)}, f32[1,8,64]{2,1,0:T(8,128)S(1)}, u32[]{:S(2)}, u32[]{:S(2)}) collective-permute-start(f32[1,8,64]{2,1,0:T(8,128)S(1)} %get-tuple-element.75), channel_id=1, source_target_pairs={{2,0},{4,2},{6,4},{8,6},{10,8},{12,10},{14,12},{16,14},{18,16},{20... | collective-permute-start | bytes 6152 | tf_op jit(solution)/shard_map/ppermute | solution.py:18
  116.4 5.5 %collective-permute-start.24 = (f32[3,4,4,32]{3,2,1,0:T(4,128)S(1)}, f32[3,4,4,32]{3,2,1,0:T(4,128)S(1)}, u32[]{:S(2)}, u32[]{:S(2)}) collective-permute-start(f32[3,4,4,32]{3,2,1,0:T(4,128)S(1)} %pad_maximum_fusion.116), channel_id=1, source_target_pairs={{0,2},{2,0},{4,6},{6,4},{8,10},{10,8},{12,14},{14,12},{16,18},{18,... | collective-permute-start | bytes 18440 | tf_op jit(solution)/shard_map/ppermute | solution.py:24
  123.4 7.2 %collective-permute-start.26 = (f32[3,8,8,32]{3,2,1,0:T(8,128)S(1)}, f32[3,8,8,32]{3,2,1,0:T(8,128)S(1)}, u32[]{:S(2)}, u32[]{:S(2)}) collective-permute-start(f32[3,8,8,32]{3,2,1,0:T(8,128)S(1)} %pad_maximum_fusion.50), channel_id=1, source_target_pairs={{0,4},{2,6},{4,0},{6,2},{8,12},{10,14},{12,8},{14,10},{16,20},{18,... | collective-permute-start | bytes 73736 | tf_op jit(solution)/shard_map/ppermute | solution.py:24
  130.6 5.6 %collective-permute-start.27 = (f32[1,8,32]{2,1,0:T(8,128)S(1)}, f32[1,8,32]{2,1,0:T(8,128)S(1)}, u32[]{:S(2)}, u32[]{:S(2)}) collective-permute-start(f32[1,8,32]{2,1,0:T(8,128)S(1)} %slice_bitcast_fusion.1), channel_id=1, source_target_pairs={{0,8},{2,10},{4,12},{6,14},{8,16},{10,18},{12,20},{14,22},{16,24},... | collective-permute-start | bytes 3080 | tf_op jit(solution)/shard_map/ppermute | solution.py:18
  134.1 5.5 %collective-permute-start.28 = (f32[1,8,32]{2,1,0:T(8,128)S(1)}, f32[1,8,32]{2,1,0:T(8,128)S(1)}, u32[]{:S(2)}, u32[]{:S(2)}) collective-permute-start(f32[1,8,32]{2,1,0:T(8,128)S(1)} %slice_bitcast_fusion), channel_id=1, source_target_pairs={{8,0},{10,2},{12,4},{14,6},{16,8},{18,10},{20,12},{22,14},{24,16},... | collective-permute-start | bytes 3080 | tf_op jit(solution)/shard_map/ppermute | solution.py:18
  139.9 5.8 %collective-permute-start.29 = (f32[1,8,32]{2,1,0:T(8,128)S(1)}, f32[1,8,32]{2,1,0:T(8,128)S(1)}, u32[]{:S(2)}, u32[]{:S(2)}) collective-permute-start(f32[1,8,32]{2,1,0:T(8,128)S(1)} %get-tuple-element.62), channel_id=1, source_target_pairs={{0,8},{2,10},{4,12},{6,14},{8,16},{10,18},{12,20},{14,22},{16,24},... | collective-permute-start | bytes 3080 | tf_op jit(solution)/shard_map/ppermute | solution.py:18
  143.4 5.5 %collective-permute-start.30 = (f32[1,8,32]{2,1,0:T(8,128)S(1)}, f32[1,8,32]{2,1,0:T(8,128)S(1)}, u32[]{:S(2)}, u32[]{:S(2)}) collective-permute-start(f32[1,8,32]{2,1,0:T(8,128)S(1)} %get-tuple-element.63), channel_id=1, source_target_pairs={{8,0},{10,2},{12,4},{14,6},{16,8},{18,10},{20,12},{22,14},{24,16},... | collective-permute-start | bytes 3080 | tf_op jit(solution)/shard_map/ppermute | solution.py:18
  151.6 5.5 %collective-permute-start.32 = (f32[1,8,32]{2,1,0:T(8,128)S(1)}, f32[1,8,32]{2,1,0:T(8,128)S(1)}, u32[]{:S(2)}, u32[]{:S(2)}) collective-permute-start(f32[1,8,32]{2,1,0:T(8,128)S(1)} %get-tuple-element.61), channel_id=1, source_target_pairs={{8,0},{10,2},{12,4},{14,6},{16,8},{18,10},{20,12},{22,14},{24,16},... | collective-permute-start | bytes 3080 | tf_op jit(solution)/shard_map/ppermute | solution.py:18
  158.1 5.2 %collective-permute-start.33 = (f32[3,8,4,16]{1,3,2,0:T(8,128)S(1)}, f32[3,8,4,16]{1,3,2,0:T(8,128)S(1)}, u32[]{:S(2)}, u32[]{:S(2)}) collective-permute-start(f32[3,8,4,16]{1,3,2,0:T(8,128)S(1)} %pad_maximum_fusion.51), channel_id=1, source_target_pairs={{0,8},{2,10},{4,12},{6,14},{8,0},{10,2},{12,4},{14,6},{16,24},{18,... | collective-permute-start | bytes 18440 | tf_op jit(solution)/shard_map/ppermute | solution.py:24
  163.4 5.6 %collective-permute-start.34 = (f32[3,16,4,16]{1,3,2,0:T(8,128)S(1)}, f32[3,16,4,16]{1,3,2,0:T(8,128)S(1)}, u32[]{:S(2)}, u32[]{:S(2)}) collective-permute-start(f32[3,16,4,16]{1,3,2,0:T(8,128)S(1)} %pad_maximum_fusion.52), channel_id=1, source_target_pairs={{0,16},{2,18},{4,20},{6,22},{8,24},{10,26},{12,28},{14,30},{16,0},... | collective-permute-start | bytes 36872 | tf_op jit(solution)/shard_map/ppermute | solution.py:24
  175.3 5.5 %collective-permute-start.36 = (f32[1,8,32]{2,1,0:T(8,128)S(1)}, f32[1,8,32]{2,1,0:T(8,128)S(1)}, u32[]{:S(2)}, u32[]{:S(2)}) collective-permute-start(f32[1,8,32]{2,1,0:T(8,128)S(1)} %get-tuple-element.59), channel_id=1, source_target_pairs={{8,0},{10,2},{12,4},{14,6},{16,8},{18,10},{20,12},{22,14},{24,16},... | collective-permute-start | bytes 3080 | tf_op jit(solution)/shard_map/ppermute | solution.py:18
  181.0 4.3 %collective-permute-start.37 = (f32[1,8,32]{2,1,0:T(8,128)S(1)}, f32[1,8,32]{2,1,0:T(8,128)S(1)}, u32[]{:S(2)}, u32[]{:S(2)}) collective-permute-start(f32[1,8,32]{2,1,0:T(8,128)S(1)} %get-tuple-element.56), channel_id=1, source_target_pairs={{0,8},{2,10},{4,12},{6,14},{8,16},{10,18},{12,20},{14,22},{16,24},... | collective-permute-start | bytes 3080 | tf_op jit(solution)/shard_map/ppermute | solution.py:18
  184.0 5.5 %collective-permute-start.38 = (f32[1,8,32]{2,1,0:T(8,128)S(1)}, f32[1,8,32]{2,1,0:T(8,128)S(1)}, u32[]{:S(2)}, u32[]{:S(2)}) collective-permute-start(f32[1,8,32]{2,1,0:T(8,128)S(1)} %get-tuple-element.57), channel_id=1, source_target_pairs={{8,0},{10,2},{12,4},{14,6},{16,8},{18,10},{20,12},{22,14},{24,16},... | collective-permute-start | bytes 3080 | tf_op jit(solution)/shard_map/ppermute | solution.py:18
  190.0 7.5 %collective-permute-start.39 = (f32[1,8,64]{2,1,0:T(8,128)S(1)}, f32[1,8,64]{2,1,0:T(8,128)S(1)}, u32[]{:S(2)}, u32[]{:S(2)}) collective-permute-start(f32[1,8,64]{2,1,0:T(8,128)S(1)} %get-tuple-element.70), channel_id=1, source_target_pairs={{0,2},{2,4},{4,6},{6,8},{8,10},{10,12},{12,14},{14,16},{16,18},{18... | collective-permute-start | bytes 6152 | tf_op jit(solution)/shard_map/ppermute | solution.py:18
  196.2 5.5 %collective-permute-start.42 = (f32[1,8,64]{2,1,0:T(8,128)S(1)}, f32[1,8,64]{2,1,0:T(8,128)S(1)}, u32[]{:S(2)}, u32[]{:S(2)}) collective-permute-start(f32[1,8,64]{2,1,0:T(8,128)S(1)} %get-tuple-element.71), channel_id=1, source_target_pairs={{2,0},{4,2},{6,4},{8,6},{10,8},{12,10},{14,12},{16,14},{18,16},{20... | collective-permute-start | bytes 6152 | tf_op jit(solution)/shard_map/ppermute | solution.py:18
  201.8 8.3 %collective-permute-start.43 = (f32[1,8,64]{2,1,0:T(8,128)S(1)}, f32[1,8,64]{2,1,0:T(8,128)S(1)}, u32[]{:S(2)}, u32[]{:S(2)}) collective-permute-start(f32[1,8,64]{2,1,0:T(8,128)S(1)} %get-tuple-element.66), channel_id=1, source_target_pairs={{0,2},{2,4},{4,6},{6,8},{8,10},{10,12},{12,14},{14,16},{16,18},{18... | collective-permute-start | bytes 6152 | tf_op jit(solution)/shard_map/ppermute | solution.py:18
  205.7 4.4 %collective-permute-start.44 = (f32[8,1,64]{2,1,0:T(1,128)S(1)}, f32[8,1,64]{2,1,0:T(1,128)S(1)}, u32[]{:S(2)}, u32[]{:S(2)}) collective-permute-start(f32[8,1,64]{2,1,0:T(1,128)S(1)} %get-tuple-element.68), channel_id=1, source_target_pairs={{0,1},{2,3},{4,5},{6,7},{8,9},{10,11},{12,13},{14,15},{16,17},{18,... | collective-permute-start | bytes 6152 | tf_op jit(solution)/shard_map/ppermute | solution.py:18
  208.8 5.5 %collective-permute-start.46 = (f32[1,8,64]{2,1,0:T(8,128)S(1)}, f32[1,8,64]{2,1,0:T(8,128)S(1)}, u32[]{:S(2)}, u32[]{:S(2)}) collective-permute-start(f32[1,8,64]{2,1,0:T(8,128)S(1)} %get-tuple-element.67), channel_id=1, source_target_pairs={{2,0},{4,2},{6,4},{8,6},{10,8},{12,10},{14,12},{16,14},{18,16},{20... | collective-permute-start | bytes 6152 | tf_op jit(solution)/shard_map/ppermute | solution.py:18
  215.3 8.6 %collective-permute-start.48 = (f32[16,1,128]{2,0,1:T(8,128)S(1)}, f32[16,1,128]{2,0,1:T(8,128)S(1)}, u32[]{:S(2)}, u32[]{:S(2)}) collective-permute-start(f32[16,1,128]{2,0,1:T(8,128)S(1)} %bitcast.224), channel_id=1, source_target_pairs={{0,1},{2,3},{4,5},{6,7},{8,9},{10,11},{12,13},{14,15},{16,17},{18,... | collective-permute-start | bytes 24584 | tf_op jit(solution)/shard_map/ppermute | solution.py:18
  217.3 6.5 %collective-permute-start.49 = (f32[16,1,128]{2,0,1:T(8,128)S(1)}, f32[16,1,128]{2,0,1:T(8,128)S(1)}, u32[]{:S(2)}, u32[]{:S(2)}) collective-permute-start(f32[16,1,128]{2,0,1:T(8,128)S(1)} %bitcast.222), channel_id=1, source_target_pairs={{1,0},{3,2},{5,4},{7,6},{9,8},{11,10},{13,12},{15,14},{17,16},{19,... | collective-permute-start | bytes 24584 | tf_op jit(solution)/shard_map/ppermute | solution.py:18
  218.6 5.3 %collective-permute-start.47 = (f32[1,16,128]{2,1,0:T(8,128)S(1)}, f32[1,16,128]{2,1,0:T(8,128)S(1)}, u32[]{:S(2)}, u32[]{:S(2)}) collective-permute-start(f32[1,16,128]{2,1,0:T(8,128)S(1)} %get-tuple-element.38), channel_id=1, source_target_pairs={{0,2},{2,4},{4,6},{6,8},{8,10},{10,12},{12,14},{14,16},{16,18},{18... | collective-permute-start | bytes 24584 | tf_op jit(solution)/shard_map/ppermute | solution.py:18
  222.6 5.5 %collective-permute-start.50 = (f32[1,16,128]{2,1,0:T(8,128)S(1)}, f32[1,16,128]{2,1,0:T(8,128)S(1)}, u32[]{:S(2)}, u32[]{:S(2)}) collective-permute-start(f32[1,16,128]{2,1,0:T(8,128)S(1)} %get-tuple-element.39), channel_id=1, source_target_pairs={{2,0},{4,2},{6,4},{8,6},{10,8},{12,10},{14,12},{16,14},{18,16},{20... | collective-permute-start | bytes 24584 | tf_op jit(solution)/shard_map/ppermute | solution.py:18
  228.4 7.9 %collective-permute-start.52 = (f32[16,1,128]{2,0,1:T(8,128)S(1)}, f32[16,1,128]{2,0,1:T(8,128)S(1)}, u32[]{:S(2)}, u32[]{:S(2)}) collective-permute-start(f32[16,1,128]{2,0,1:T(8,128)S(1)} %bitcast.225), channel_id=1, source_target_pairs={{0,1},{2,3},{4,5},{6,7},{8,9},{10,11},{12,13},{14,15},{16,17},{18,... | collective-permute-start | bytes 24584 | tf_op jit(solution)/shard_map/ppermute | solution.py:18
  230.0 6.3 %collective-permute-start.53 = (f32[16,1,128]{2,0,1:T(8,128)S(1)}, f32[16,1,128]{2,0,1:T(8,128)S(1)}, u32[]{:S(2)}, u32[]{:S(2)}) collective-permute-start(f32[16,1,128]{2,0,1:T(8,128)S(1)} %bitcast.223), channel_id=1, source_target_pairs={{1,0},{3,2},{5,4},{7,6},{9,8},{11,10},{13,12},{15,14},{17,16},{19,... | collective-permute-start | bytes 24584 | tf_op jit(solution)/shard_map/ppermute | solution.py:18
  231.3 5.1 %collective-permute-start.51 = (f32[1,16,128]{2,1,0:T(8,128)S(1)}, f32[1,16,128]{2,1,0:T(8,128)S(1)}, u32[]{:S(2)}, u32[]{:S(2)}) collective-permute-start(f32[1,16,128]{2,1,0:T(8,128)S(1)} %get-tuple-element.34), channel_id=1, source_target_pairs={{0,2},{2,4},{4,6},{6,8},{8,10},{10,12},{12,14},{14,16},{16,18},{18... | collective-permute-start | bytes 24584 | tf_op jit(solution)/shard_map/ppermute | solution.py:18
  235.0 5.5 %collective-permute-start.54 = (f32[1,16,128]{2,1,0:T(8,128)S(1)}, f32[1,16,128]{2,1,0:T(8,128)S(1)}, u32[]{:S(2)}, u32[]{:S(2)}) collective-permute-start(f32[1,16,128]{2,1,0:T(8,128)S(1)} %get-tuple-element.35), channel_id=1, source_target_pairs={{2,0},{4,2},{6,4},{8,6},{10,8},{12,10},{14,12},{16,14},{18,16},{20... | collective-permute-start | bytes 24584 | tf_op jit(solution)/shard_map/ppermute | solution.py:18
  (10 other events, 69.2 us)
where the time goes:
time: 243 us; the launch traced here: 241 us
  starting transfers between devices  120 us (49%)
  waiting for transfers between devices  60.5 us (25%)
  local copies, waits for them, and re-layouts  40.3 us (17%)
  other arithmetic  19.2 us (8%)
    ppermute x50, starting transfers between devices, from_behind(): return lax.ppermute(array, axis, pairs)  112 us
    ppermute x50, waiting for transfers between devices, from_behind(): return lax.ppermute(array, axis, pairs)  44 us
    another operation x6, local copies, waits for them, and re-layouts, restrict(): grid_field.reshape(half_x, 2, half_z, 2, half_y, 2).sum(axis=(1, 3, 5))  22.1 us
    ppermute x5, waiting for transfers between devices, partner_2(): return lax.ppermute(value, axis, pairs)  16.5 us
    reduce_sum x17, other arithmetic, restrict(): grid_field.reshape(half_x, 2, half_z, 2, half_y, 2).sum(axis=(1, 3, 5))  13.7 us
    reshape x4, local copies, waits for them, and re-layouts, restrict(): grid_field.reshape(half_x, 2, half_z, 2, half_y, 2).sum(axis=(1, 3, 5))  11.7 us
    ppermute x5, starting transfers between devices, partner_2(): return lax.ppermute(value, axis, pairs)  8.08 us
  transfers between devices with their start and end apart: 55, of which 19 were waited for; matrix products, arithmetic and copies ran while one was open for 20% of the time, Pallas kernels for 0%

commit v1 on v0

v1 whole, which is shorter than its diff:
```python
import functools
import math

import jax
import jax.numpy as jnp
from jax import lax
from jax.experimental import pallas as pl
from jax.experimental.pallas import tpu as pltpu
from jax.sharding import PartitionSpec as P

LEVELS = 6
BOTTOM = 6
OMEGA = 2.0 / 3.0
LANES = 128
H = 11
H1 = 5
LONGEST = 2048


def short(n, rows):
    return n * rows <= LONGEST


def each(n, rows, body):
    if short(n, rows):
        for i in range(n):
            body(i)
    else:

        def step(i, _):
            body(i)
            return 0

        lax.fori_loop(0, n, step, 0)


F, W, CX, CZ, CY, U, A, B, V = range(9)
KEPT = 6


class Level:
    def __init__(self, ref, zw, index, base=0):
        self.ref, self.zw, self.base = ref, zw, base
        self.d, self.s = 2**index, 0.25**index

    def at(self, plane):
        return Level.moved(self, self.base + plane * self.zw)

    def moved(self, base):
        other = Level(self.ref, self.zw, 0, base)
        other.d, other.s = self.d, self.s
        return other

    def get(self, q, r, n):
        return self.ref[q, pl.ds(r, n), :]

    def put(self, q, r, value):
        self.ref[q, pl.ds(r, value.shape[0]), :] = value

    def setup(self, first, count, chunk, valid=None):
        zw, d = self.zw, self.d
        n = chunk * zw
        row = lax.broadcasted_iota(jnp.int32, (n, LANES), 0) % zw
        lane = lax.broadcasted_iota(jnp.int32, (n, LANES), 1)
        z0, z1, y0, y1 = row == 0, row == zw - 1, lane < d, lane >= LANES - d
        hs = 0.5 * self.s

        def body(i):
            p = first + i * chunk
            r = self.base + p * zw
            b = self.get(B, r, n)
            bxp = self.get(B, r + zw, n)
            bxm = self.get(B, r - zw, n)
            bzp = jnp.where(z1, 0.0, self.get(B, r + 1, n))
            bzm = jnp.where(z0, 0.0, self.get(B, r - 1, n))
            byp = jnp.where(y1, 0.0, pltpu.roll(b, LANES - d, 1))
            bym = jnp.where(y0, 0.0, pltpu.roll(b, d, 1))
            dg = self.get(A, r, n) + hs * (6.0 * b + bxp + bxm + bzp + bzm + byp + bym)
            w = OMEGA / dg
            if valid is not None:
                w = jnp.where(valid(p), w, 0.0)
            self.put(A, r, dg)
            self.put(W, r, w)
            self.put(U, r, w * self.get(F, r, n))
            self.put(CX, r, hs * (b + bxp))
            self.put(CZ, r, jnp.where(z1, 0.0, hs * (b + bzp)))
            self.put(CY, r, jnp.where(y1, 0.0, hs * (b + byp)))

        assert count % chunk == 0
        each(count // chunk, n, body)

    def first_cx(self, plane):
        r = self.base + plane * self.zw
        n = self.zw
        self.put(CX, r, (0.5 * self.s) * (self.get(B, r, n) + self.get(B, r + n, n)))

    def around(self, q, r, n):
        zw, d = self.zw, self.d
        v = self.get(q, r, n)
        t = self.get(CX, r, n) * self.get(q, r + zw, n)
        t = t + self.get(CX, r - zw, n) * self.get(q, r - zw, n)
        t = t + self.get(CZ, r, n) * self.get(q, r + 1, n)
        t = t + self.get(CZ, r - 1, n) * self.get(q, r - 1, n)
        cy = self.get(CY, r, n)
        t = t + cy * pltpu.roll(v, LANES - d, 1)
        t = t + pltpu.roll(cy * v, d, 1)
        return v, t

    def sweep(self, src, dst, first, count, chunk):
        n = chunk * self.zw

        def body(i):
            r = self.base + (first + i * chunk) * self.zw
            v, t = self.around(src, r, n)
            self.put(dst, r, (1.0 - OMEGA) * v + self.get(W, r, n) * (self.get(F, r, n) + t))

        assert count % chunk == 0
        each(count // chunk, n, body)

    def residual(self, q, r, n):
        v, t = self.around(q, r, n)
        return self.get(F, r, n) + t - self.get(A, r, n) * v


def lane_pairs(t, d):
    s = t + pltpu.roll(t, LANES - d, 1)
    lane = lax.broadcasted_iota(jnp.int32, t.shape, 1)
    return jnp.where((lane // d) % 2 == 0, s, pltpu.roll(s, d, 1))


def restrict_planes(get, fine, first, pairs, coarse, q, plane, tmp, per):
    zw = fine.zw
    half = zw // 2

    def body(i):
        r = fine.base + (first + 2 * i * per) * zw
        t0 = i * per * zw if short(pairs // per, 2 * per * zw) else 0
        for k in range(per):
            v = get(r + 2 * k * zw, 2 * zw)
            tmp[pl.ds(t0 + k * zw, zw), :] = v[:zw] + v[zw:]
        t = tmp[pl.ds(t0, per * half, 2), :] + tmp[pl.ds(t0 + 1, per * half, 2), :]
        coarse.put(q, coarse.base + plane * half + i * per * half, lane_pairs(t, fine.d) * 0.125)

    assert pairs % per == 0
    each(pairs // per, 2 * per * zw, body)


def restrict_small(value, fine, coarse, q, tmp, count):
    zw, zc = fine.zw, coarse.zw
    tmp[pl.ds(0, count * 2 * zw), :] = value
    for z in range(zc):
        t = None
        for dx in range(2):
            for dz in range(2):
                part = tmp[pl.ds(dx * zw + 2 * z + dz, count, 2 * zw), :]
                t = part if t is None else t + part
        t = lane_pairs(t, fine.d) * 0.125
        if zc == 1:
            coarse.put(q, coarse.base, t)
        else:
            coarse.ref[q, pl.ds(coarse.base + z, count, zc), :] = t


def prolong_small(coarse, q, fine, p, tmp, count):
    zw, zc = fine.zw, coarse.zw
    for z in range(zc):
        v = coarse.get(q, coarse.base, count) if zc == 1 else coarse.ref[q, pl.ds(coarse.base + z, count, zc), :]
        for dx in range(2):
            for dz in range(2):
                tmp[pl.ds(dx * zw + 2 * z + dz, count, 2 * zw), :] = v
    n = count * 2 * zw
    fine.put(p, fine.base, fine.get(p, fine.base, n) + tmp[pl.ds(0, n), :])


def prolong_planes(coarse, q, plane, count, fine, src, dst, first, tmp, per=1):
    zw = fine.zw
    half = zw // 2

    def body(i):
        v = coarse.get(q, coarse.base + (plane + i * per) * half, per * half)
        t0 = i * per * zw if short(count // per, 2 * per * zw) else 0
        tmp[pl.ds(t0, per * half, 2), :] = v
        tmp[pl.ds(t0 + 1, per * half, 2), :] = v
        for k in range(per):
            e = tmp[pl.ds(t0 + k * zw, zw), :]
            r = fine.base + (first + 2 * (i * per + k)) * zw
            fine.put(dst, r, fine.get(src, r, zw) + e)
            fine.put(dst, r + zw, fine.get(src, r + zw, zw) + e)

    assert count % per == 0
    each(count // per, 2 * per * zw, body)


def keep(level, q, first, count, dst, k, sem):
    src = level.ref.at[q, pl.ds(first * level.zw, count * level.zw)]
    copy = pltpu.make_async_copy(src, dst.at[k], sem.at[k])
    copy.start()
    return copy


def down_kernel(
    bx, bz, n_wide, n_narrow, rhs, alpha, beta, lo, hi, other, packed, keep0, keep1, lev0, lev1, part, tmp, sem0, sem1
):
    zw = bz * n_narrow
    planes = bx + 2 * H
    wide = lax.axis_index("wide")
    narrow = lax.axis_index("narrow")
    l0 = Level(lev0, zw, 0)
    l1 = Level(lev1, zw // 2, 1)

    def place(q, src, src_plane, count, plane, z):
        def body(i):
            r = pl.multiple_of((plane + i) * zw + z, 8)
            l0.put(q, r, src[pl.ds((src_plane + i) * bz, bz), :])

        each(count, bz, body)

    g = H - 1
    all_h = 2 * g + H
    total = 3 * bx + 2 * all_h
    for q, own, at, size in ((F, rhs, 0, g), (A, alpha, g, g), (B, beta, 2 * g, H)):
        place(q, lo, at, size, H - size, narrow * bz)
        place(q, own, 0, bx, H, narrow * bz)
        place(q, hi, at, size, H + bx, narrow * bz)
        for k in range(n_narrow - 1):
            z = (1 - narrow if n_narrow == 2 else lax.rem(narrow + 1 + k, n_narrow)) * bz
            o = k * total + 3 * bx
            place(q, other, k * total + (F, A, B).index(q) * bx, bx, H, z)
            place(q, other, o + at, size, H - size, z)
            place(q, other, o + all_h + at, size, H + bx, z)
    first0, count0 = H - 2, bx + 4
    p1 = bx // 2 + 2 * H1
    waits = [keep(l0, F, first0, count0, keep0, F, sem0)]

    def valid0(p):
        x = wide * bx - H + p
        return jnp.logical_and(x >= 0, x < n_wide * bx)

    restrict_planes(lambda r, n: l0.get(B, r, n), l0, 1, p1, l1, B, 0, tmp.at[0], 1)
    restrict_planes(lambda r, n: l0.get(A, r, n), l0, 3, p1 - 2, l1, A, 1, tmp.at[1], 1)
    l0.first_cx(0)
    l0.setup(1, planes - 2, 1, valid0)
    waits += [keep(l0, q, first0, count0, keep0, q, sem0) for q in (W, CX, CZ, CY)]
    l0.sweep(U, V, 2, planes - 4, 1)
    waits.append(keep(l0, V, first0, count0, keep0, U, sem0))
    restrict_planes(lambda r, n: l0.residual(V, r, n), l0, 3, p1 - 2, l1, F, 1, tmp.at[2], 1)

    def valid1(p):
        x = wide * (bx // 2) - H1 + p
        return jnp.logical_and(x >= 0, x < n_wide * (bx // 2))

    k2 = bx // 4
    z2 = zw // 4
    n2 = k2 * z2
    l2 = Level(part, z2, 2)
    restrict_planes(lambda r, n: l1.get(A, r, n), l1, H1, k2, l2, 1, 0, tmp.at[1], 1)
    restrict_planes(lambda r, n: l1.get(B, r, n), l1, H1, k2, l2, 2, 0, tmp.at[0], 1)
    l1.first_cx(0)
    l1.setup(1, p1 - 2, 1, valid1)
    l1.sweep(U, V, 2, p1 - 4, 1)
    waits += [keep(l1, q, 1, p1 - 2, keep1, q, sem1) for q in (F, W, CX, CZ, CY)]
    waits.append(keep(l1, V, 1, p1 - 2, keep1, U, sem1))
    restrict_planes(lambda r, n: l1.residual(V, r, n), l1, H1, k2, l2, 0, 0, tmp.at[2], 1)
    which = lax.broadcasted_iota(jnp.int32, (n2, LANES), 1) % 4
    packed[...] = jnp.where(which == 0, part[0], jnp.where(which == 1, part[1], part[2]))
    for copy in waits:
        copy.wait()


def margin(zl, index):
    return max(8, (4 if index == 2 else 2) * zl)


def up_kernel(
    bx, bz, n_wide, n_narrow, gathered, keep0, keep1, out, lev2, lev3, lev4, lev5, lev0, lev1, tmp, sem, sem0, sem1
):
    wide = lax.axis_index("wide")
    narrow = lax.axis_index("narrow")
    zw = bz * n_narrow
    fetch = []
    for kept, lev, done in ((keep1, lev1, sem1), (keep0, lev0, sem0)):
        for q in range(KEPT):
            copy = pltpu.make_async_copy(kept.at[q], lev.at[q], done.at[q])
            copy.start()
            fetch.append(copy)
    m = margin(zw // 4, 2)
    arrive = pltpu.make_async_copy(gathered, lev2.at[U, pl.ds(m, n_wide * bx // 4 * (zw // 4))], sem)
    arrive.start()
    levels = []
    for index, ref in enumerate((lev2, lev3, lev4, lev5), 2):
        zl = zw // 2**index
        m = margin(zl, index)
        level = Level(ref, zl, index, m)
        level.nx = n_wide * bx // 2**index
        levels.append(level)
        zero = jnp.zeros((m, LANES), jnp.float32)
        for q in (F, W, CX, CZ, CY, U, B):
            level.put(q, 0, zero)
            level.put(q, m + level.nx * zl, zero)
    l2, l3, l4, l5 = levels
    planes2 = bx // 4
    n = planes2 * l2.zw
    lane = lax.broadcasted_iota(jnp.int32, (n, LANES), 1) % 4

    def unpack(i):
        p = l2.get(U, l2.base + i * n, n)
        for q, k, first, second in ((F, 0, 1, 2), (A, 1, LANES - 1, 2), (B, 2, 1, LANES - 2)):
            t = jnp.where(lane == k, p, 0.0)
            t = t + pltpu.roll(t, first, 1)
            t = t + pltpu.roll(t, second, 1)
            l2.put(q, l2.base + i * n, t)

    arrive.wait()
    each(n_wide, n, unpack)

    def chunk_of(level):
        return max(1, min(32 // level.zw, level.nx))

    def down(level, coarse, q, get, t):
        if level.zw >= 8:
            restrict_planes(get, level, 0, coarse.nx, coarse, q, 0, t, max(1, 16 // level.zw))
        else:
            restrict_small(get(level.base, level.nx * level.zw), level, coarse, q, t, coarse.nx)

    for level, coarse in ((l2, l3), (l3, l4), (l4, l5)):
        down(level, coarse, A, lambda r, m, level=level: level.get(A, r, m), tmp.at[0])
        down(level, coarse, B, lambda r, m, level=level: level.get(B, r, m), tmp.at[1])
    for level, coarse in ((l2, l3), (l3, l4), (l4, l5)):
        level.setup(0, level.nx, chunk_of(level))
        level.sweep(U, B, 0, level.nx, chunk_of(level))
        down(level, coarse, F, lambda r, m, level=level: level.residual(B, r, m), tmp.at[2])
    l5.setup(0, l5.nx, chunk_of(l5))
    src, dst = U, B
    for _ in range(BOTTOM - 1):
        l5.sweep(src, dst, 0, l5.nx, chunk_of(l5))
        src, dst = dst, src
    coarse = l5
    for level in (l4, l3):
        if level.zw >= 8:
            prolong_planes(coarse, src, 0, coarse.nx, level, B, B, 0, tmp.at[0], max(1, 16 // level.zw))
        else:
            prolong_small(coarse, src, level, B, tmp.at[0], coarse.nx)
        level.sweep(B, U, 0, level.nx, chunk_of(level))
        level.sweep(U, B, 0, level.nx, chunk_of(level))
        coarse, src = level, B
    start = wide * planes2
    r2 = pl.multiple_of(l2.base + start * l2.zw, 8)
    near2 = l2.moved(r2)
    near3 = l3.moved(l3.base + (start // 2) * l3.zw)
    prolong_planes(near3, B, -2, planes2 // 2 + 4, near2, B, B, -4, tmp.at[1], 2 if l2.zw < 16 else 1)
    near2.sweep(B, U, -3, planes2 + 6, 2)
    near2.sweep(U, B, -2, planes2 + 4, 2)
    for copy in fetch:
        copy.wait()
    l1 = Level(lev1, zw // 2, 1)
    count1 = bx // 2 + 2 * H1 - 2
    prolong_planes(near2, B, -2, count1 // 2, l1, U, U, 0, tmp.at[0])
    l1.sweep(U, KEPT, 2, count1 - 4, 1)
    l1.sweep(KEPT, U, 3, count1 - 6, 1)
    l0 = Level(lev0, zw, 0)
    prolong_planes(l1, U, 3, bx // 2 + 2, l0, U, U, 0, tmp.at[1])
    l0.sweep(U, KEPT, 1, bx + 2, 1)
    l0.sweep(KEPT, U, 2, bx, 1)

    def give(i):
        r = pl.multiple_of((2 + i) * zw + narrow * bz, 8)
        out[pl.ds(i * bz, bz), :] = l0.get(U, r, bz)

    each(bx, bz, give)


def shift(array, by):
    n = lax.axis_size("wide")
    return lax.ppermute(array, "wide", [(i, i + by) for i in range(n) if 0 <= i + by < n])


def shards(n_wide, n_narrow, rhs, alpha, beta):
    bx, bz, lanes = rhs.shape
    g = H - 1
    lo = shift(jnp.concatenate([rhs[bx - g :], alpha[bx - g :], beta[bx - H :]]), 1)
    hi = shift(jnp.concatenate([rhs[:g], alpha[:g], beta[:H]]), -1)
    bundle = jnp.concatenate([rhs, alpha, beta, lo, hi])
    if n_narrow == 2:
        other = lax.ppermute(bundle, "narrow", [(0, 1), (1, 0)])
    else:
        other = jnp.concatenate(
            [
                lax.ppermute(bundle, "narrow", [((i + k) % n_narrow, i) for i in range(n_narrow)])
                for k in range(1, n_narrow)
            ]
        )
    flat = lambda t: t.reshape(-1, lanes)
    zw = bz * n_narrow
    f32 = jnp.float32
    planes, p1 = bx + 2 * H, bx // 2 + 2 * H1
    n2 = (bx // 4) * (zw // 4)
    vmem, hbm = pl.BlockSpec(memory_space=pltpu.VMEM), pl.BlockSpec(memory_space=pl.ANY)
    keep0 = jax.ShapeDtypeStruct((KEPT, (bx + 4) * zw, lanes), f32)
    keep1 = jax.ShapeDtypeStruct((KEPT, (p1 - 2) * (zw // 2), lanes), f32)
    sems = [pltpu.SemaphoreType.DMA((KEPT,)), pltpu.SemaphoreType.DMA((KEPT,))]

    def params(scratch, rows):
        size = 4 * sum(math.prod(t.shape) for t in scratch[:-2]) + 4 * lanes * rows
        return pltpu.CompilerParams(vmem_limit_bytes=min(63 * 2**20, size + size // 8 + 2**21))

    scratch = [
        pltpu.VMEM((9, planes * zw, lanes), f32),
        pltpu.VMEM((9, p1 * (zw // 2), lanes), f32),
        pltpu.VMEM((3, n2, lanes), f32),
        pltpu.VMEM((3, p1 * zw, lanes), f32),
        *sems,
    ]
    packed, keep0, keep1 = pl.pallas_call(
        functools.partial(down_kernel, bx, bz, n_wide, n_narrow),
        out_shape=[jax.ShapeDtypeStruct((n2, lanes), f32), keep0, keep1],
        in_specs=[vmem] * 6,
        out_specs=[vmem, hbm, hbm],
        scratch_shapes=scratch,
        compiler_params=params(scratch, 3 * planes * zw),
        name="down",
    )(flat(rhs), flat(alpha), flat(beta), flat(lo), flat(hi), flat(other))
    gathered = lax.all_gather(packed, "wide", tiled=True)
    nx = n_wide * bx
    scratch = []
    for index in range(2, LEVELS):
        zl = zw // 2**index
        scratch.append(pltpu.VMEM((8, nx // 2**index * zl + 2 * margin(zl, index), lanes), f32))
    scratch += [
        pltpu.VMEM((KEPT + 1, *keep0.shape[1:]), f32),
        pltpu.VMEM((KEPT + 1, *keep1.shape[1:]), f32),
        pltpu.VMEM((3, max((bx // 2 + 2) * zw, LONGEST // 2), lanes), f32),
        pltpu.SemaphoreType.DMA,
        *sems,
    ]
    out = pl.pallas_call(
        functools.partial(up_kernel, bx, bz, n_wide, n_narrow),
        out_shape=jax.ShapeDtypeStruct((bx * bz, lanes), f32),
        in_specs=[hbm] * 3,
        out_specs=vmem,
        scratch_shapes=scratch,
        compiler_params=params(scratch[:-3] + sems, bx * bz),
        name="up",
    )(gathered, keep0, keep1)
    return out.reshape(bx, bz, lanes)


def solution(mesh):
    n_wide, n_narrow = mesh.shape["wide"], mesh.shape["narrow"]
    spec = P("wide", "narrow", None)
    return jax.shard_map(
        functools.partial(shards, n_wide, n_narrow),
        mesh=mesh,
        in_specs=(spec, spec, spec),
        out_specs=spec,
        check_vma=False,
    )
```

time: 243 us -> 75.3 us (0.31)
  starting transfers between devices: 120 us -> 6.22 us
  waiting for transfers between devices: 60.5 us -> 13.7 us
  blocking collectives: 0 us -> 40.4 us
  local copies, waits for them, and re-layouts: 40.3 us -> 2.16 us
  other arithmetic: 19.2 us -> 0.04 us
  Pallas kernels: 0 us -> 12.4 us
    ppermute x55 -> x3, starting transfers between devices: 120 us -> 6.22 us  [the longest x2 6.15 us: shift(): lax.ppermute(array, 'wide', [(i, i + by) for i in range(n) if 0 <= i + by...]
    ppermute x55 -> x3, waiting for transfers between devices: 60.5 us -> 13.7 us  [the longest x2 11.3 us: shift(): lax.ppermute(array, 'wide', [(i, i + by) for i in range(n) if 0 <= i + by...]
    all_gather x0 -> x1, blocking collectives: none -> 40.4 us  [shards(): gathered = lax.all_gather(packed, 'wide', tiled=True)]
    another operation x12 -> x0, local copies, waits for them, and re-layouts: 22.1 us -> none  [the longest x6 22.1 us: restrict(): grid_field.reshape(half_x, 2, half_z, 2, half_y, 2).sum(axis=(1, 3, 5))]
    reduce_sum x17 -> x0, other arithmetic: 13.7 us -> none  [restrict(): grid_field.reshape(half_x, 2, half_z, 2, half_y, 2).sum(axis=(1, 3, 5))]
    reshape x11 -> x0, local copies, waits for them, and re-layouts: 12.9 us -> none  [the longest x4 11.7 us: restrict(): grid_field.reshape(half_x, 2, half_z, 2, half_y, 2).sum(axis=(1, 3, 5))]
    pallas_call x0 -> x2, Pallas kernels: none -> 12.4 us  [the longest x1 6.54 us: shards(): pl.pallas_call(functools.partial(down_kernel, bx, bz, n_wide, n_narrow),...]
    add x29 -> x0, other arithmetic: 3.69 us -> none  [the longest x20 3.16 us: relax_once(): iterate + OMEGA * (source - apply_operator(extended, couple, diagonal, fa...]
  transfers between devices with their start and end apart: 55 -> 3, of which waited for: 19 -> 3; matrix products, arithmetic and copies ran while one was open for 20% -> 0% of each run, Pallas kernels for 0% -> 0%
where the time goes in v1:
time: 75.3 us; the launch traced here: 75.1 us
  blocking collectives  40.4 us (54%)
  waiting for transfers between devices  13.7 us (18%)
  Pallas kernels  12.4 us (16%)
  starting transfers between devices  6.22 us (8%)
  local copies, waits for them, and re-layouts  2.16 us (3%)
    all_gather x1, blocking collectives, shards(): gathered = lax.all_gather(packed, 'wide', tiled=True)  40.4 us
    ppermute x2, waiting for transfers between devices, shift(): lax.ppermute(array, 'wide', [(i, i + by) for i in range(n) if 0 <= i + by...  11.3 us
    pallas_call x1, Pallas kernels, shards(): pl.pallas_call(functools.partial(down_kernel, bx, bz, n_wide, n_narrow),...  6.54 us
    ppermute x2, starting transfers between devices, shift(): lax.ppermute(array, 'wide', [(i, i + by) for i in range(n) if 0 <= i + by...  6.15 us
    pallas_call x1, Pallas kernels, shards(): pl.pallas_call(functools.partial(up_kernel, bx, bz, n_wide, n_narrow), ou...  5.85 us
    ppermute x1, waiting for transfers between devices, shards(): other = lax.ppermute(bundle, 'narrow', [(0, 1), (1, 0)])  2.44 us
    slice x2, local copies, waits for them, and re-layouts, shards(): hi = shift(jnp.concatenate([rhs[:g], alpha[:g], beta[:H]]), -1)  2.08 us
  transfers between devices with their start and end apart: 3, of which 3 were waited for; matrix products, arithmetic and copies ran while one was open for 0% of the time, Pallas kernels for 0%

profile of v1, /device:TPU:0, one launch (start us, length us, event | category | flops | bytes accessed | tf_op | source)
XLA Modules:
  0.0 75.1 jit_solution(14604624283875389583)
XLA Ops:
  0.0 0.0 copy-start
  0.0 0.0 copy-start.2
  0.0 0.0 copy-start.1
  0.0 1.0 %fusion.2 = (f32[11,16,128]{2,1,0:T(8,128)S(1)}, f32[11,16,128]{2,1,0:T(8,128)S(1)}) fusion(f32[16,16,128]{2,1,0:T(8,128)} %param.5), kind=kLoop, calls=%fused_computation.9 | loop fusion | bytes 360448 | tf_op jit(solution)/shard_map/slice | solution.py:381
  1.1 1.0 %fusion = (f32[10,16,128]{2,1,0:T(8,128)S(1)}, f32[10,16,128]{2,1,0:T(8,128)S(1)}, f32[10,16,128]{2,1,0:T(8,128)S(1)}, f32[10,16,128]{2,1,0:T(8,128)S(1)}) fusion(f32[16,16,128]{2,1,0:T(8,128)} %param.3, f32[16,16,128]{2,1,0:T(8,128)} %param.4), kind=kLoop, calls=%fused_computation.7 | loop fusion | bytes 655360 | tf_op jit(solution)/shard_map/slice | solution.py:381
  2.1 4.9 %collective-permute-start = (f32[31,16,128]{2,1,0:T(8,128)S(1)}, f32[31,16,128]{2,1,0:T(8,128)S(1)}, u32[]{:S(2)}, u32[]{:S(2)}) collective-permute-start(f32[31,16,128]{2,1,0:T(8,128)S(1)} %pad_maximum_fusion), channel_id=1, source_target_pairs={{0,2},{2,4},{4,6},{6,8},{8,10},{10,12},{12,14},{14,16},{16,18},{18... | collective-permute-start | bytes 761864 | tf_op jit(solution)/shard_map/ppermute | solution.py:374
  7.0 1.3 %collective-permute-start.1 = (f32[31,16,128]{2,1,0:T(8,128)S(1)}, f32[31,16,128]{2,1,0:T(8,128)S(1)}, u32[]{:S(2)}, u32[]{:S(2)}) collective-permute-start(f32[31,16,128]{2,1,0:T(8,128)S(1)} %pad_maximum_fusion.1), channel_id=1, source_target_pairs={{2,0},{4,2},{6,4},{8,6},{10,8},{12,10},{14,12},{16,14},{18,16},{20... | collective-permute-start | bytes 761864 | tf_op jit(solution)/shard_map/ppermute | solution.py:374
  8.3 0.0 copy-done.1
  8.3 0.0 copy-done.2
  8.4 0.0 copy-done
  8.4 9.4 %collective-permute-done = f32[31,16,128]{2,1,0:T(8,128)S(1)} collective-permute-done((f32[31,16,128]{2,1,0:T(8,128)S(1)}, f32[31,16,128]{2,1,0:T(8,128)S(1)}, u32[]{:S(2)}, u32[]{:S(2)}) %collective-permute-start) | collective-permute-done | bytes 253984 | tf_op jit(solution)/shard_map/ppermute | solution.py:374
  17.8 1.9 %collective-permute-done.1 = f32[31,16,128]{2,1,0:T(8,128)S(1)} collective-permute-done((f32[31,16,128]{2,1,0:T(8,128)S(1)}, f32[31,16,128]{2,1,0:T(8,128)S(1)}, u32[]{:S(2)}, u32[]{:S(2)}) %collective-permute-start.1) | collective-permute-done | bytes 253984 | tf_op jit(solution)/shard_map/ppermute | solution.py:374
  19.7 0.1 collective-permute-start.2
  19.8 2.4 %collective-permute-done.2 = f32[110,16,128]{2,1,0:T(8,128)S(1)} collective-permute-done((f32[110,16,128]{2,1,0:T(8,128)S(1)}, f32[110,16,128]{2,1,0:T(8,128)S(1)}, u32[]{:S(2)}, u32[]{:S(2)}) %collective-permute-start.2) | collective-permute-done | bytes 901152 | tf_op jit(solution)/shard_map/ppermute | solution.py:384
  22.3 6.5 %down.1 = (f32[32,128]{1,0:T(8,128)S(1)}, f32[6,640,128]{2,1,0:T(8,128)S(1)}, f32[6,256,128]{2,1,0:T(8,128)S(1)}) custom-call(f32[256,128]{1,0:T(8,128)S(1)} %bitcast.8, f32[256,128]{1,0:T(8,128)S(1)} %bitcast.9, f32[256,128]{1,0:T(8,128)S(1)} %bitcast.7, f32[496,128]{1,0:T(8,128)S(1)} %bitcast.10, f32[496,128]{1,0:T(8,128)S(1)} %bitcast.11, ...), custom_call_target="tpu_custom_call" | custom-call | tf_op jit(solution)/shard_map/down/pallas_call | solution.py:413
  28.8 40.4 %all_gather.3.gathered = f32[512,128]{1,0:T(8,128)S(1)} all-gather(f32[32,128]{1,0:T(8,128)S(1)} %get-tuple-element.8), channel_id=1, replica_groups=mesh['wide'=16,'narrow'=2] {'wide'}, dimensions={0}, use_global_device_ids=true | all-gather | bytes 278528 | tf_op jit(solution)/shard_map/all_gather | solution.py:422
  69.2 5.8 %up.1 = f32[256,128]{1,0:T(8,128)} custom-call(f32[512,128]{1,0:T(8,128)S(1)} %all_gather.3.gathered, f32[6,640,128]{2,1,0:T(8,128)S(1)} %get-tuple-element.9.keep0, f32[6,256,128]{2,1,0:T(8,128)S(1)} %get-tuple-element.10.keep1), custom_call_target="tpu_custom_call" | custom-call | tf_op jit(solution)/shard_map/up/pallas_call | solution.py:435
  (7 shorter events, 0.1 us)
Async XLA Ops:
  0.0 8.4 %copy-start = (f32[16,16,128]{2,1,0:T(8,128)S(1)}, f32[16,16,128]{2,1,0:T(8,128)}, u32[]{:S(2)}) copy-start(f32[16,16,128]{2,1,0:T(8,128)} %param.5) | copy-start | bytes 393220
  0.0 8.3 %copy-start.2 = (f32[16,16,128]{2,1,0:T(8,128)S(1)}, f32[16,16,128]{2,1,0:T(8,128)}, u32[]{:S(2)}) copy-start(f32[16,16,128]{2,1,0:T(8,128)} %param.4) | copy-start | bytes 393220
  0.0 8.3 %copy-start.1 = (f32[16,16,128]{2,1,0:T(8,128)S(1)}, f32[16,16,128]{2,1,0:T(8,128)}, u32[]{:S(2)}) copy-start(f32[16,16,128]{2,1,0:T(8,128)} %param.3) | copy-start | bytes 393220
  2.1 15.7 %collective-permute-start = (f32[31,16,128]{2,1,0:T(8,128)S(1)}, f32[31,16,128]{2,1,0:T(8,128)S(1)}, u32[]{:S(2)}, u32[]{:S(2)}) collective-permute-start(f32[31,16,128]{2,1,0:T(8,128)S(1)} %pad_maximum_fusion), channel_id=1, source_target_pairs={{0,2},{2,4},{4,6},{6,8},{8,10},{10,12},{12,14},{14,16},{16,18},{18... | collective-permute-start | bytes 761864 | tf_op jit(solution)/shard_map/ppermute | solution.py:374
  7.0 12.7 %collective-permute-start.1 = (f32[31,16,128]{2,1,0:T(8,128)S(1)}, f32[31,16,128]{2,1,0:T(8,128)S(1)}, u32[]{:S(2)}, u32[]{:S(2)}) collective-permute-start(f32[31,16,128]{2,1,0:T(8,128)S(1)} %pad_maximum_fusion.1), channel_id=1, source_target_pairs={{2,0},{4,2},{6,4},{8,6},{10,8},{12,10},{14,12},{16,14},{18,16},{20... | collective-permute-start | bytes 761864 | tf_op jit(solution)/shard_map/ppermute | solution.py:374
  19.7 2.5 %collective-permute-start.2 = (f32[110,16,128]{2,1,0:T(8,128)S(1)}, f32[110,16,128]{2,1,0:T(8,128)S(1)}, u32[]{:S(2)}, u32[]{:S(2)}) collective-permute-start(f32[110,16,128]{2,1,0:T(8,128)S(1)} %constant_dynamic-update-slice_fusion), channel_id=1, source_target_pairs={{0,1},{1,0},{2,3},{3,2},{4,5},{5,4},{6,7},{7,6},{8,9},{9,8},{10,11... | collective-permute-start | bytes 2703368 | tf_op jit(solution)/shard_map/ppermute | solution.py:384

commit v2 on v1

--- a/solution.py
+++ b/solution.py
@@ -12,8 +12,8 @@
 BOTTOM = 6
 OMEGA = 2.0 / 3.0
 LANES = 128
-H = 11
-H1 = 5
+H1 = 3
+H = 2 * H1 + 1
 LONGEST = 2048
 
 
@@ -198,13 +198,43 @@
     return copy
 
 
+def rev(x, bits):
+    return sum(((x >> k) & 1) << (bits - 1 - k) for k in range(bits)) if bits else 0
+
+
+def bits_of(n):
+    return n.bit_length() - 1
+
+
+def pack_kernel(bx, bz, rhs, alpha, beta, even, odd, own, sem):
+    up = 1 - lax.axis_index("wide") % 2
+    waits = []
+    at = [0, 0]
+    for q, (src, size) in enumerate(((rhs, H - 1), (alpha, H - 1), (beta, H))):
+        for k, dst in enumerate((even, odd)):
+            upper = up if k == 0 else 1 - up
+            start = pl.multiple_of(upper * ((bx - size) * bz), 8)
+            copy = pltpu.make_async_copy(
+                src.at[pl.ds(start, size * bz)], dst.at[pl.ds(at[k] * bz, size * bz)], sem.at[2 * q + k]
+            )
+            copy.start()
+            waits.append(copy)
+            at[k] += size
+        copy = pltpu.make_async_copy(src, own.at[pl.ds(q * bx * bz, bx * bz)], sem.at[6 + q])
+        copy.start()
+        waits.append(copy)
+    for copy in waits:
+        copy.wait()
+
+
 def down_kernel(
-    bx, bz, n_wide, n_narrow, rhs, alpha, beta, lo, hi, other, packed, keep0, keep1, lev0, lev1, part, tmp, sem0, sem1
+    bx, bz, n_wide, n_narrow, own, even, odd, other, others, packed, ueven, uodd, keep0, keep1, lev0, lev1, part, tmp, sem0, sem1
 ):
     zw = bz * n_narrow
     planes = bx + 2 * H
     wide = lax.axis_index("wide")
     narrow = lax.axis_index("narrow")
+    up = 1 - wide % 2
     l0 = Level(lev0, zw, 0)
     l1 = Level(lev1, zw // 2, 1)
 
@@ -217,17 +247,18 @@
 
     g = H - 1
     all_h = 2 * g + H
-    total = 3 * bx + 2 * all_h
-    for q, own, at, size in ((F, rhs, 0, g), (A, alpha, g, g), (B, beta, 2 * g, H)):
-        place(q, lo, at, size, H - size, narrow * bz)
-        place(q, own, 0, bx, H, narrow * bz)
-        place(q, hi, at, size, H + bx, narrow * bz)
+    for index, (q, at, size) in enumerate(((F, 0, g), (A, g, g), (B, 2 * g, H))):
+        above, below = H + bx, H - size
+        p_even = up * above + (1 - up) * below
+        p_odd = (1 - up) * above + up * below
+        place(q, own, index * bx, bx, H, narrow * bz)
+        place(q, even, at, size, p_even, narrow * bz)
+        place(q, odd, at, size, p_odd, narrow * bz)
         for k in range(n_narrow - 1):
             z = (1 - narrow if n_narrow == 2 else lax.rem(narrow + 1 + k, n_narrow)) * bz
-            o = k * total + 3 * bx
-            place(q, other, k * total + (F, A, B).index(q) * bx, bx, H, z)
-            place(q, other, o + at, size, H - size, z)
-            place(q, other, o + all_h + at, size, H + bx, z)
+            place(q, other, (3 * k + index) * bx, bx, H, z)
+            place(q, others, 2 * k * all_h + at, size, p_even, z)
+            place(q, others, (2 * k + 1) * all_h + at, size, p_odd, z)
     first0, count0 = H - 2, bx + 4
     p1 = bx // 2 + 2 * H1
     waits = [keep(l0, F, first0, count0, keep0, F, sem0)]
@@ -256,13 +287,20 @@
     restrict_planes(lambda r, n: l1.get(A, r, n), l1, H1, k2, l2, 1, 0, tmp.at[1], 1)
     restrict_planes(lambda r, n: l1.get(B, r, n), l1, H1, k2, l2, 2, 0, tmp.at[0], 1)
     l1.first_cx(0)
+    l1.put(CZ, 0, jnp.zeros((l1.zw, LANES), jnp.float32))
     l1.setup(1, p1 - 2, 1, valid1)
     l1.sweep(U, V, 2, p1 - 4, 1)
-    waits += [keep(l1, q, 1, p1 - 2, keep1, q, sem1) for q in (F, W, CX, CZ, CY)]
-    waits.append(keep(l1, V, 1, p1 - 2, keep1, U, sem1))
+    waits += [keep(l1, q, 0, p1, keep1, q, sem1) for q in (F, W, CX, CZ, CY)]
+    waits.append(keep(l1, V, 0, p1, keep1, U, sem1))
+    n1 = 2 * l1.zw
+    upper, lower = H1 + bx // 2 - 3, H1 + 1
+    ueven[...] = l1.get(V, pl.multiple_of((up * upper + (1 - up) * lower) * l1.zw, 8), n1)
+    uodd[...] = l1.get(V, pl.multiple_of(((1 - up) * upper + up * lower) * l1.zw, 8), n1)
     restrict_planes(lambda r, n: l1.residual(V, r, n), l1, H1, k2, l2, 0, 0, tmp.at[2], 1)
     which = lax.broadcasted_iota(jnp.int32, (n2, LANES), 1) % 4
-    packed[...] = jnp.where(which == 0, part[0], jnp.where(which == 1, part[1], part[2]))
+    part[0] = jnp.where(which == 0, part[0], jnp.where(which == 1, part[1], part[2]))
+    share = n2 // n_narrow
+    packed[...] = part[0, pl.ds(pl.multiple_of(narrow * share, 8), share), :]
     for copy in waits:
         copy.wait()
 
@@ -272,15 +310,16 @@
 
 
 def up_kernel(
-    bx, bz, n_wide, n_narrow, gathered, keep0, keep1, out, lev2, lev3, lev4, lev5, lev0, lev1, tmp, sem, sem0, sem1
+    bx, bz, n_wide, n_narrow, gathered, heven, hodd, keep0, keep1, out, lev2, lev3, lev4, lev5, lev0, lev1, tmp, sem, sem0, sem1
 ):
     wide = lax.axis_index("wide")
     narrow = lax.axis_index("narrow")
     zw = bz * n_narrow
     fetch = []
-    for kept, lev, done in ((keep1, lev1, sem1), (keep0, lev0, sem0)):
+    z1 = zw // 2
+    for kept, lev, done, r in ((keep1, lev1, sem1, z1), (keep0, lev0, sem0, 0)):
         for q in range(KEPT):
-            copy = pltpu.make_async_copy(kept.at[q], lev.at[q], done.at[q])
+            copy = pltpu.make_async_copy(kept.at[q], lev.at[q, pl.ds(r, kept.shape[1])], done.at[q])
             copy.start()
             fetch.append(copy)
     m = margin(zw // 4, 2)
@@ -299,11 +338,16 @@
             level.put(q, m + level.nx * zl, zero)
     l2, l3, l4, l5 = levels
     planes2 = bx // 4
-    n = planes2 * l2.zw
+    n2 = planes2 * l2.zw
+    n = n2 // n_narrow
+    bw, bn = bits_of(n_wide), bits_of(n_narrow)
+    me = rev(wide, bw) + n_wide * rev(narrow, bn)
     lane = lax.broadcasted_iota(jnp.int32, (n, LANES), 1) % 4
 
     def unpack(i):
-        p = l2.get(U, l2.base + i * n, n)
+        w, c = i // n_narrow, i % n_narrow
+        at = me ^ (rev(w, bw) + n_wide * rev(c, bn))
+        p = l2.get(U, pl.multiple_of(l2.base + at * n, 8), n)
         for q, k, first, second in ((F, 0, 1, 2), (A, 1, LANES - 1, 2), (B, 2, 1, LANES - 2)):
             t = jnp.where(lane == k, p, 0.0)
             t = t + pltpu.roll(t, first, 1)
@@ -311,7 +355,7 @@
             l2.put(q, l2.base + i * n, t)
 
     arrive.wait()
-    each(n_wide, n, unpack)
+    each(n_wide * n_narrow, n, unpack)
 
     def chunk_of(level):
         return max(1, min(32 // level.zw, level.nx))
@@ -352,8 +396,12 @@
     near2.sweep(U, B, -2, planes2 + 4, 2)
     for copy in fetch:
         copy.wait()
-    l1 = Level(lev1, zw // 2, 1)
-    count1 = bx // 2 + 2 * H1 - 2
+    l1 = Level(lev1, z1, 1)
+    count1 = bx // 2 + 2 * H1 + 2
+    up = 1 - wide % 2
+    above, below = H1 + bx // 2 + 2, 1
+    l1.put(U, pl.multiple_of((up * above + (1 - up) * below) * z1, 8), heven[...])
+    l1.put(U, pl.multiple_of(((1 - up) * above + up * below) * z1, 8), hodd[...])
     prolong_planes(near2, B, -2, count1 // 2, l1, U, U, 0, tmp.at[0])
     l1.sweep(U, KEPT, 2, count1 - 4, 1)
     l1.sweep(KEPT, U, 3, count1 - 6, 1)
@@ -369,26 +417,28 @@
     each(bx, bz, give)
 
 
-def shift(array, by):
+def swap(array, axis, bit):
+    n = lax.axis_size(axis)
+    return lax.ppermute(array, axis, [(i, i ^ (1 << bit)) for i in range(n)])
+
+
+def swap_odd(array):
     n = lax.axis_size("wide")
-    return lax.ppermute(array, "wide", [(i, i + by) for i in range(n) if 0 <= i + by < n])
+    pairs = [(i, i + 1) for i in range(1, n - 1, 2)]
+    return lax.ppermute(array, "wide", pairs + [(j, i) for i, j in pairs])
+
+
+def from_others(array):
+    n = lax.axis_size("narrow")
+    if n == 2:
+        return swap(array, "narrow", 0)
+    return jnp.concatenate(
+        [lax.ppermute(array, "narrow", [((i + k) % n, i) for i in range(n)]) for k in range(1, n)]
+    )
 
 
 def shards(n_wide, n_narrow, rhs, alpha, beta):
     bx, bz, lanes = rhs.shape
-    g = H - 1
-    lo = shift(jnp.concatenate([rhs[bx - g :], alpha[bx - g :], beta[bx - H :]]), 1)
-    hi = shift(jnp.concatenate([rhs[:g], alpha[:g], beta[:H]]), -1)
-    bundle = jnp.concatenate([rhs, alpha, beta, lo, hi])
-    if n_narrow == 2:
-        other = lax.ppermute(bundle, "narrow", [(0, 1), (1, 0)])
-    else:
-        other = jnp.concatenate(
-            [
-                lax.ppermute(bundle, "narrow", [((i + k) % n_narrow, i) for i in range(n_narrow)])
-                for k in range(1, n_narrow)
-            ]
-        )
     flat = lambda t: t.reshape(-1, lanes)
     zw = bz * n_narrow
     f32 = jnp.float32
@@ -396,13 +446,28 @@
     n2 = (bx // 4) * (zw // 4)
     vmem, hbm = pl.BlockSpec(memory_space=pltpu.VMEM), pl.BlockSpec(memory_space=pl.ANY)
     keep0 = jax.ShapeDtypeStruct((KEPT, (bx + 4) * zw, lanes), f32)
-    keep1 = jax.ShapeDtypeStruct((KEPT, (p1 - 2) * (zw // 2), lanes), f32)
+    keep1 = jax.ShapeDtypeStruct((KEPT, p1 * (zw // 2), lanes), f32)
+    u_face = jax.ShapeDtypeStruct((zw, lanes), f32)
     sems = [pltpu.SemaphoreType.DMA((KEPT,)), pltpu.SemaphoreType.DMA((KEPT,))]
 
     def params(scratch, rows):
         size = 4 * sum(math.prod(t.shape) for t in scratch[:-2]) + 4 * lanes * rows
         return pltpu.CompilerParams(vmem_limit_bytes=min(63 * 2**20, size + size // 8 + 2**21))
 
+    face = jax.ShapeDtypeStruct(((3 * H - 2) * bz, lanes), f32)
+    even, odd, own = pl.pallas_call(
+        functools.partial(pack_kernel, bx, bz),
+        out_shape=[face, face, jax.ShapeDtypeStruct((3 * bx * bz, lanes), f32)],
+        in_specs=[hbm] * 3,
+        out_specs=[vmem] * 3,
+        scratch_shapes=[pltpu.SemaphoreType.DMA((9,))],
+        compiler_params=pltpu.CompilerParams(vmem_limit_bytes=2**22),
+        name="pack",
+    )(flat(rhs), flat(alpha), flat(beta))
+    even = swap(even, "wide", 0)
+    odd = swap_odd(odd)
+    other = from_others(own)
+    others = from_others(jnp.concatenate([even, odd]))
     scratch = [
         pltpu.VMEM((9, planes * zw, lanes), f32),
         pltpu.VMEM((9, p1 * (zw // 2), lanes), f32),
@@ -410,16 +475,25 @@
         pltpu.VMEM((3, p1 * zw, lanes), f32),
         *sems,
     ]
-    packed, keep0, keep1 = pl.pallas_call(
+    packed, ueven, uodd, keep0, keep1 = pl.pallas_call(
         functools.partial(down_kernel, bx, bz, n_wide, n_narrow),
-        out_shape=[jax.ShapeDtypeStruct((n2, lanes), f32), keep0, keep1],
-        in_specs=[vmem] * 6,
-        out_specs=[vmem, hbm, hbm],
+        out_shape=[jax.ShapeDtypeStruct((n2 // n_narrow, lanes), f32), u_face, u_face, keep0, keep1],
+        in_specs=[vmem] * 5,
+        out_specs=[vmem, vmem, vmem, hbm, hbm],
         scratch_shapes=scratch,
         compiler_params=params(scratch, 3 * planes * zw),
         name="down",
-    )(flat(rhs), flat(alpha), flat(beta), flat(lo), flat(hi), flat(other))
-    gathered = lax.all_gather(packed, "wide", tiled=True)
+    )(own, even, odd, other, others)
+    hodd = swap_odd(uodd)
+    gathered = packed
+    for bit in reversed(range(bits_of(n_wide))):
+        rows = gathered.shape[0]
+        sent = jnp.concatenate([gathered, ueven]) if bit == 0 else gathered
+        came = swap(sent, "wide", bit)
+        gathered = jnp.concatenate([gathered, came[:rows]])
+    heven = came[rows:]
+    for bit in reversed(range(bits_of(n_narrow))):
+        gathered = jnp.concatenate([gathered, swap(gathered, "narrow", bit)])
     nx = n_wide * bx
     scratch = []
     for index in range(2, LEVELS):
@@ -427,7 +501,7 @@
         scratch.append(pltpu.VMEM((8, nx // 2**index * zl + 2 * margin(zl, index), lanes), f32))
     scratch += [
         pltpu.VMEM((KEPT + 1, *keep0.shape[1:]), f32),
-        pltpu.VMEM((KEPT + 1, *keep1.shape[1:]), f32),
+        pltpu.VMEM((KEPT + 1, (p1 + 2) * (zw // 2), lanes), f32),
         pltpu.VMEM((3, max((bx // 2 + 2) * zw, LONGEST // 2), lanes), f32),
         pltpu.SemaphoreType.DMA,
         *sems,
@@ -435,12 +509,12 @@
     out = pl.pallas_call(
         functools.partial(up_kernel, bx, bz, n_wide, n_narrow),
         out_shape=jax.ShapeDtypeStruct((bx * bz, lanes), f32),
-        in_specs=[hbm] * 3,
+        in_specs=[hbm, vmem, vmem, hbm, hbm],
         out_specs=vmem,
         scratch_shapes=scratch,
         compiler_params=params(scratch[:-3] + sems, bx * bz),
         name="up",
-    )(gathered, keep0, keep1)
+    )(gathered, heven, hodd, keep0, keep1)
     return out.reshape(bx, bz, lanes)
 
 

time: 75.3 us -> 55.3 us (0.73)
  the two profiles are of different devices: /device:TPU:0 before, /device:TPU:24 now
where the time goes in v2:
time: 55.3 us; the launch traced here: 55.1 us
  waiting for transfers between devices  25.8 us (47%)
  Pallas kernels  15.6 us (28%)
  starting transfers between devices  10.8 us (20%)
  local copies, waits for them, and re-layouts  2.76 us (5%)
    ppermute x8, waiting for transfers between devices, swap(): return lax.ppermute(array, axis, [(i, i ^ 1 << bit) for i in range(n)])  16.8 us
    pallas_call x1, Pallas kernels, shards(): pl.pallas_call(functools.partial(up_kernel, bx, bz, n_wide, n_narrow), ou...  9.86 us
    ppermute x2, waiting for transfers between devices, swap_odd(): return lax.ppermute(array, 'wide', pairs + [(j, i) for i, j in pairs])  8.99 us
    ppermute x2, starting transfers between devices, swap_odd(): return lax.ppermute(array, 'wide', pairs + [(j, i) for i, j in pairs])  6.56 us
    pallas_call x1, Pallas kernels, shards(): pl.pallas_call(functools.partial(down_kernel, bx, bz, n_wide, n_narrow),...  4.82 us
    ppermute x8, starting transfers between devices, swap(): return lax.ppermute(array, axis, [(i, i ^ 1 << bit) for i in range(n)])  4.2 us
    unnamed x10, local copies, waits for them, and re-layouts  2.73 us
  transfers between devices with their start and end apart: 10, of which 8 were waited for; matrix products, arithmetic and copies ran while one was open for 0% of the time, Pallas kernels for 0%

profile of v2, /device:TPU:24, one launch (start us, length us, event | category | flops | bytes accessed | tf_op | source)
XLA Modules:
  0.0 55.1 jit_solution(15484526453366259275)
XLA Ops:
  0.0 0.0 copy-start
  0.0 0.9 %copy-done = f32[16,16,128]{2,1,0:T(8,128)S(1)} copy-done((f32[16,16,128]{2,1,0:T(8,128)S(1)}, f32[16,16,128]{2,1,0:T(8,128)}, u32[]{:S(2)}) %copy-start) | copy-done | bytes 131096
  0.9 0.0 copy-start.1
  0.9 0.9 %copy-done.1 = f32[16,16,128]{2,1,0:T(8,128)S(1)} copy-done((f32[16,16,128]{2,1,0:T(8,128)S(1)}, f32[16,16,128]{2,1,0:T(8,128)}, u32[]{:S(2)}) %copy-start.1) | copy-done | bytes 131096
  1.8 0.0 copy-start.2
  1.8 0.9 %copy-done.2 = f32[16,16,128]{2,1,0:T(8,128)S(1)} copy-done((f32[16,16,128]{2,1,0:T(8,128)S(1)}, f32[16,16,128]{2,1,0:T(8,128)}, u32[]{:S(2)}) %copy-start.2) | copy-done | bytes 131096
  2.7 1.0 %pack.1 = (f32[304,128]{1,0:T(8,128)S(1)}, f32[304,128]{1,0:T(8,128)S(1)}, f32[768,128]{1,0:T(8,128)S(1)}) custom-call(f32[256,128]{1,0:T(8,128)S(1)} %bitcast.4, f32[256,128]{1,0:T(8,128)S(1)} %bitcast.5, f32[256,128]{1,0:T(8,128)S(1)} %bitcast.6), custom_call_target="tpu_custom_call" | custom-call | tf_op jit(solution)/shard_map/pack/pallas_call | solution.py:458
  3.7 1.6 %collective-permute-start = (f32[304,128]{1,0:T(8,128)S(1)}, f32[304,128]{1,0:T(8,128)S(1)}, u32[]{:S(2)}, u32[]{:S(2)}) collective-permute-start(f32[304,128]{1,0:T(8,128)S(1)} %get-tuple-element.14), channel_id=1, source_target_pairs={{0,2},{2,0},{4,6},{6,4},{8,10},{10,8},{12,14},{14,12},{16,18},{18,... | collective-permute-start | bytes 466952 | tf_op jit(solution)/shard_map/ppermute | solution.py:422
  5.2 3.3 %collective-permute-start.1 = (f32[304,128]{1,0:T(8,128)S(1)}, f32[304,128]{1,0:T(8,128)S(1)}, u32[]{:S(2)}, u32[]{:S(2)}) collective-permute-start(f32[304,128]{1,0:T(8,128)S(1)} %get-tuple-element.15), channel_id=1, source_target_pairs={{2,4},{6,8},{10,12},{14,16},{18,20},{22,24},{26,28},{4,2},{8,6},{1... | collective-permute-start | bytes 466952 | tf_op jit(solution)/shard_map/ppermute | solution.py:428
  8.5 0.1 collective-permute-start.2
  8.6 0.9 %collective-permute-done.even = f32[304,128]{1,0:T(8,128)S(1)} collective-permute-done((f32[304,128]{1,0:T(8,128)S(1)}, f32[304,128]{1,0:T(8,128)S(1)}, u32[]{:S(2)}, u32[]{:S(2)}) %collective-permute-start) | collective-permute-done | bytes 155680 | tf_op jit(solution)/shard_map/ppermute | solution.py:422
  9.5 4.9 %collective-permute-done.1.odd = f32[304,128]{1,0:T(8,128)S(1)} collective-permute-done((f32[304,128]{1,0:T(8,128)S(1)}, f32[304,128]{1,0:T(8,128)S(1)}, u32[]{:S(2)}, u32[]{:S(2)}) %collective-permute-start.1) | collective-permute-done | bytes 155680 | tf_op jit(solution)/shard_map/ppermute | solution.py:428
  14.4 0.1 collective-permute-start.3
  14.5 0.0 collective-permute-done.2.other
  14.5 1.6 %collective-permute-done.3.others = f32[608,128]{1,0:T(8,128)S(1)} collective-permute-done((f32[608,128]{1,0:T(8,128)S(1)}, f32[608,128]{1,0:T(8,128)S(1)}, u32[]{:S(2)}, u32[]{:S(2)}) %collective-permute-start.3) | collective-permute-done | bytes 311328 | tf_op jit(solution)/shard_map/ppermute | solution.py:422
  16.1 4.8 %down.1 = (f32[16,128]{1,0:T(8,128)S(1)}, f32[32,128]{1,0:T(8,128)S(1)}, f32[32,128]{1,0:T(8,128)S(1)}, f32[6,640,128]{2,1,0:T(8,128)S(1)}, f32[6,224,128]{2,1,0:T(8,128)S(1)}) custom-call(f32[768,128]{1,0:T(8,128)S(1)} %get-tuple-element.13.own, f32[304,128]{1,0:T(8,128)S(1)} %collective-permute-done.even, f32[304,128]{1,0:T(8,128)S(1)} %collective-permute-done.1.odd, ...), custom_call_target="tpu_custom_call" | custom-call | tf_op jit(solution)/shard_map/down/pallas_call | solution.py:478
  20.9 0.4 collective-permute-start.4
  21.3 4.2 %collective-permute-done.4 = f32[16,128]{1,0:T(8,128)S(1)} collective-permute-done((f32[16,128]{1,0:T(8,128)S(1)}, f32[16,128]{1,0:T(8,128)S(1)}, u32[]{:S(2)}, u32[]{:S(2)}) %collective-permute-start.4) | collective-permute-done | bytes 8224 | tf_op jit(solution)/shard_map/ppermute | solution.py:422
  25.6 0.4 collective-permute-start.5
  26.0 3.3 %collective-permute-done.5 = f32[32,128]{1,0:T(8,128)S(1)} collective-permute-done((f32[32,128]{1,0:T(8,128)S(1)}, f32[32,128]{1,0:T(8,128)S(1)}, u32[]{:S(2)}, u32[]{:S(2)}) %collective-permute-start.5) | collective-permute-done | bytes 16416 | tf_op jit(solution)/shard_map/ppermute | solution.py:422
  29.3 0.6 %collective-permute-start.6 = (f32[64,128]{1,0:T(8,128)S(1)}, f32[64,128]{1,0:T(8,128)S(1)}, u32[]{:S(2)}, u32[]{:S(2)}) collective-permute-start(f32[64,128]{1,0:T(8,128)S(1)} %pad_maximum_fusion.1), channel_id=1, source_target_pairs={{0,4},{2,6},{4,0},{6,2},{8,12},{10,14},{12,8},{14,10},{16,20},{18,... | collective-permute-start | bytes 98312 | tf_op jit(solution)/shard_map/ppermute | solution.py:422
  29.9 3.3 %collective-permute-done.6 = f32[64,128]{1,0:T(8,128)S(1)} collective-permute-done((f32[64,128]{1,0:T(8,128)S(1)}, f32[64,128]{1,0:T(8,128)S(1)}, u32[]{:S(2)}, u32[]{:S(2)}) %collective-permute-start.6) | collective-permute-done | bytes 32800 | tf_op jit(solution)/shard_map/ppermute | solution.py:422
  33.2 1.0 %collective-permute-start.7 = (f32[160,128]{1,0:T(8,128)S(1)}, f32[160,128]{1,0:T(8,128)S(1)}, u32[]{:S(2)}, u32[]{:S(2)}) collective-permute-start(f32[160,128]{1,0:T(8,128)S(1)} %constant_dynamic-update-slice_fusion), channel_id=1, source_target_pairs={{0,2},{2,0},{4,6},{6,4},{8,10},{10,8},{12,14},{14,12},{16,18},{18,... | collective-permute-start | bytes 245768 | tf_op jit(solution)/shard_map/ppermute | solution.py:422
  34.2 3.5 %collective-permute-done.7 = f32[160,128]{1,0:T(8,128)S(1)} collective-permute-done((f32[160,128]{1,0:T(8,128)S(1)}, f32[160,128]{1,0:T(8,128)S(1)}, u32[]{:S(2)}, u32[]{:S(2)}) %collective-permute-start.7) | collective-permute-done | bytes 81952 | tf_op jit(solution)/shard_map/ppermute | solution.py:422
  37.8 0.1 collective-permute-start.8
  37.8 3.3 %collective-permute-start.9 = (f32[32,128]{1,0:T(8,128)S(1)}, f32[32,128]{1,0:T(8,128)S(1)}, u32[]{:S(2)}, u32[]{:S(2)}) collective-permute-start(f32[32,128]{1,0:T(8,128)S(1)} %get-tuple-element.18), channel_id=1, source_target_pairs={{2,4},{6,8},{10,12},{14,16},{18,20},{22,24},{26,28},{4,2},{8,6},{1... | collective-permute-start | bytes 49160 | tf_op jit(solution)/shard_map/ppermute | solution.py:428
  41.1 0.0 collective-permute-done.8
  41.2 4.1 %collective-permute-done.9.hodd = f32[32,128]{1,0:T(8,128)S(1)} collective-permute-done((f32[32,128]{1,0:T(8,128)S(1)}, f32[32,128]{1,0:T(8,128)S(1)}, u32[]{:S(2)}, u32[]{:S(2)}) %collective-permute-start.9) | collective-permute-done | bytes 16416 | tf_op jit(solution)/shard_map/ppermute | solution.py:428
  45.3 9.9 %up.1 = f32[256,128]{1,0:T(8,128)} custom-call(f32[512,128]{1,0:T(8,128)S(1)} %constant_dynamic-update-slice_fusion.9.gathered, f32[32,128]{1,0:T(8,128)S(1)} %slice.9.heven, f32[32,128]{1,0:T(8,128)S(1)} %collective-permute-done.9.hodd, f32[6,640,128]{2,1,0:T(8,128)S(1)} %get-tuple-element.19.keep0, f32[6,224,128]{2,1,0:T(8,128)S(1)} %get-tuple-element.20.keep1), custom_call_target="tpu_custom_call" | custom-call | tf_op jit(solution)/shard_map/up/pallas_call | solution.py:509
  (11 shorter events, 0.1 us)
Async XLA Ops:
  0.0 0.9 %copy-start = (f32[16,16,128]{2,1,0:T(8,128)S(1)}, f32[16,16,128]{2,1,0:T(8,128)}, u32[]{:S(2)}) copy-start(f32[16,16,128]{2,1,0:T(8,128)} %param.3) | copy-start | bytes 393220
  0.9 0.9 %copy-start.1 = (f32[16,16,128]{2,1,0:T(8,128)S(1)}, f32[16,16,128]{2,1,0:T(8,128)}, u32[]{:S(2)}) copy-start(f32[16,16,128]{2,1,0:T(8,128)} %param.4) | copy-start | bytes 393220
  1.8 0.9 %copy-start.2 = (f32[16,16,128]{2,1,0:T(8,128)S(1)}, f32[16,16,128]{2,1,0:T(8,128)}, u32[]{:S(2)}) copy-start(f32[16,16,128]{2,1,0:T(8,128)} %param.5) | copy-start | bytes 393220
  3.7 5.8 %collective-permute-start = (f32[304,128]{1,0:T(8,128)S(1)}, f32[304,128]{1,0:T(8,128)S(1)}, u32[]{:S(2)}, u32[]{:S(2)}) collective-permute-start(f32[304,128]{1,0:T(8,128)S(1)} %get-tuple-element.14), channel_id=1, source_target_pairs={{0,2},{2,0},{4,6},{6,4},{8,10},{10,8},{12,14},{14,12},{16,18},{18,... | collective-permute-start | bytes 466952 | tf_op jit(solution)/shard_map/ppermute | solution.py:422
  5.2 9.2 %collective-permute-start.1 = (f32[304,128]{1,0:T(8,128)S(1)}, f32[304,128]{1,0:T(8,128)S(1)}, u32[]{:S(2)}, u32[]{:S(2)}) collective-permute-start(f32[304,128]{1,0:T(8,128)S(1)} %get-tuple-element.15), channel_id=1, source_target_pairs={{2,4},{6,8},{10,12},{14,16},{18,20},{22,24},{26,28},{4,2},{8,6},{1... | collective-permute-start | bytes 466952 | tf_op jit(solution)/shard_map/ppermute | solution.py:428
  8.5 6.0 %collective-permute-start.2 = (f32[768,128]{1,0:T(8,128)S(1)}, f32[768,128]{1,0:T(8,128)S(1)}, u32[]{:S(2)}, u32[]{:S(2)}) collective-permute-start(f32[768,128]{1,0:T(8,128)S(1)} %get-tuple-element.13.own), channel_id=1, source_target_pairs={{0,1},{1,0},{2,3},{3,2},{4,5},{5,4},{6,7},{7,6},{8,9},{9,8},{10,11... | collective-permute-start | bytes 1179656 | tf_op jit(solution)/shard_map/ppermute | solution.py:422
  14.4 1.7 %collective-permute-start.3 = (f32[608,128]{1,0:T(8,128)S(1)}, f32[608,128]{1,0:T(8,128)S(1)}, u32[]{:S(2)}, u32[]{:S(2)}) collective-permute-start(f32[608,128]{1,0:T(8,128)S(1)} %pad_maximum_fusion), channel_id=1, source_target_pairs={{0,1},{1,0},{2,3},{3,2},{4,5},{5,4},{6,7},{7,6},{8,9},{9,8},{10,11... | collective-permute-start | bytes 933896 | tf_op jit(solution)/shard_map/ppermute | solution.py:422
  20.9 4.6 %collective-permute-start.4 = (f32[16,128]{1,0:T(8,128)S(1)}, f32[16,128]{1,0:T(8,128)S(1)}, u32[]{:S(2)}, u32[]{:S(2)}) collective-permute-start(f32[16,128]{1,0:T(8,128)S(1)} %get-tuple-element.16), channel_id=1, source_target_pairs={{0,16},{2,18},{4,20},{6,22},{8,24},{10,26},{12,28},{14,30},{16,0},... | collective-permute-start | bytes 24584 | tf_op jit(solution)/shard_map/ppermute | solution.py:422
  25.6 3.7 %collective-permute-start.5 = (f32[32,128]{1,0:T(8,128)S(1)}, f32[32,128]{1,0:T(8,128)S(1)}, u32[]{:S(2)}, u32[]{:S(2)}) collective-permute-start(f32[32,128]{1,0:T(8,128)S(1)} %pad_maximum_fusion.2), channel_id=1, source_target_pairs={{0,8},{2,10},{4,12},{6,14},{8,0},{10,2},{12,4},{14,6},{16,24},{18,... | collective-permute-start | bytes 49160 | tf_op jit(solution)/shard_map/ppermute | solution.py:422
  29.3 3.9 %collective-permute-start.6 = (f32[64,128]{1,0:T(8,128)S(1)}, f32[64,128]{1,0:T(8,128)S(1)}, u32[]{:S(2)}, u32[]{:S(2)}) collective-permute-start(f32[64,128]{1,0:T(8,128)S(1)} %pad_maximum_fusion.1), channel_id=1, source_target_pairs={{0,4},{2,6},{4,0},{6,2},{8,12},{10,14},{12,8},{14,10},{16,20},{18,... | collective-permute-start | bytes 98312 | tf_op jit(solution)/shard_map/ppermute | solution.py:422
  33.2 4.5 %collective-permute-start.7 = (f32[160,128]{1,0:T(8,128)S(1)}, f32[160,128]{1,0:T(8,128)S(1)}, u32[]{:S(2)}, u32[]{:S(2)}) collective-permute-start(f32[160,128]{1,0:T(8,128)S(1)} %constant_dynamic-update-slice_fusion), channel_id=1, source_target_pairs={{0,2},{2,0},{4,6},{6,4},{8,10},{10,8},{12,14},{14,12},{16,18},{18,... | collective-permute-start | bytes 245768 | tf_op jit(solution)/shard_map/ppermute | solution.py:422
  37.8 3.4 %collective-permute-start.8 = (f32[256,128]{1,0:T(8,128)S(1)}, f32[256,128]{1,0:T(8,128)S(1)}, u32[]{:S(2)}, u32[]{:S(2)}) collective-permute-start(f32[256,128]{1,0:T(8,128)S(1)} %get-tuple-element.21), channel_id=1, source_target_pairs={{0,1},{1,0},{2,3},{3,2},{4,5},{5,4},{6,7},{7,6},{8,9},{9,8},{10,11... | collective-permute-start | bytes 393224 | tf_op jit(solution)/shard_map/ppermute | solution.py:422
  37.8 7.4 %collective-permute-start.9 = (f32[32,128]{1,0:T(8,128)S(1)}, f32[32,128]{1,0:T(8,128)S(1)}, u32[]{:S(2)}, u32[]{:S(2)}) collective-permute-start(f32[32,128]{1,0:T(8,128)S(1)} %get-tuple-element.18), channel_id=1, source_target_pairs={{2,4},{6,8},{10,12},{14,16},{18,20},{22,24},{26,28},{4,2},{8,6},{1... | collective-permute-start | bytes 49160 | tf_op jit(solution)/shard_map/ppermute | solution.py:428

commit v3 on v2

--- a/solution.py
+++ b/solution.py
@@ -198,14 +198,6 @@
     return copy
 
 
-def rev(x, bits):
-    return sum(((x >> k) & 1) << (bits - 1 - k) for k in range(bits)) if bits else 0
-
-
-def bits_of(n):
-    return n.bit_length() - 1
-
-
 def pack_kernel(bx, bz, rhs, alpha, beta, even, odd, own, sem):
     up = 1 - lax.axis_index("wide") % 2
     waits = []
@@ -300,7 +292,12 @@
     which = lax.broadcasted_iota(jnp.int32, (n2, LANES), 1) % 4
     part[0] = jnp.where(which == 0, part[0], jnp.where(which == 1, part[1], part[2]))
     share = n2 // n_narrow
-    packed[...] = part[0, pl.ds(pl.multiple_of(narrow * share, 8), share), :]
+    mine = part[0, pl.ds(pl.multiple_of(narrow * share, 8), share), :]
+
+    def spread(i):
+        packed[pl.ds(i * share, share), :] = mine
+
+    each(n_wide * n_narrow, share, spread)
     for copy in waits:
         copy.wait()
 
@@ -310,7 +307,7 @@
 
 
 def up_kernel(
-    bx, bz, n_wide, n_narrow, gathered, heven, hodd, keep0, keep1, out, lev2, lev3, lev4, lev5, lev0, lev1, tmp, sem, sem0, sem1
+    bx, bz, n_wide, n_narrow, gathered, heven, hodd, keep0, keep1, out, lev2, lev3, lev4, lev5, lev0, lev1, near2, near3, tmp, sem0, sem1
 ):
     wide = lax.axis_index("wide")
     narrow = lax.axis_index("narrow")
@@ -322,9 +319,6 @@
             copy = pltpu.make_async_copy(kept.at[q], lev.at[q, pl.ds(r, kept.shape[1])], done.at[q])
             copy.start()
             fetch.append(copy)
-    m = margin(zw // 4, 2)
-    arrive = pltpu.make_async_copy(gathered, lev2.at[U, pl.ds(m, n_wide * bx // 4 * (zw // 4))], sem)
-    arrive.start()
     levels = []
     for index, ref in enumerate((lev2, lev3, lev4, lev5), 2):
         zl = zw // 2**index
@@ -340,21 +334,16 @@
     planes2 = bx // 4
     n2 = planes2 * l2.zw
     n = n2 // n_narrow
-    bw, bn = bits_of(n_wide), bits_of(n_narrow)
-    me = rev(wide, bw) + n_wide * rev(narrow, bn)
     lane = lax.broadcasted_iota(jnp.int32, (n, LANES), 1) % 4
 
     def unpack(i):
-        w, c = i // n_narrow, i % n_narrow
-        at = me ^ (rev(w, bw) + n_wide * rev(c, bn))
-        p = l2.get(U, pl.multiple_of(l2.base + at * n, 8), n)
+        p = gathered[pl.ds(i * n, n), :]
         for q, k, first, second in ((F, 0, 1, 2), (A, 1, LANES - 1, 2), (B, 2, 1, LANES - 2)):
             t = jnp.where(lane == k, p, 0.0)
             t = t + pltpu.roll(t, first, 1)
             t = t + pltpu.roll(t, second, 1)
             l2.put(q, l2.base + i * n, t)
 
-    arrive.wait()
     each(n_wide * n_narrow, n, unpack)
 
     def chunk_of(level):
@@ -372,7 +361,7 @@
     for level, coarse in ((l2, l3), (l3, l4), (l4, l5)):
         level.setup(0, level.nx, chunk_of(level))
         level.sweep(U, B, 0, level.nx, chunk_of(level))
-        down(level, coarse, F, lambda r, m, level=level: level.residual(B, r, m), tmp.at[2])
+        down(level, coarse, F, lambda r, m, level=level: level.residual(B, r, m), tmp.at[0])
     l5.setup(0, l5.nx, chunk_of(l5))
     src, dst = U, B
     for _ in range(BOTTOM - 1):
@@ -388,12 +377,20 @@
         level.sweep(U, B, 0, level.nx, chunk_of(level))
         coarse, src = level, B
     start = wide * planes2
-    r2 = pl.multiple_of(l2.base + start * l2.zw, 8)
-    near2 = l2.moved(r2)
-    near3 = l3.moved(l3.base + (start // 2) * l3.zw)
-    prolong_planes(near3, B, -2, planes2 // 2 + 4, near2, B, B, -4, tmp.at[1], 2 if l2.zw < 16 else 1)
-    near2.sweep(B, U, -3, planes2 + 6, 2)
-    near2.sweep(U, B, -2, planes2 + 4, 2)
+    w2 = Level(near2, l2.zw, 2)
+    w3 = Level(near3, l3.zw, 3)
+
+    def window(src, q, dst, k, first, count):
+        n = count * src.zw
+        dst.put(k, 0, src.get(q, pl.multiple_of(src.base + first * src.zw, 8), n))
+
+    window(l3, B, w3, 0, start // 2 - 2, planes2 // 2 + 4)
+    for q in (F, W, CX, CZ, CY):
+        window(l2, q, w2, q, start - 4, planes2 + 8)
+    window(l2, B, w2, U, start - 4, planes2 + 8)
+    prolong_planes(w3, 0, 0, planes2 // 2 + 4, w2, U, U, 0, tmp.at[1], 2 if l2.zw < 16 else 1)
+    w2.sweep(U, KEPT, 1, planes2 + 6, 2)
+    w2.sweep(KEPT, U, 2, planes2 + 4, 2)
     for copy in fetch:
         copy.wait()
     l1 = Level(lev1, z1, 1)
@@ -402,7 +399,7 @@
     above, below = H1 + bx // 2 + 2, 1
     l1.put(U, pl.multiple_of((up * above + (1 - up) * below) * z1, 8), heven[...])
     l1.put(U, pl.multiple_of(((1 - up) * above + up * below) * z1, 8), hodd[...])
-    prolong_planes(near2, B, -2, count1 // 2, l1, U, U, 0, tmp.at[0])
+    prolong_planes(w2, U, 2, count1 // 2, l1, U, U, 0, tmp.at[0])
     l1.sweep(U, KEPT, 2, count1 - 4, 1)
     l1.sweep(KEPT, U, 3, count1 - 6, 1)
     l0 = Level(lev0, zw, 0)
@@ -452,16 +449,16 @@
 
     def params(scratch, rows):
         size = 4 * sum(math.prod(t.shape) for t in scratch[:-2]) + 4 * lanes * rows
-        return pltpu.CompilerParams(vmem_limit_bytes=min(63 * 2**20, size + size // 8 + 2**21))
+        return pltpu.CompilerParams(vmem_limit_bytes=min(255 * 2**18, size + size // 8 + 2**21))
 
     face = jax.ShapeDtypeStruct(((3 * H - 2) * bz, lanes), f32)
     even, odd, own = pl.pallas_call(
         functools.partial(pack_kernel, bx, bz),
         out_shape=[face, face, jax.ShapeDtypeStruct((3 * bx * bz, lanes), f32)],
-        in_specs=[hbm] * 3,
+        in_specs=[pl.BlockSpec(memory_space=pltpu.HBM)] * 3,
         out_specs=[vmem] * 3,
         scratch_shapes=[pltpu.SemaphoreType.DMA((9,))],
-        compiler_params=pltpu.CompilerParams(vmem_limit_bytes=2**22),
+        compiler_params=pltpu.CompilerParams(vmem_limit_bytes=62 * 2**20),
         name="pack",
     )(flat(rhs), flat(alpha), flat(beta))
     even = swap(even, "wide", 0)
@@ -477,23 +474,15 @@
     ]
     packed, ueven, uodd, keep0, keep1 = pl.pallas_call(
         functools.partial(down_kernel, bx, bz, n_wide, n_narrow),
-        out_shape=[jax.ShapeDtypeStruct((n2 // n_narrow, lanes), f32), u_face, u_face, keep0, keep1],
+        out_shape=[jax.ShapeDtypeStruct((n_wide * n2, lanes), f32), u_face, u_face, keep0, keep1],
         in_specs=[vmem] * 5,
         out_specs=[vmem, vmem, vmem, hbm, hbm],
         scratch_shapes=scratch,
         compiler_params=params(scratch, 3 * planes * zw),
         name="down",
     )(own, even, odd, other, others)
-    hodd = swap_odd(uodd)
-    gathered = packed
-    for bit in reversed(range(bits_of(n_wide))):
-        rows = gathered.shape[0]
-        sent = jnp.concatenate([gathered, ueven]) if bit == 0 else gathered
-        came = swap(sent, "wide", bit)
-        gathered = jnp.concatenate([gathered, came[:rows]])
-    heven = came[rows:]
-    for bit in reversed(range(bits_of(n_narrow))):
-        gathered = jnp.concatenate([gathered, swap(gathered, "narrow", bit)])
+    heven, hodd = swap(ueven, "wide", 0), swap_odd(uodd)
+    gathered = lax.all_to_all(packed, ("wide", "narrow"), 0, 0, tiled=True)
     nx = n_wide * bx
     scratch = []
     for index in range(2, LEVELS):
@@ -502,17 +491,18 @@
     scratch += [
         pltpu.VMEM((KEPT + 1, *keep0.shape[1:]), f32),
         pltpu.VMEM((KEPT + 1, (p1 + 2) * (zw // 2), lanes), f32),
-        pltpu.VMEM((3, max((bx // 2 + 2) * zw, LONGEST // 2), lanes), f32),
-        pltpu.SemaphoreType.DMA,
+        pltpu.VMEM((KEPT + 1, (bx // 4 + 8) * (zw // 4), lanes), f32),
+        pltpu.VMEM((1, (bx // 8 + 4) * (zw // 8), lanes), f32),
+        pltpu.VMEM((2, LONGEST // 2, lanes), f32),
         *sems,
     ]
     out = pl.pallas_call(
         functools.partial(up_kernel, bx, bz, n_wide, n_narrow),
         out_shape=jax.ShapeDtypeStruct((bx * bz, lanes), f32),
-        in_specs=[hbm, vmem, vmem, hbm, hbm],
+        in_specs=[vmem, vmem, vmem, hbm, hbm],
         out_specs=vmem,
         scratch_shapes=scratch,
-        compiler_params=params(scratch[:-3] + sems, bx * bz),
+        compiler_params=params(scratch, bx * bz + n_wide * n2 + 2 * zw),
         name="up",
     )(gathered, heven, hodd, keep0, keep1)
     return out.reshape(bx, bz, lanes)

time: 55.3 us -> 43.7 us (0.79)
  the two profiles are of different devices: /device:TPU:24 before, /device:TPU:0 now
where the time goes in v3:
time: 43.7 us; the launch traced here: 43.4 us
  starting transfers between devices  15.7 us (36%)
  Pallas kernels  13.5 us (31%)
  waiting for transfers between devices  13.2 us (30%)
  local copies, waits for them, and re-layouts  1 us (2%)
    all_to_all x1, starting transfers between devices, shards(): gathered = lax.all_to_all(packed, ('wide', 'narrow'), 0, 0, tiled=True)  9.44 us
    all_to_all x1, waiting for transfers between devices, shards(): gathered = lax.all_to_all(packed, ('wide', 'narrow'), 0, 0, tiled=True)  6.66 us
    ppermute x4, waiting for transfers between devices, swap(): return lax.ppermute(array, axis, [(i, i ^ 1 << bit) for i in range(n)])  6.52 us
    pallas_call x1, Pallas kernels, shards(): pl.pallas_call(functools.partial(up_kernel, bx, bz, n_wide, n_narrow), ou...  5.77 us
    pallas_call x1, Pallas kernels, shards(): pl.pallas_call(functools.partial(down_kernel, bx, bz, n_wide, n_narrow),...  5.54 us
    ppermute x4, starting transfers between devices, swap(): return lax.ppermute(array, axis, [(i, i ^ 1 << bit) for i in range(n)])  4.98 us
    pallas_call x1, Pallas kernels, shards(): pl.pallas_call(functools.partial(pack_kernel, bx, bz), out_shape=[face, f...  2.14 us
    ppermute x2, starting transfers between devices, swap_odd(): return lax.ppermute(array, 'wide', pairs + [(j, i) for i, j in pairs])  1.31 us
  transfers between devices with their start and end apart: 7, of which 4 were waited for; matrix products, arithmetic and copies ran while one was open for 0% of the time, Pallas kernels for 0%

profile of v3, /device:TPU:0, one launch (start us, length us, event | category | flops | bytes accessed | tf_op | source)
XLA Modules:
  0.0 43.4 jit_solution(15613068258631967069)
XLA Ops:
  0.0 2.1 %pack.1 = (f32[304,128]{1,0:T(8,128)}, f32[304,128]{1,0:T(8,128)}, f32[768,128]{1,0:T(8,128)}) custom-call(f32[256,128]{1,0:T(8,128)} %bitcast.7, f32[256,128]{1,0:T(8,128)} %bitcast.8, f32[256,128]{1,0:T(8,128)} %bitcast.9), custom_call_target="tpu_custom_call" | custom-call | tf_op jit(solution)/shard_map/pack/pallas_call | solution.py:455
  2.1 3.0 %collective-permute-start = (f32[304,128]{1,0:T(8,128)}, f32[304,128]{1,0:T(8,128)S(1)}, u32[]{:S(2)}, u32[]{:S(2)}) collective-permute-start(f32[304,128]{1,0:T(8,128)} %get-tuple-element.14), channel_id=1, source_target_pairs={{0,2},{2,0},{4,6},{6,4},{8,10},{10,8},{12,14},{14,12},{16,18},{18,... | collective-permute-start | bytes 466952 | tf_op jit(solution)/shard_map/ppermute | solution.py:419
  5.2 0.7 %collective-permute-start.1 = (f32[304,128]{1,0:T(8,128)}, f32[304,128]{1,0:T(8,128)S(1)}, u32[]{:S(2)}, u32[]{:S(2)}) collective-permute-start(f32[304,128]{1,0:T(8,128)} %get-tuple-element.15), channel_id=1, source_target_pairs={{2,4},{6,8},{10,12},{14,16},{18,20},{22,24},{26,28},{4,2},{8,6},{1... | collective-permute-start | bytes 466952 | tf_op jit(solution)/shard_map/ppermute | solution.py:425
  5.8 0.1 collective-permute-start.2
  5.9 3.5 %collective-permute-done.even = f32[304,128]{1,0:T(8,128)S(1)} collective-permute-done((f32[304,128]{1,0:T(8,128)}, f32[304,128]{1,0:T(8,128)S(1)}, u32[]{:S(2)}, u32[]{:S(2)}) %collective-permute-start) | collective-permute-done | bytes 155680 | tf_op jit(solution)/shard_map/ppermute | solution.py:419
  9.4 0.0 collective-permute-done.1.odd
  9.4 0.1 collective-permute-start.3
  9.5 0.0 collective-permute-done.2.other
  9.5 1.6 %collective-permute-done.3.others = f32[608,128]{1,0:T(8,128)S(1)} collective-permute-done((f32[608,128]{1,0:T(8,128)S(1)}, f32[608,128]{1,0:T(8,128)S(1)}, u32[]{:S(2)}, u32[]{:S(2)}) %collective-permute-start.3) | collective-permute-done | bytes 311328 | tf_op jit(solution)/shard_map/ppermute | solution.py:419
  11.1 0.0 copy-start
  11.1 1.0 %copy-done = f32[768,128]{1,0:T(8,128)S(1)} copy-done((f32[768,128]{1,0:T(8,128)S(1)}, f32[768,128]{1,0:T(8,128)}, u32[]{:S(2)}) %copy-start) | copy-done | bytes 393240
  12.1 5.5 %down.1 = (f32[512,128]{1,0:T(8,128)}, f32[32,128]{1,0:T(8,128)S(1)}, f32[32,128]{1,0:T(8,128)S(1)}, f32[6,640,128]{2,1,0:T(8,128)S(1)}, f32[6,224,128]{2,1,0:T(8,128)S(1)}) custom-call(f32[768,128]{1,0:T(8,128)S(1)} %copy-done, f32[304,128]{1,0:T(8,128)S(1)} %collective-permute-done.even, f32[304,128]{1,0:T(8,128)S(1)} %collective-permute-done.1.odd, ...), custom_call_target="tpu_custom_call" | custom-call | tf_op jit(solution)/shard_map/down/pallas_call | solution.py:475
  17.6 9.4 %all-to-all-start = ((f32[32,16,128]{2,1,0:T(8,128)}), f32[32,16,128]{2,1,0:T(8,128)S(1)}, u32[]{:S(2)}, u32[]{:S(2)}) async-start(f32[32,16,128]{2,1,0:T(8,128)} %bitcast.3), calls=%async_computation | async-start | bytes 524288 | tf_op jit(solution)/shard_map/all_to_all | solution.py:485
  27.1 1.8 %collective-permute-start.4 = (f32[32,128]{1,0:T(8,128)S(1)}, f32[32,128]{1,0:T(8,128)S(1)}, u32[]{:S(2)}, u32[]{:S(2)}) collective-permute-start(f32[32,128]{1,0:T(8,128)S(1)} %get-tuple-element.17), channel_id=1, source_target_pairs={{0,2},{2,0},{4,6},{6,4},{8,10},{10,8},{12,14},{14,12},{16,18},{18,... | collective-permute-start | bytes 49160 | tf_op jit(solution)/shard_map/ppermute | solution.py:419
  28.9 0.7 %collective-permute-start.5 = (f32[32,128]{1,0:T(8,128)S(1)}, f32[32,128]{1,0:T(8,128)S(1)}, u32[]{:S(2)}, u32[]{:S(2)}) collective-permute-start(f32[32,128]{1,0:T(8,128)S(1)} %get-tuple-element.18), channel_id=1, source_target_pairs={{2,4},{6,8},{10,12},{14,16},{18,20},{22,24},{26,28},{4,2},{8,6},{1... | collective-permute-start | bytes 49160 | tf_op jit(solution)/shard_map/ppermute | solution.py:425
  29.6 1.4 %collective-permute-done.4.heven = f32[32,128]{1,0:T(8,128)S(1)} collective-permute-done((f32[32,128]{1,0:T(8,128)S(1)}, f32[32,128]{1,0:T(8,128)S(1)}, u32[]{:S(2)}, u32[]{:S(2)}) %collective-permute-start.4) | collective-permute-done | bytes 16416 | tf_op jit(solution)/shard_map/ppermute | solution.py:419
  31.0 0.0 collective-permute-done.5.hodd
  31.0 6.7 %all-to-all-done = f32[32,16,128]{2,1,0:T(8,128)S(1)} async-done(((f32[32,16,128]{2,1,0:T(8,128)}), f32[32,16,128]{2,1,0:T(8,128)S(1)}, u32[]{:S(2)}, u32[]{:S(2)}) %all-to-all-start) | async-done | bytes 262176 | tf_op jit(solution)/shard_map/all_to_all | solution.py:485
  37.7 5.8 %up.1 = f32[256,128]{1,0:T(8,128)} custom-call(f32[512,128]{1,0:T(8,128)S(1)} %bitcast.6, f32[32,128]{1,0:T(8,128)S(1)} %collective-permute-done.4.heven, f32[32,128]{1,0:T(8,128)S(1)} %collective-permute-done.5.hodd, f32[6,640,128]{2,1,0:T(8,128)S(1)} %get-tuple-element.19.keep0, f32[6,224,128]{2,1,0:T(8,128)S(1)} %get-tuple-element.20.keep1), custom_call_target="tpu_custom_call" | custom-call | tf_op jit(solution)/shard_map/up/pallas_call | solution.py:499
  (1 shorter events, 0.0 us)
Async XLA Ops:
  2.1 7.2 %collective-permute-start = (f32[304,128]{1,0:T(8,128)}, f32[304,128]{1,0:T(8,128)S(1)}, u32[]{:S(2)}, u32[]{:S(2)}) collective-permute-start(f32[304,128]{1,0:T(8,128)} %get-tuple-element.14), channel_id=1, source_target_pairs={{0,2},{2,0},{4,6},{6,4},{8,10},{10,8},{12,14},{14,12},{16,18},{18,... | collective-permute-start | bytes 466952 | tf_op jit(solution)/shard_map/ppermute | solution.py:419
  5.2 4.2 %collective-permute-start.1 = (f32[304,128]{1,0:T(8,128)}, f32[304,128]{1,0:T(8,128)S(1)}, u32[]{:S(2)}, u32[]{:S(2)}) collective-permute-start(f32[304,128]{1,0:T(8,128)} %get-tuple-element.15), channel_id=1, source_target_pairs={{2,4},{6,8},{10,12},{14,16},{18,20},{22,24},{26,28},{4,2},{8,6},{1... | collective-permute-start | bytes 466952 | tf_op jit(solution)/shard_map/ppermute | solution.py:425
  5.8 3.7 %collective-permute-start.2 = (f32[768,128]{1,0:T(8,128)}, f32[768,128]{1,0:T(8,128)S(1)}, u32[]{:S(2)}, u32[]{:S(2)}) collective-permute-start(f32[768,128]{1,0:T(8,128)} %get-tuple-element.13.own), channel_id=1, source_target_pairs={{0,1},{1,0},{2,3},{3,2},{4,5},{5,4},{6,7},{7,6},{8,9},{9,8},{10,11... | collective-permute-start | bytes 1179656 | tf_op jit(solution)/shard_map/ppermute | solution.py:419
  9.4 1.7 %collective-permute-start.3 = (f32[608,128]{1,0:T(8,128)S(1)}, f32[608,128]{1,0:T(8,128)S(1)}, u32[]{:S(2)}, u32[]{:S(2)}) collective-permute-start(f32[608,128]{1,0:T(8,128)S(1)} %pad_maximum_fusion), channel_id=1, source_target_pairs={{0,1},{1,0},{2,3},{3,2},{4,5},{5,4},{6,7},{7,6},{8,9},{9,8},{10,11... | collective-permute-start | bytes 933896 | tf_op jit(solution)/shard_map/ppermute | solution.py:419
  11.1 1.0 %copy-start = (f32[768,128]{1,0:T(8,128)S(1)}, f32[768,128]{1,0:T(8,128)}, u32[]{:S(2)}) copy-start(f32[768,128]{1,0:T(8,128)} %get-tuple-element.13.own) | copy-start | bytes 1179652
  17.6 20.0 %all-to-all-start = ((f32[32,16,128]{2,1,0:T(8,128)}), f32[32,16,128]{2,1,0:T(8,128)S(1)}, u32[]{:S(2)}, u32[]{:S(2)}) async-start(f32[32,16,128]{2,1,0:T(8,128)} %bitcast.3), calls=%async_computation | async-start | bytes 524288 | tf_op jit(solution)/shard_map/all_to_all | solution.py:485
  27.1 3.9 %collective-permute-start.4 = (f32[32,128]{1,0:T(8,128)S(1)}, f32[32,128]{1,0:T(8,128)S(1)}, u32[]{:S(2)}, u32[]{:S(2)}) collective-permute-start(f32[32,128]{1,0:T(8,128)S(1)} %get-tuple-element.17), channel_id=1, source_target_pairs={{0,2},{2,0},{4,6},{6,4},{8,10},{10,8},{12,14},{14,12},{16,18},{18,... | collective-permute-start | bytes 49160 | tf_op jit(solution)/shard_map/ppermute | solution.py:419
  28.9 2.1 %collective-permute-start.5 = (f32[32,128]{1,0:T(8,128)S(1)}, f32[32,128]{1,0:T(8,128)S(1)}, u32[]{:S(2)}, u32[]{:S(2)}) collective-permute-start(f32[32,128]{1,0:T(8,128)S(1)} %get-tuple-element.18), channel_id=1, source_target_pairs={{2,4},{6,8},{10,12},{14,16},{18,20},{22,24},{26,28},{4,2},{8,6},{1... | collective-permute-start | bytes 49160 | tf_op jit(solution)/shard_map/ppermute | solution.py:425

commit v4 on v3

--- a/solution.py
+++ b/solution.py
@@ -198,29 +198,67 @@
     return copy
 
 
-def pack_kernel(bx, bz, rhs, alpha, beta, even, odd, own, sem):
+def pack_kernel(bx, bz, rhs, alpha, beta, even, odd, sem):
     up = 1 - lax.axis_index("wide") % 2
     waits = []
-    at = [0, 0]
+    at = 0
     for q, (src, size) in enumerate(((rhs, H - 1), (alpha, H - 1), (beta, H))):
         for k, dst in enumerate((even, odd)):
             upper = up if k == 0 else 1 - up
             start = pl.multiple_of(upper * ((bx - size) * bz), 8)
             copy = pltpu.make_async_copy(
-                src.at[pl.ds(start, size * bz)], dst.at[pl.ds(at[k] * bz, size * bz)], sem.at[2 * q + k]
+                src.at[pl.ds(start, size * bz)], dst.at[pl.ds(at * bz, size * bz)], sem.at[2 * q + k]
             )
             copy.start()
             waits.append(copy)
-            at[k] += size
-        copy = pltpu.make_async_copy(src, own.at[pl.ds(q * bx * bz, bx * bz)], sem.at[6 + q])
-        copy.start()
-        waits.append(copy)
+        at += size
     for copy in waits:
         copy.wait()
 
 
+def z_of(narrow, k, n_narrow):
+    return 1 - narrow if n_narrow == 2 else lax.rem(narrow + 1 + k, n_narrow)
+
+
+def spread4(p, lane, k):
+    t = jnp.where(lane == k, p, 0.0)
+    t = t + pltpu.roll(t, 1 if k % 2 == 0 else LANES - 1, 1)
+    return t + pltpu.roll(t, 2 if k < 2 else LANES - 2, 1)
+
+
+def coarsen_kernel(bx, bz, n_wide, n_narrow, alpha, beta, other_a, other_b, packed, fine, mid, part, tmp):
+    zw = bz * n_narrow
+    narrow = lax.axis_index("narrow")
+    z2 = zw // 4
+    for q, own, other in ((0, alpha, other_a), (1, beta, other_b)):
+
+        def place(i, q=q, own=own, other=other):
+            fine[q, pl.ds(pl.multiple_of(i * zw + narrow * bz, 8), bz), :] = own[pl.ds(i * bz, bz), :]
+            for k in range(n_narrow - 1):
+                r = pl.multiple_of(i * zw + z_of(narrow, k, n_narrow) * bz, 8)
+                fine[q, pl.ds(r, bz), :] = other[pl.ds((k * bx + i) * bz, bz), :]
+
+        each(bx, zw, place)
+    l0, l1, l2 = Level(fine, zw, 0), Level(mid, zw // 2, 1), Level(part, z2, 2)
+    for q in range(2):
+        restrict_planes(lambda r, n, q=q: l0.get(q, r, n), l0, 0, bx // 2, l1, q, 0, tmp.at[q], 1)
+        restrict_planes(lambda r, n, q=q: l1.get(q, r, n), l1, 0, bx // 4, l2, q, 0, tmp.at[q], 1)
+    lane = lax.broadcasted_iota(jnp.int32, (z2, LANES), 1) % 4
+    for k in range(bx // 8):
+        a0, a1 = l2.get(0, 2 * k * z2, z2), l2.get(0, (2 * k + 1) * z2, z2)
+        b0, b1 = l2.get(1, 2 * k * z2, z2), l2.get(1, (2 * k + 1) * z2, z2)
+        l2.put(2, k * z2, jnp.where(lane == 0, a0, jnp.where(lane == 1, b0, jnp.where(lane == 2, a1, b1))))
+    mine = part[2, pl.ds(pl.multiple_of(narrow * 8, 8), 8), :]
+
+    def spread(i):
+        packed[pl.ds(i * 8, 8), :] = mine
+
+    each(n_wide * n_narrow, 8, spread)
+
+
 def down_kernel(
-    bx, bz, n_wide, n_narrow, own, even, odd, other, others, packed, ueven, uodd, keep0, keep1, lev0, lev1, part, tmp, sem0, sem1
+    bx, bz, n_wide, n_narrow, rhs, alpha, beta, even, odd, other_r, other_a, other_b, others, packed, keep0, keep1, lev0, lev1,
+    part, tmp, sem0, sem1
 ):
     zw = bz * n_narrow
     planes = bx + 2 * H
@@ -239,16 +277,16 @@
 
     g = H - 1
     all_h = 2 * g + H
-    for index, (q, at, size) in enumerate(((F, 0, g), (A, g, g), (B, 2 * g, H))):
+    for q, at, size, own, other in ((F, 0, g, rhs, other_r), (A, g, g, alpha, other_a), (B, 2 * g, H, beta, other_b)):
         above, below = H + bx, H - size
         p_even = up * above + (1 - up) * below
         p_odd = (1 - up) * above + up * below
-        place(q, own, index * bx, bx, H, narrow * bz)
+        place(q, own, 0, bx, H, narrow * bz)
         place(q, even, at, size, p_even, narrow * bz)
         place(q, odd, at, size, p_odd, narrow * bz)
         for k in range(n_narrow - 1):
-            z = (1 - narrow if n_narrow == 2 else lax.rem(narrow + 1 + k, n_narrow)) * bz
-            place(q, other, (3 * k + index) * bx, bx, H, z)
+            z = z_of(narrow, k, n_narrow) * bz
+            place(q, other, k * bx, bx, H, z)
             place(q, others, 2 * k * all_h + at, size, p_even, z)
             place(q, others, (2 * k + 1) * all_h + at, size, p_odd, z)
     first0, count0 = H - 2, bx + 4
@@ -276,38 +314,52 @@
     z2 = zw // 4
     n2 = k2 * z2
     l2 = Level(part, z2, 2)
-    restrict_planes(lambda r, n: l1.get(A, r, n), l1, H1, k2, l2, 1, 0, tmp.at[1], 1)
-    restrict_planes(lambda r, n: l1.get(B, r, n), l1, H1, k2, l2, 2, 0, tmp.at[0], 1)
     l1.first_cx(0)
     l1.put(CZ, 0, jnp.zeros((l1.zw, LANES), jnp.float32))
     l1.setup(1, p1 - 2, 1, valid1)
     l1.sweep(U, V, 2, p1 - 4, 1)
     waits += [keep(l1, q, 0, p1, keep1, q, sem1) for q in (F, W, CX, CZ, CY)]
     waits.append(keep(l1, V, 0, p1, keep1, U, sem1))
-    n1 = 2 * l1.zw
-    upper, lower = H1 + bx // 2 - 3, H1 + 1
-    ueven[...] = l1.get(V, pl.multiple_of((up * upper + (1 - up) * lower) * l1.zw, 8), n1)
-    uodd[...] = l1.get(V, pl.multiple_of(((1 - up) * upper + up * lower) * l1.zw, 8), n1)
     restrict_planes(lambda r, n: l1.residual(V, r, n), l1, H1, k2, l2, 0, 0, tmp.at[2], 1)
-    which = lax.broadcasted_iota(jnp.int32, (n2, LANES), 1) % 4
-    part[0] = jnp.where(which == 0, part[0], jnp.where(which == 1, part[1], part[2]))
-    share = n2 // n_narrow
-    mine = part[0, pl.ds(pl.multiple_of(narrow * share, 8), share), :]
+    which = lax.broadcasted_iota(jnp.int32, (z2, LANES), 1) % 4
+    f2 = [part[0, pl.ds(k * z2, z2), :] for k in range(4)]
+    part[1, pl.ds(0, z2), :] = jnp.where(
+        which == 0, f2[0], jnp.where(which == 1, f2[1], jnp.where(which == 2, f2[2], f2[3]))
+    )
+    mine = part[1, pl.ds(pl.multiple_of(narrow // 2 * 8, 8), 8), :]
+    first = jnp.broadcast_to(lax.broadcasted_iota(jnp.int32, (8, LANES), 1) % 2 == 0, (8, LANES))
+
+    def face(plane):
+        r = pl.multiple_of((H1 + plane) * l1.zw + narrow * 8, 8)
+        return jnp.where(first, l1.get(V, r, 8), l1.get(V, pl.multiple_of(r + l1.zw, 8), 8))
+
+    upper, lower = face(bx // 2 - 3), face(1)
 
     def spread(i):
-        packed[pl.ds(i * share, share), :] = mine
-
-    each(n_wide * n_narrow, share, spread)
+        packed[pl.ds(i * 16, 8), :] = mine
+        packed[pl.ds(i * 16 + 8, 8), :] = upper
+
+    each(n_wide * n_narrow, 16, spread)
+
+    @pl.when(wide > 0)
+    def _():
+        for c in range(n_narrow):
+            packed[pl.ds(pl.multiple_of(((wide - 1) * n_narrow + c) * 16 + 8, 8), 8), :] = lower
+
     for copy in waits:
         copy.wait()
 
 
+def big(devices):
+    return devices > 64
+
+
 def margin(zl, index):
     return max(8, (4 if index == 2 else 2) * zl)
 
 
 def up_kernel(
-    bx, bz, n_wide, n_narrow, gathered, heven, hodd, keep0, keep1, out, lev2, lev3, lev4, lev5, lev0, lev1, near2, near3, tmp, sem0, sem1
+    bx, bz, n_wide, n_narrow, gathered, coarse, keep0, keep1, out, lev2, lev3, lev4, lev5, lev0, lev1, near2, near3, faces, tmp, sem0, sem1
 ):
     wide = lax.axis_index("wide")
     narrow = lax.axis_index("narrow")
@@ -332,19 +384,48 @@
             level.put(q, m + level.nx * zl, zero)
     l2, l3, l4, l5 = levels
     planes2 = bx // 4
-    n2 = planes2 * l2.zw
-    n = n2 // n_narrow
-    lane = lax.broadcasted_iota(jnp.int32, (n, LANES), 1) % 4
-
-    def unpack(i):
-        p = gathered[pl.ds(i * n, n), :]
-        for q, k, first, second in ((F, 0, 1, 2), (A, 1, LANES - 1, 2), (B, 2, 1, LANES - 2)):
-            t = jnp.where(lane == k, p, 0.0)
-            t = t + pltpu.roll(t, first, 1)
-            t = t + pltpu.roll(t, second, 1)
-            l2.put(q, l2.base + i * n, t)
-
-    each(n_wide * n_narrow, n, unpack)
+    z2 = l2.zw
+    devices = n_wide * n_narrow
+    if big(devices):
+        for src, q in ((gathered, U), (coarse, W)):
+            dst = lev2.at[q, pl.ds(l2.base, src.shape[0])]
+            pltpu.sync_copy(src, dst)
+        read = lambda r: l2.get(U, l2.base + r, 8)
+        read_ab = lambda r: l2.get(W, l2.base + r, 8)
+    else:
+        read = lambda r: gathered[pl.ds(r, 8), :]
+        read_ab = lambda r: coarse[pl.ds(r, 8), :]
+    lane = lax.broadcasted_iota(jnp.int32, (8, LANES), 1) % 4
+
+    def unpack_ab(i):
+        w, c = i // n_narrow, i % n_narrow
+        p = read_ab(i * 8)
+        pair, z = c * 8 // z2, c * 8 % z2
+        r = l2.base + (w * planes2 + 2 * pair) * z2 + z
+        for k, (q, plane) in enumerate(((A, 0), (B, 0), (A, 1), (B, 1))):
+            l2.put(q, r + plane * z2, spread4(p, lane, k))
+
+    each(devices, 32, unpack_ab)
+
+    def unpack_f(i):
+        w, h = i // (n_narrow // 2), i % (n_narrow // 2)
+        p = read((w * n_narrow + 2 * h) * 16)
+        r = l2.base + w * planes2 * z2 + h * 8
+        for k in range(4):
+            l2.put(F, r + k * z2, spread4(p, lane, k))
+
+    each(devices // 2, 32, unpack_f)
+    even_lane = lane % 2 == 0
+    for k, by in ((0, -1), (1, 1)):
+        there = wide + by
+        valid = jnp.logical_and(there >= 0, there < n_wide)
+        there = jnp.clip(there, 0, n_wide - 1)
+        for c in range(n_narrow):
+            p = jnp.where(valid, read(pl.multiple_of((there * n_narrow + c) * 16 + 8, 8)), 0.0)
+            t = jnp.where(even_lane, p, 0.0)
+            faces[k, pl.ds(c * 8, 8), :] = t + pltpu.roll(t, 1, 1)
+            t = p - t
+            faces[k, pl.ds(z1 + c * 8, 8), :] = t + pltpu.roll(t, LANES - 1, 1)
 
     def chunk_of(level):
         return max(1, min(32 // level.zw, level.nx))
@@ -395,10 +476,8 @@
         copy.wait()
     l1 = Level(lev1, z1, 1)
     count1 = bx // 2 + 2 * H1 + 2
-    up = 1 - wide % 2
-    above, below = H1 + bx // 2 + 2, 1
-    l1.put(U, pl.multiple_of((up * above + (1 - up) * below) * z1, 8), heven[...])
-    l1.put(U, pl.multiple_of(((1 - up) * above + up * below) * z1, 8), hodd[...])
+    l1.put(U, z1, faces[0])
+    l1.put(U, (H1 + bx // 2 + 2) * z1, faces[1])
     prolong_planes(w2, U, 2, count1 // 2, l1, U, U, 0, tmp.at[0])
     l1.sweep(U, KEPT, 2, count1 - 4, 1)
     l1.sweep(KEPT, U, 3, count1 - 6, 1)
@@ -444,26 +523,43 @@
     vmem, hbm = pl.BlockSpec(memory_space=pltpu.VMEM), pl.BlockSpec(memory_space=pl.ANY)
     keep0 = jax.ShapeDtypeStruct((KEPT, (bx + 4) * zw, lanes), f32)
     keep1 = jax.ShapeDtypeStruct((KEPT, p1 * (zw // 2), lanes), f32)
-    u_face = jax.ShapeDtypeStruct((zw, lanes), f32)
     sems = [pltpu.SemaphoreType.DMA((KEPT,)), pltpu.SemaphoreType.DMA((KEPT,))]
 
     def params(scratch, rows):
-        size = 4 * sum(math.prod(t.shape) for t in scratch[:-2]) + 4 * lanes * rows
+        size = 4 * sum(math.prod(t.shape) for t in scratch if t.dtype == f32) + 4 * lanes * rows
         return pltpu.CompilerParams(vmem_limit_bytes=min(255 * 2**18, size + size // 8 + 2**21))
 
     face = jax.ShapeDtypeStruct(((3 * H - 2) * bz, lanes), f32)
-    even, odd, own = pl.pallas_call(
+    even, odd = pl.pallas_call(
         functools.partial(pack_kernel, bx, bz),
-        out_shape=[face, face, jax.ShapeDtypeStruct((3 * bx * bz, lanes), f32)],
+        out_shape=[face, face],
         in_specs=[pl.BlockSpec(memory_space=pltpu.HBM)] * 3,
-        out_specs=[vmem] * 3,
-        scratch_shapes=[pltpu.SemaphoreType.DMA((9,))],
+        out_specs=[hbm] * 2,
+        scratch_shapes=[pltpu.SemaphoreType.DMA((6,))],
         compiler_params=pltpu.CompilerParams(vmem_limit_bytes=62 * 2**20),
         name="pack",
     )(flat(rhs), flat(alpha), flat(beta))
     even = swap(even, "wide", 0)
     odd = swap_odd(odd)
-    other = from_others(own)
+    other_b, other_a, other_r = from_others(flat(beta)), from_others(flat(alpha)), from_others(flat(rhs))
+    devices = n_wide * n_narrow
+    scratch = [
+        pltpu.VMEM((2, bx * zw, lanes), f32),
+        pltpu.VMEM((2, bx // 2 * (zw // 2), lanes), f32),
+        pltpu.VMEM((3, n2, lanes), f32),
+        pltpu.VMEM((2, max(bx * zw // 2, LONGEST // 2), lanes), f32),
+    ]
+    coarse = pl.pallas_call(
+        functools.partial(coarsen_kernel, bx, bz, n_wide, n_narrow),
+        out_shape=jax.ShapeDtypeStruct((devices * 8, lanes), f32),
+        in_specs=[vmem] * 4,
+        out_specs=vmem,
+        scratch_shapes=scratch,
+        compiler_params=params(scratch + [], 2 * bx * zw + devices * 8),
+        name="coarsen",
+    )(flat(alpha), flat(beta), other_a, other_b)
+    coarse = lax.all_to_all(coarse, ("wide", "narrow"), 0, 0, tiled=True)
+    even, odd, coarse = lax.optimization_barrier((even, odd, coarse))
     others = from_others(jnp.concatenate([even, odd]))
     scratch = [
         pltpu.VMEM((9, planes * zw, lanes), f32),
@@ -472,16 +568,15 @@
         pltpu.VMEM((3, p1 * zw, lanes), f32),
         *sems,
     ]
-    packed, ueven, uodd, keep0, keep1 = pl.pallas_call(
+    packed, keep0, keep1 = pl.pallas_call(
         functools.partial(down_kernel, bx, bz, n_wide, n_narrow),
-        out_shape=[jax.ShapeDtypeStruct((n_wide * n2, lanes), f32), u_face, u_face, keep0, keep1],
-        in_specs=[vmem] * 5,
-        out_specs=[vmem, vmem, vmem, hbm, hbm],
+        out_shape=[jax.ShapeDtypeStruct((devices * 16, lanes), f32), keep0, keep1],
+        in_specs=[vmem] * 9,
+        out_specs=[vmem, hbm, hbm],
         scratch_shapes=scratch,
         compiler_params=params(scratch, 3 * planes * zw),
         name="down",
-    )(own, even, odd, other, others)
-    heven, hodd = swap(ueven, "wide", 0), swap_odd(uodd)
+    )(flat(rhs), flat(alpha), flat(beta), even, odd, other_r, other_a, other_b, others)
     gathered = lax.all_to_all(packed, ("wide", "narrow"), 0, 0, tiled=True)
     nx = n_wide * bx
     scratch = []
@@ -493,18 +588,19 @@
         pltpu.VMEM((KEPT + 1, (p1 + 2) * (zw // 2), lanes), f32),
         pltpu.VMEM((KEPT + 1, (bx // 4 + 8) * (zw // 4), lanes), f32),
         pltpu.VMEM((1, (bx // 8 + 4) * (zw // 8), lanes), f32),
+        pltpu.VMEM((2, zw, lanes), f32),
         pltpu.VMEM((2, LONGEST // 2, lanes), f32),
         *sems,
     ]
     out = pl.pallas_call(
         functools.partial(up_kernel, bx, bz, n_wide, n_narrow),
         out_shape=jax.ShapeDtypeStruct((bx * bz, lanes), f32),
-        in_specs=[vmem, vmem, vmem, hbm, hbm],
+        in_specs=[hbm if big(devices) else vmem] * 2 + [hbm, hbm],
         out_specs=vmem,
         scratch_shapes=scratch,
-        compiler_params=params(scratch, bx * bz + n_wide * n2 + 2 * zw),
+        compiler_params=params(scratch, bx * bz + devices * 24),
         name="up",
-    )(gathered, heven, hodd, keep0, keep1)
+    )(gathered, coarse, keep0, keep1)
     return out.reshape(bx, bz, lanes)
 
 

time: 43.7 us -> 61.4 us (1.41)
  blocking collectives: 0 us -> 19.5 us
  Pallas kernels: 13.5 us -> 22.3 us
  waiting for transfers between devices: 13.2 us -> 6.96 us
  starting transfers between devices: 15.7 us -> 10.6 us
  local copies, waits for them, and re-layouts: 1 us -> 1.82 us
    all_to_all x0 -> x1, blocking collectives: none -> 19.5 us  [shards(): gathered = lax.all_to_all(packed, ('wide', 'narrow'), 0, 0, tiled=True)]
    pallas_call x1, Pallas kernels: 2.14 us -> 10.6 us  [shards(): pl.pallas_call(functools.partial(pack_kernel, bx, bz), out_shape=[face, f...]
    all_to_all x1, waiting for transfers between devices: 6.66 us -> 0.01 us  [shards(): coarse = lax.all_to_all(coarse, ('wide', 'narrow'), 0, 0, tiled=True)]
    all_to_all x1, starting transfers between devices: 9.44 us -> 7.03 us  [shards(): coarse = lax.all_to_all(coarse, ('wide', 'narrow'), 0, 0, tiled=True)]
    ppermute x4 -> x5, starting transfers between devices: 4.98 us -> 2.91 us  [swap(): return lax.ppermute(array, axis, [(i, i ^ 1 << bit) for i in range(n)])]
    pallas_call x0 -> x1, Pallas kernels: none -> 1.18 us  [shards(): pl.pallas_call(functools.partial(coarsen_kernel, bx, bz, n_wide, n_narrow...]
    pallas_call x1, Pallas kernels: 5.54 us -> 4.72 us  [shards(): pl.pallas_call(functools.partial(down_kernel, bx, bz, n_wide, n_narrow),...]
    unnamed x2 -> x10, local copies, waits for them, and re-layouts: 1 us -> 1.82 us
  transfers between devices with their start and end apart: 7 -> 7, of which waited for: 4 -> 4; matrix products, arithmetic and copies ran while one was open for 0% -> 0% of each run, Pallas kernels for 0% -> 17%
where the time goes in v4:
time: 61.4 us; the launch traced here: 61.2 us
  Pallas kernels  22.3 us (36%)
  blocking collectives  19.5 us (32%)
  starting transfers between devices  10.6 us (17%)
  waiting for transfers between devices  6.96 us (11%)
  local copies, waits for them, and re-layouts  1.82 us (3%)
    all_to_all x1, blocking collectives, shards(): gathered = lax.all_to_all(packed, ('wide', 'narrow'), 0, 0, tiled=True)  19.5 us
    pallas_call x1, Pallas kernels, shards(): pl.pallas_call(functools.partial(pack_kernel, bx, bz), out_shape=[face, f...  10.6 us
    all_to_all x1, starting transfers between devices, shards(): coarse = lax.all_to_all(coarse, ('wide', 'narrow'), 0, 0, tiled=True)  7.03 us
    ppermute x5, waiting for transfers between devices, swap(): return lax.ppermute(array, axis, [(i, i ^ 1 << bit) for i in range(n)])  6.95 us
    pallas_call x1, Pallas kernels, shards(): pl.pallas_call(functools.partial(up_kernel, bx, bz, n_wide, n_narrow), ou...  5.79 us
    pallas_call x1, Pallas kernels, shards(): pl.pallas_call(functools.partial(down_kernel, bx, bz, n_wide, n_narrow),...  4.72 us
    ppermute x5, starting transfers between devices, swap(): return lax.ppermute(array, axis, [(i, i ^ 1 << bit) for i in range(n)])  2.91 us
    unnamed x10, local copies, waits for them, and re-layouts  1.82 us
  transfers between devices with their start and end apart: 7, of which 4 were waited for; matrix products, arithmetic and copies ran while one was open for 0% of the time, Pallas kernels for 17%

profile of v4, /device:TPU:0, one launch (start us, length us, event | category | flops | bytes accessed | tf_op | source)
XLA Modules:
  0.0 61.2 jit_solution(16084453158181162188)
XLA Ops:
  0.0 0.5 collective-permute-start.2
  0.5 0.1 collective-permute-start.3
  0.5 1.1 %collective-permute-done.2.other_a = f32[256,128]{1,0:T(8,128)S(1)} collective-permute-done((f32[256,128]{1,0:T(8,128)}, f32[256,128]{1,0:T(8,128)S(1)}, u32[]{:S(2)}, u32[]{:S(2)}) %collective-permute-start.2) | collective-permute-done | bytes 131104 | tf_op jit(solution)/shard_map/ppermute | solution.py:498
  1.7 0.4 collective-permute-done.3.other_b
  2.0 0.0 copy-start
  2.0 0.9 %copy-done = f32[16,16,128]{2,1,0:T(8,128)S(1)} copy-done((f32[16,16,128]{2,1,0:T(8,128)S(1)}, f32[16,16,128]{2,1,0:T(8,128)}, u32[]{:S(2)}) %copy-start) | copy-done | bytes 131096
  2.9 0.0 copy-start.2
  2.9 0.9 %copy-done.2 = f32[16,16,128]{2,1,0:T(8,128)S(1)} copy-done((f32[16,16,128]{2,1,0:T(8,128)S(1)}, f32[16,16,128]{2,1,0:T(8,128)}, u32[]{:S(2)}) %copy-start.2) | copy-done | bytes 131096
  3.8 0.0 copy-start.1
  3.8 0.0 copy-start.3
  3.8 0.0 copy-start.4
  3.8 1.2 %coarsen.1 = f32[256,128]{1,0:T(8,128)} custom-call(f32[256,128]{1,0:T(8,128)S(1)} %bitcast.10, f32[256,128]{1,0:T(8,128)S(1)} %bitcast.14, f32[256,128]{1,0:T(8,128)S(1)} %collective-permute-done.2.other_a, f32[256,128]{1,0:T(8,128)S(1)} %collective-permute-done.3.other_b), custom_call_target="tpu_custom_call" | custom-call | tf_op jit(solution)/shard_map/coarsen/pallas_call | solution.py:552
  5.0 7.0 %all-to-all-start = ((f32[32,8,128]{2,1,0:T(8,128)}), f32[32,8,128]{2,1,0:T(8,128)S(1)}, u32[]{:S(2)}, u32[]{:S(2)}) async-start(f32[32,8,128]{2,1,0:T(8,128)} %bitcast.3), calls=%async_computation | async-start | bytes 262144 | tf_op jit(solution)/shard_map/all_to_all | solution.py:561
  12.0 10.6 %pack.1 = (f32[304,128]{1,0:T(8,128)}, f32[304,128]{1,0:T(8,128)}) custom-call(f32[256,128]{1,0:T(8,128)} %bitcast.18, f32[256,128]{1,0:T(8,128)} %bitcast.9, f32[256,128]{1,0:T(8,128)} %bitcast.13), custom_call_target="tpu_custom_call" | custom-call | tf_op jit(solution)/shard_map/pack/pallas_call | solution.py:533
  22.7 1.8 %collective-permute-start = (f32[304,128]{1,0:T(8,128)}, f32[304,128]{1,0:T(8,128)S(1)}, u32[]{:S(2)}, u32[]{:S(2)}) collective-permute-start(f32[304,128]{1,0:T(8,128)} %get-tuple-element.13), channel_id=1, source_target_pairs={{0,2},{2,0},{4,6},{6,4},{8,10},{10,8},{12,14},{14,12},{16,18},{18,... | collective-permute-start | bytes 466952 | tf_op jit(solution)/shard_map/ppermute | solution.py:498
  24.5 0.7 %collective-permute-start.1 = (f32[304,128]{1,0:T(8,128)}, f32[304,128]{1,0:T(8,128)S(1)}, u32[]{:S(2)}, u32[]{:S(2)}) collective-permute-start(f32[304,128]{1,0:T(8,128)} %get-tuple-element.14), channel_id=1, source_target_pairs={{2,4},{6,8},{10,12},{14,16},{18,20},{22,24},{26,28},{4,2},{8,6},{1... | collective-permute-start | bytes 466952 | tf_op jit(solution)/shard_map/ppermute | solution.py:504
  25.2 4.0 %collective-permute-done.even = f32[304,128]{1,0:T(8,128)S(1)} collective-permute-done((f32[304,128]{1,0:T(8,128)}, f32[304,128]{1,0:T(8,128)S(1)}, u32[]{:S(2)}, u32[]{:S(2)}) %collective-permute-start) | collective-permute-done | bytes 155680 | tf_op jit(solution)/shard_map/ppermute | solution.py:498
  29.1 0.0 collective-permute-done.1.odd
  29.1 0.0 all-to-all-done
  29.1 0.1 collective-permute-start.5
  29.2 0.5 collective-permute-start.4
  29.7 1.5 %collective-permute-done.4.other_r = f32[256,128]{1,0:T(8,128)S(1)} collective-permute-done((f32[256,128]{1,0:T(8,128)}, f32[256,128]{1,0:T(8,128)S(1)}, u32[]{:S(2)}, u32[]{:S(2)}) %collective-permute-start.4) | collective-permute-done | bytes 131104 | tf_op jit(solution)/shard_map/ppermute | solution.py:498
  31.2 0.0 collective-permute-done.5.others
  31.2 0.0 copy-done.1
  31.2 0.0 copy-done.3
  31.2 0.0 copy-done.4
  31.2 4.7 %down.1 = (f32[512,128]{1,0:T(8,128)S(1)}, f32[6,640,128]{2,1,0:T(8,128)S(1)}, f32[6,224,128]{2,1,0:T(8,128)S(1)}) custom-call(f32[256,128]{1,0:T(8,128)S(1)} %bitcast.20, f32[256,128]{1,0:T(8,128)S(1)} %bitcast.11, f32[256,128]{1,0:T(8,128)S(1)} %bitcast.15, f32[304,128]{1,0:T(8,128)S(1)} %collective-permute-done.even, ...), custom_call_target="tpu_custom_call" | custom-call | tf_op jit(solution)/shard_map/down/pallas_call | solution.py:571
  36.0 19.5 %all_to_all.23 = f32[32,16,128]{2,1,0:T(8,128)S(1)} all-to-all(f32[32,16,128]{2,1,0:T(8,128)S(1)} %bitcast.21), channel_id=1, replica_groups=mesh['wide'=16,'narrow'=2] {'wide','narrow'}, dimensions={0} | all-to-all | bytes 524288 | tf_op jit(solution)/shard_map/all_to_all | solution.py:580
  55.4 5.8 %up.1 = f32[256,128]{1,0:T(8,128)} custom-call(f32[512,128]{1,0:T(8,128)S(1)} %bitcast.16, f32[256,128]{1,0:T(8,128)S(1)} %bitcast.17, f32[6,640,128]{2,1,0:T(8,128)S(1)} %get-tuple-element.19.keep0, f32[6,224,128]{2,1,0:T(8,128)S(1)} %get-tuple-element.20.keep1), custom_call_target="tpu_custom_call" | custom-call | tf_op jit(solution)/shard_map/up/pallas_call | solution.py:595
  (1 shorter events, 0.0 us)
Async XLA Ops:
  0.0 1.6 %collective-permute-start.2 = (f32[256,128]{1,0:T(8,128)}, f32[256,128]{1,0:T(8,128)S(1)}, u32[]{:S(2)}, u32[]{:S(2)}) collective-permute-start(f32[256,128]{1,0:T(8,128)} %bitcast.8), channel_id=1, source_target_pairs={{0,1},{1,0},{2,3},{3,2},{4,5},{5,4},{6,7},{7,6},{8,9},{9,8},{10,11... | collective-permute-start | bytes 393224 | tf_op jit(solution)/shard_map/ppermute | solution.py:498
  0.5 1.6 %collective-permute-start.3 = (f32[256,128]{1,0:T(8,128)}, f32[256,128]{1,0:T(8,128)S(1)}, u32[]{:S(2)}, u32[]{:S(2)}) collective-permute-start(f32[256,128]{1,0:T(8,128)} %bitcast.12), channel_id=1, source_target_pairs={{0,1},{1,0},{2,3},{3,2},{4,5},{5,4},{6,7},{7,6},{8,9},{9,8},{10,11... | collective-permute-start | bytes 393224 | tf_op jit(solution)/shard_map/ppermute | solution.py:498
  2.0 0.9 %copy-start = (f32[16,16,128]{2,1,0:T(8,128)S(1)}, f32[16,16,128]{2,1,0:T(8,128)}, u32[]{:S(2)}) copy-start(f32[16,16,128]{2,1,0:T(8,128)} %param.4) | copy-start | bytes 393220
  2.9 0.9 %copy-start.2 = (f32[16,16,128]{2,1,0:T(8,128)S(1)}, f32[16,16,128]{2,1,0:T(8,128)}, u32[]{:S(2)}) copy-start(f32[16,16,128]{2,1,0:T(8,128)} %param.5) | copy-start | bytes 393220
  3.8 27.4 %copy-start.1 = (f32[16,16,128]{2,1,0:T(8,128)S(1)}, f32[16,16,128]{2,1,0:T(8,128)}, u32[]{:S(2)}) copy-start(f32[16,16,128]{2,1,0:T(8,128)} %param.4) | copy-start | bytes 393220
  3.8 27.4 %copy-start.3 = (f32[16,16,128]{2,1,0:T(8,128)S(1)}, f32[16,16,128]{2,1,0:T(8,128)}, u32[]{:S(2)}) copy-start(f32[16,16,128]{2,1,0:T(8,128)} %param.5) | copy-start | bytes 393220
  3.8 27.4 %copy-start.4 = (f32[16,16,128]{2,1,0:T(8,128)S(1)}, f32[16,16,128]{2,1,0:T(8,128)}, u32[]{:S(2)}) copy-start(f32[16,16,128]{2,1,0:T(8,128)} %param.3) | copy-start | bytes 393220
  5.0 24.1 %all-to-all-start = ((f32[32,8,128]{2,1,0:T(8,128)}), f32[32,8,128]{2,1,0:T(8,128)S(1)}, u32[]{:S(2)}, u32[]{:S(2)}) async-start(f32[32,8,128]{2,1,0:T(8,128)} %bitcast.3), calls=%async_computation | async-start | bytes 262144 | tf_op jit(solution)/shard_map/all_to_all | solution.py:561
  22.7 6.5 %collective-permute-start = (f32[304,128]{1,0:T(8,128)}, f32[304,128]{1,0:T(8,128)S(1)}, u32[]{:S(2)}, u32[]{:S(2)}) collective-permute-start(f32[304,128]{1,0:T(8,128)} %get-tuple-element.13), channel_id=1, source_target_pairs={{0,2},{2,0},{4,6},{6,4},{8,10},{10,8},{12,14},{14,12},{16,18},{18,... | collective-permute-start | bytes 466952 | tf_op jit(solution)/shard_map/ppermute | solution.py:498
  24.5 4.6 %collective-permute-start.1 = (f32[304,128]{1,0:T(8,128)}, f32[304,128]{1,0:T(8,128)S(1)}, u32[]{:S(2)}, u32[]{:S(2)}) collective-permute-start(f32[304,128]{1,0:T(8,128)} %get-tuple-element.14), channel_id=1, source_target_pairs={{2,4},{6,8},{10,12},{14,16},{18,20},{22,24},{26,28},{4,2},{8,6},{1... | collective-permute-start | bytes 466952 | tf_op jit(solution)/shard_map/ppermute | solution.py:504
  29.1 2.1 %collective-permute-start.5 = (f32[608,128]{1,0:T(8,128)S(1)}, f32[608,128]{1,0:T(8,128)S(1)}, u32[]{:S(2)}, u32[]{:S(2)}) collective-permute-start(f32[608,128]{1,0:T(8,128)S(1)} %pad_maximum_fusion), channel_id=1, source_target_pairs={{0,1},{1,0},{2,3},{3,2},{4,5},{5,4},{6,7},{7,6},{8,9},{9,8},{10,11... | collective-permute-start | bytes 933896 | tf_op jit(solution)/shard_map/ppermute | solution.py:498
  29.2 2.0 %collective-permute-start.4 = (f32[256,128]{1,0:T(8,128)}, f32[256,128]{1,0:T(8,128)S(1)}, u32[]{:S(2)}, u32[]{:S(2)}) collective-permute-start(f32[256,128]{1,0:T(8,128)} %bitcast.19), channel_id=1, source_target_pairs={{0,1},{1,0},{2,3},{3,2},{4,5},{5,4},{6,7},{7,6},{8,9},{9,8},{10,11... | collective-permute-start | bytes 393224 | tf_op jit(solution)/shard_map/ppermute | solution.py:498

commit v5 on v3

--- a/solution.py
+++ b/solution.py
@@ -198,29 +198,36 @@
     return copy
 
 
-def pack_kernel(bx, bz, rhs, alpha, beta, even, odd, own, sem):
+def pack_kernel(bx, bz, rhs, alpha, beta, even, odd, sem):
     up = 1 - lax.axis_index("wide") % 2
     waits = []
-    at = [0, 0]
+    at = 0
     for q, (src, size) in enumerate(((rhs, H - 1), (alpha, H - 1), (beta, H))):
         for k, dst in enumerate((even, odd)):
             upper = up if k == 0 else 1 - up
             start = pl.multiple_of(upper * ((bx - size) * bz), 8)
             copy = pltpu.make_async_copy(
-                src.at[pl.ds(start, size * bz)], dst.at[pl.ds(at[k] * bz, size * bz)], sem.at[2 * q + k]
+                src.at[pl.ds(start, size * bz)], dst.at[pl.ds(at * bz, size * bz)], sem.at[2 * q + k]
             )
             copy.start()
             waits.append(copy)
-            at[k] += size
-        copy = pltpu.make_async_copy(src, own.at[pl.ds(q * bx * bz, bx * bz)], sem.at[6 + q])
-        copy.start()
-        waits.append(copy)
+        at += size
     for copy in waits:
         copy.wait()
 
 
+def z_of(narrow, k, n_narrow):
+    return 1 - narrow if n_narrow == 2 else lax.rem(narrow + 1 + k, n_narrow)
+
+
+def spread4(p, lane, k):
+    t = jnp.where(lane == k, p, 0.0)
+    t = t + pltpu.roll(t, 1 if k % 2 == 0 else LANES - 1, 1)
+    return t + pltpu.roll(t, 2 if k < 2 else LANES - 2, 1)
+
+
 def down_kernel(
-    bx, bz, n_wide, n_narrow, own, even, odd, other, others, packed, ueven, uodd, keep0, keep1, lev0, lev1, part, tmp, sem0, sem1
+    bx, bz, n_wide, n_narrow, own, even, odd, other, others, packed, keep0, keep1, lev0, lev1, part, tmp, sem0, sem1
 ):
     zw = bz * n_narrow
     planes = bx + 2 * H
@@ -247,7 +254,7 @@
         place(q, even, at, size, p_even, narrow * bz)
         place(q, odd, at, size, p_odd, narrow * bz)
         for k in range(n_narrow - 1):
-            z = (1 - narrow if n_narrow == 2 else lax.rem(narrow + 1 + k, n_narrow)) * bz
+            z = z_of(narrow, k, n_narrow) * bz
             place(q, other, (3 * k + index) * bx, bx, H, z)
             place(q, others, 2 * k * all_h + at, size, p_even, z)
             place(q, others, (2 * k + 1) * all_h + at, size, p_odd, z)
@@ -284,30 +291,49 @@
     l1.sweep(U, V, 2, p1 - 4, 1)
     waits += [keep(l1, q, 0, p1, keep1, q, sem1) for q in (F, W, CX, CZ, CY)]
     waits.append(keep(l1, V, 0, p1, keep1, U, sem1))
-    n1 = 2 * l1.zw
-    upper, lower = H1 + bx // 2 - 3, H1 + 1
-    ueven[...] = l1.get(V, pl.multiple_of((up * upper + (1 - up) * lower) * l1.zw, 8), n1)
-    uodd[...] = l1.get(V, pl.multiple_of(((1 - up) * upper + up * lower) * l1.zw, 8), n1)
     restrict_planes(lambda r, n: l1.residual(V, r, n), l1, H1, k2, l2, 0, 0, tmp.at[2], 1)
-    which = lax.broadcasted_iota(jnp.int32, (n2, LANES), 1) % 4
-    part[0] = jnp.where(which == 0, part[0], jnp.where(which == 1, part[1], part[2]))
-    share = n2 // n_narrow
-    mine = part[0, pl.ds(pl.multiple_of(narrow * share, 8), share), :]
+    which = lax.broadcasted_iota(jnp.int32, (z2, LANES), 1) % 4
+    fs, as_, bs = [[part[q, pl.ds(k * z2, z2), :] for k in range(4)] for q in range(3)]
+
+    def four(p):
+        return jnp.where(which == 0, p[0], jnp.where(which == 1, p[1], jnp.where(which == 2, p[2], p[3])))
+
+    parts = [four(fs), four((as_[0], bs[0], as_[1], bs[1])), four((as_[2], bs[2], as_[3], bs[3]))]
+    z1 = l1.zw
+    first = lax.broadcasted_iota(jnp.int32, (z1, LANES), 1) % 2 == 0
+
+    def face(plane):
+        r = (H1 + plane) * z1
+        return jnp.where(first, l1.get(V, r, z1), l1.get(V, r + z1, z1))
+
+    upper, lower = face(bx // 2 - 3), face(1)
+    slot = 3 * z2 + z1
 
     def spread(i):
-        packed[pl.ds(i * share, share), :] = mine
-
-    each(n_wide * n_narrow, share, spread)
+        for k in range(3):
+            packed[pl.ds(i * slot + k * z2, z2), :] = parts[k]
+        packed[pl.ds(i * slot + 3 * z2, z1), :] = upper
+
+    each(n_wide, slot, spread)
+
+    @pl.when(wide > 0)
+    def _():
+        packed[pl.ds(pl.multiple_of((wide - 1) * slot + 3 * z2, 8), z1), :] = lower
+
     for copy in waits:
         copy.wait()
 
 
+def big(n_wide):
+    return n_wide > 32
+
+
 def margin(zl, index):
     return max(8, (4 if index == 2 else 2) * zl)
 
 
 def up_kernel(
-    bx, bz, n_wide, n_narrow, gathered, heven, hodd, keep0, keep1, out, lev2, lev3, lev4, lev5, lev0, lev1, near2, near3, tmp, sem0, sem1
+    bx, bz, n_wide, n_narrow, gathered, keep0, keep1, out, lev2, lev3, lev4, lev5, lev0, lev1, near2, near3, faces, slots, tmp, sem0, sem1
 ):
     wide = lax.axis_index("wide")
     narrow = lax.axis_index("narrow")
@@ -332,19 +358,39 @@
             level.put(q, m + level.nx * zl, zero)
     l2, l3, l4, l5 = levels
     planes2 = bx // 4
-    n2 = planes2 * l2.zw
-    n = n2 // n_narrow
-    lane = lax.broadcasted_iota(jnp.int32, (n, LANES), 1) % 4
-
-    def unpack(i):
-        p = gathered[pl.ds(i * n, n), :]
-        for q, k, first, second in ((F, 0, 1, 2), (A, 1, LANES - 1, 2), (B, 2, 1, LANES - 2)):
-            t = jnp.where(lane == k, p, 0.0)
-            t = t + pltpu.roll(t, first, 1)
-            t = t + pltpu.roll(t, second, 1)
-            l2.put(q, l2.base + i * n, t)
-
-    each(n_wide * n_narrow, n, unpack)
+    z2 = l2.zw
+    slot = 3 * z2 + z1
+    lane = lax.broadcasted_iota(jnp.int32, (z2, LANES), 1) % 4
+
+    def slot_of(w):
+        if not big(n_wide):
+            return gathered, w * slot
+        pltpu.sync_copy(gathered.at[pl.ds(pl.multiple_of(w * slot, 8), slot)], slots)
+        return slots, 0
+
+    def unpack(w):
+        src, at = slot_of(w)
+        r = l2.base + w * planes2 * z2
+        for part, wanted in (
+            (0, ((F, 0), (F, 1), (F, 2), (F, 3))),
+            (1, ((A, 0), (B, 0), (A, 1), (B, 1))),
+            (2, ((A, 2), (B, 2), (A, 3), (B, 3))),
+        ):
+            p = src[pl.ds(at + part * z2, z2), :]
+            for k, (q, plane) in enumerate(wanted):
+                l2.put(q, r + plane * z2, spread4(p, lane, k))
+
+    each(n_wide, 12 * z2, unpack)
+    first = lax.broadcasted_iota(jnp.int32, (z1, LANES), 1) % 2 == 0
+    for k, by in ((0, -1), (1, 1)):
+        there = wide + by
+        valid = jnp.logical_and(there >= 0, there < n_wide)
+        src, at = slot_of(jnp.clip(there, 0, n_wide - 1))
+        p = jnp.where(valid, src[pl.ds(pl.multiple_of(at + 3 * z2, 8), z1), :], 0.0)
+        t = jnp.where(first, p, 0.0)
+        faces[k, pl.ds(0, z1), :] = t + pltpu.roll(t, 1, 1)
+        t = p - t
+        faces[k, pl.ds(z1, z1), :] = t + pltpu.roll(t, LANES - 1, 1)
 
     def chunk_of(level):
         return max(1, min(32 // level.zw, level.nx))
@@ -395,10 +441,8 @@
         copy.wait()
     l1 = Level(lev1, z1, 1)
     count1 = bx // 2 + 2 * H1 + 2
-    up = 1 - wide % 2
-    above, below = H1 + bx // 2 + 2, 1
-    l1.put(U, pl.multiple_of((up * above + (1 - up) * below) * z1, 8), heven[...])
-    l1.put(U, pl.multiple_of(((1 - up) * above + up * below) * z1, 8), hodd[...])
+    l1.put(U, z1, faces[0])
+    l1.put(U, (H1 + bx // 2 + 2) * z1, faces[1])
     prolong_planes(w2, U, 2, count1 // 2, l1, U, U, 0, tmp.at[0])
     l1.sweep(U, KEPT, 2, count1 - 4, 1)
     l1.sweep(KEPT, U, 3, count1 - 6, 1)
@@ -444,27 +488,29 @@
     vmem, hbm = pl.BlockSpec(memory_space=pltpu.VMEM), pl.BlockSpec(memory_space=pl.ANY)
     keep0 = jax.ShapeDtypeStruct((KEPT, (bx + 4) * zw, lanes), f32)
     keep1 = jax.ShapeDtypeStruct((KEPT, p1 * (zw // 2), lanes), f32)
-    u_face = jax.ShapeDtypeStruct((zw, lanes), f32)
     sems = [pltpu.SemaphoreType.DMA((KEPT,)), pltpu.SemaphoreType.DMA((KEPT,))]
 
     def params(scratch, rows):
-        size = 4 * sum(math.prod(t.shape) for t in scratch[:-2]) + 4 * lanes * rows
+        size = 4 * sum(math.prod(t.shape) for t in scratch if t.dtype == f32) + 4 * lanes * rows
         return pltpu.CompilerParams(vmem_limit_bytes=min(255 * 2**18, size + size // 8 + 2**21))
 
     face = jax.ShapeDtypeStruct(((3 * H - 2) * bz, lanes), f32)
-    even, odd, own = pl.pallas_call(
+    even, odd = pl.pallas_call(
         functools.partial(pack_kernel, bx, bz),
-        out_shape=[face, face, jax.ShapeDtypeStruct((3 * bx * bz, lanes), f32)],
+        out_shape=[face, face],
         in_specs=[pl.BlockSpec(memory_space=pltpu.HBM)] * 3,
-        out_specs=[vmem] * 3,
-        scratch_shapes=[pltpu.SemaphoreType.DMA((9,))],
+        out_specs=[hbm] * 2,
+        scratch_shapes=[pltpu.SemaphoreType.DMA((6,))],
         compiler_params=pltpu.CompilerParams(vmem_limit_bytes=62 * 2**20),
         name="pack",
     )(flat(rhs), flat(alpha), flat(beta))
+    even, odd, rhs, alpha, beta = lax.optimization_barrier((even, odd, rhs, alpha, beta))
+    own = jnp.concatenate([flat(rhs), flat(alpha), flat(beta)])
     even = swap(even, "wide", 0)
     odd = swap_odd(odd)
     other = from_others(own)
     others = from_others(jnp.concatenate([even, odd]))
+    slot = 3 * (zw // 4) + zw // 2
     scratch = [
         pltpu.VMEM((9, planes * zw, lanes), f32),
         pltpu.VMEM((9, p1 * (zw // 2), lanes), f32),
@@ -472,17 +518,16 @@
         pltpu.VMEM((3, p1 * zw, lanes), f32),
         *sems,
     ]
-    packed, ueven, uodd, keep0, keep1 = pl.pallas_call(
+    packed, keep0, keep1 = pl.pallas_call(
         functools.partial(down_kernel, bx, bz, n_wide, n_narrow),
-        out_shape=[jax.ShapeDtypeStruct((n_wide * n2, lanes), f32), u_face, u_face, keep0, keep1],
+        out_shape=[jax.ShapeDtypeStruct((n_wide * slot, lanes), f32), keep0, keep1],
         in_specs=[vmem] * 5,
-        out_specs=[vmem, vmem, vmem, hbm, hbm],
+        out_specs=[vmem, hbm, hbm],
         scratch_shapes=scratch,
         compiler_params=params(scratch, 3 * planes * zw),
         name="down",
     )(own, even, odd, other, others)
-    heven, hodd = swap(ueven, "wide", 0), swap_odd(uodd)
-    gathered = lax.all_to_all(packed, ("wide", "narrow"), 0, 0, tiled=True)
+    gathered = lax.all_to_all(packed, "wide", 0, 0, tiled=True)
     nx = n_wide * bx
     scratch = []
     for index in range(2, LEVELS):
@@ -493,18 +538,20 @@
         pltpu.VMEM((KEPT + 1, (p1 + 2) * (zw // 2), lanes), f32),
         pltpu.VMEM((KEPT + 1, (bx // 4 + 8) * (zw // 4), lanes), f32),
         pltpu.VMEM((1, (bx // 8 + 4) * (zw // 8), lanes), f32),
+        pltpu.VMEM((2, zw, lanes), f32),
+        pltpu.VMEM((slot, lanes), f32),
         pltpu.VMEM((2, LONGEST // 2, lanes), f32),
         *sems,
     ]
     out = pl.pallas_call(
         functools.partial(up_kernel, bx, bz, n_wide, n_narrow),
         out_shape=jax.ShapeDtypeStruct((bx * bz, lanes), f32),
-        in_specs=[vmem, vmem, vmem, hbm, hbm],
+        in_specs=[hbm if big(n_wide) else vmem, hbm, hbm],
         out_specs=vmem,
         scratch_shapes=scratch,
-        compiler_params=params(scratch, bx * bz + n_wide * n2 + 2 * zw),
+        compiler_params=params(scratch, bx * bz + (0 if big(n_wide) else n_wide * slot)),
         name="up",
-    )(gathered, heven, hodd, keep0, keep1)
+    )(gathered, keep0, keep1)
     return out.reshape(bx, bz, lanes)
 
 

time: 43.7 us -> 52.2 us (1.19)
  blocking collectives: 0 us -> 21.9 us
  starting transfers between devices: 15.7 us -> 3.8 us
  waiting for transfers between devices: 13.2 us -> 4.01 us
  Pallas kernels: 13.5 us -> 21.2 us
  other arithmetic: 0.02 us -> 1.08 us
  local copies, waits for them, and re-layouts: 1 us -> 0 us
    all_to_all x0 -> x1, blocking collectives: none -> 21.9 us  [shards(): gathered = lax.all_to_all(packed, 'wide', 0, 0, tiled=True)]
    all_to_all x1 -> x0, starting transfers between devices: 9.44 us -> none  [shards(): gathered = lax.all_to_all(packed, ('wide', 'narrow'), 0, 0, tiled=True)]
    pallas_call x1, Pallas kernels: 2.14 us -> 10.6 us  [shards(): pl.pallas_call(functools.partial(pack_kernel, bx, bz), out_shape=[face, f...]
    all_to_all x1 -> x0, waiting for transfers between devices: 6.66 us -> none  [shards(): gathered = lax.all_to_all(packed, ('wide', 'narrow'), 0, 0, tiled=True)]
    ppermute x4 -> x3, waiting for transfers between devices: 6.52 us -> 4.01 us  [swap(): return lax.ppermute(array, axis, [(i, i ^ 1 << bit) for i in range(n)])]
    ppermute x4 -> x3, starting transfers between devices: 4.98 us -> 3.15 us  [swap(): return lax.ppermute(array, axis, [(i, i ^ 1 << bit) for i in range(n)])]
    concatenate x0 -> x1, other arithmetic: none -> 1.06 us  [shards(): own = jnp.concatenate([flat(rhs), flat(alpha), flat(beta)])]
    unnamed x2 -> x0, local copies, waits for them, and re-layouts: 1 us -> none
  transfers between devices with their start and end apart: 7 -> 4, of which waited for: 4 -> 2; matrix products, arithmetic and copies ran while one was open for 0% -> 2% of each run, Pallas kernels for 0% -> 0%
where the time goes in v5:
time: 52.2 us; the launch traced here: 52 us
  blocking collectives  21.9 us (42%)
  Pallas kernels  21.2 us (41%)
  waiting for transfers between devices  4.01 us (8%)
  starting transfers between devices  3.8 us (7%)
  other arithmetic  1.08 us (2%)
    all_to_all x1, blocking collectives, shards(): gathered = lax.all_to_all(packed, 'wide', 0, 0, tiled=True)  21.9 us
    pallas_call x1, Pallas kernels, shards(): pl.pallas_call(functools.partial(pack_kernel, bx, bz), out_shape=[face, f...  10.6 us
    pallas_call x1, Pallas kernels, shards(): pl.pallas_call(functools.partial(up_kernel, bx, bz, n_wide, n_narrow), ou...  5.79 us
    pallas_call x1, Pallas kernels, shards(): pl.pallas_call(functools.partial(down_kernel, bx, bz, n_wide, n_narrow),...  4.82 us
    ppermute x3, waiting for transfers between devices, swap(): return lax.ppermute(array, axis, [(i, i ^ 1 << bit) for i in range(n)])  4.01 us
    ppermute x3, starting transfers between devices, swap(): return lax.ppermute(array, axis, [(i, i ^ 1 << bit) for i in range(n)])  3.15 us
    concatenate x1, other arithmetic, shards(): own = jnp.concatenate([flat(rhs), flat(alpha), flat(beta)])  1.06 us
  transfers between devices with their start and end apart: 4, of which 2 were waited for; matrix products, arithmetic and copies ran while one was open for 2% of the time, Pallas kernels for 0%

profile of v5, /device:TPU:0, one launch (start us, length us, event | category | flops | bytes accessed | tf_op | source)
XLA Modules:
  0.0 52.0 jit_solution(1028015990615284486)
XLA Ops:
  0.0 10.6 %pack.1 = (f32[304,128]{1,0:T(8,128)}, f32[304,128]{1,0:T(8,128)}) custom-call(f32[256,128]{1,0:T(8,128)} %bitcast.15, f32[256,128]{1,0:T(8,128)} %bitcast.13, f32[256,128]{1,0:T(8,128)} %bitcast.11), custom_call_target="tpu_custom_call" | custom-call | tf_op jit(solution)/shard_map/pack/pallas_call | solution.py:498
  10.6 3.0 %collective-permute-start = (f32[304,128]{1,0:T(8,128)}, f32[304,128]{1,0:T(8,128)S(1)}, u32[]{:S(2)}, u32[]{:S(2)}) collective-permute-start(f32[304,128]{1,0:T(8,128)} %get-tuple-element.20), channel_id=1, source_target_pairs={{0,2},{2,0},{4,6},{6,4},{8,10},{10,8},{12,14},{14,12},{16,18},{18,... | collective-permute-start | bytes 466952 | tf_op jit(solution)/shard_map/ppermute | solution.py:463
  13.6 0.7 %collective-permute-start.1 = (f32[304,128]{1,0:T(8,128)}, f32[304,128]{1,0:T(8,128)S(1)}, u32[]{:S(2)}, u32[]{:S(2)}) collective-permute-start(f32[304,128]{1,0:T(8,128)} %get-tuple-element.21), channel_id=1, source_target_pairs={{2,4},{6,8},{10,12},{14,16},{18,20},{22,24},{26,28},{4,2},{8,6},{1... | collective-permute-start | bytes 466952 | tf_op jit(solution)/shard_map/ppermute | solution.py:469
  14.3 1.1 %pad_maximum_fusion.own = f32[768,128]{1,0:T(8,128)S(1)} fusion(f32[256,128]{1,0:T(8,128)} %bitcast.12, f32[256,128]{1,0:T(8,128)} %bitcast.14, f32[256,128]{1,0:T(8,128)} %bitcast.16), kind=kLoop, calls=%fused_computation | loop fusion | flops 196608 | bytes 786432 | tf_op jit(solution)/shard_map/concatenate | solution.py:508
  15.3 0.1 collective-permute-start.2
  15.4 2.4 %collective-permute-done.even = f32[304,128]{1,0:T(8,128)S(1)} collective-permute-done((f32[304,128]{1,0:T(8,128)}, f32[304,128]{1,0:T(8,128)S(1)}, u32[]{:S(2)}, u32[]{:S(2)}) %collective-permute-start) | collective-permute-done | bytes 155680 | tf_op jit(solution)/shard_map/ppermute | solution.py:463
  17.8 0.0 collective-permute-done.1.odd
  17.9 0.1 collective-permute-start.3
  17.9 0.0 collective-permute-done.2.other
  17.9 1.6 %collective-permute-done.3.others = f32[608,128]{1,0:T(8,128)S(1)} collective-permute-done((f32[608,128]{1,0:T(8,128)S(1)}, f32[608,128]{1,0:T(8,128)S(1)}, u32[]{:S(2)}, u32[]{:S(2)}) %collective-permute-start.3) | collective-permute-done | bytes 311328 | tf_op jit(solution)/shard_map/ppermute | solution.py:463
  19.5 4.8 %down.1 = (f32[640,128]{1,0:T(8,128)S(1)}, f32[6,640,128]{2,1,0:T(8,128)S(1)}, f32[6,224,128]{2,1,0:T(8,128)S(1)}) custom-call(f32[768,128]{1,0:T(8,128)S(1)} %pad_maximum_fusion.own, f32[304,128]{1,0:T(8,128)S(1)} %collective-permute-done.even, f32[304,128]{1,0:T(8,128)S(1)} %collective-permute-done.1.odd, f32[768,128]{1,0:T(8,128)S(1)} %collective-permute-done.2.other, ...), custom_call_target="tpu_custom_call" | custom-call | tf_op jit(solution)/shard_map/down/pallas_call | solution.py:521
  24.4 21.9 %all_to_all.11 = f32[16,40,128]{2,1,0:T(8,128)S(1)} all-to-all(f32[16,40,128]{2,1,0:T(8,128)S(1)} %bitcast.10), channel_id=1, replica_groups=mesh['wide'=16,'narrow'=2] {'wide'}, dimensions={0} | all-to-all | bytes 655360 | tf_op jit(solution)/shard_map/all_to_all | solution.py:530
  46.2 5.8 %up.1 = f32[256,128]{1,0:T(8,128)} custom-call(f32[640,128]{1,0:T(8,128)S(1)} %bitcast.9, f32[6,640,128]{2,1,0:T(8,128)S(1)} %get-tuple-element.23.keep0, f32[6,224,128]{2,1,0:T(8,128)S(1)} %get-tuple-element.24.keep1), custom_call_target="tpu_custom_call" | custom-call | tf_op jit(solution)/shard_map/up/pallas_call | solution.py:546
  (1 shorter events, 0.0 us)
Async XLA Ops:
  10.6 7.2 %collective-permute-start = (f32[304,128]{1,0:T(8,128)}, f32[304,128]{1,0:T(8,128)S(1)}, u32[]{:S(2)}, u32[]{:S(2)}) collective-permute-start(f32[304,128]{1,0:T(8,128)} %get-tuple-element.20), channel_id=1, source_target_pairs={{0,2},{2,0},{4,6},{6,4},{8,10},{10,8},{12,14},{14,12},{16,18},{18,... | collective-permute-start | bytes 466952 | tf_op jit(solution)/shard_map/ppermute | solution.py:463
  13.6 4.2 %collective-permute-start.1 = (f32[304,128]{1,0:T(8,128)}, f32[304,128]{1,0:T(8,128)S(1)}, u32[]{:S(2)}, u32[]{:S(2)}) collective-permute-start(f32[304,128]{1,0:T(8,128)} %get-tuple-element.21), channel_id=1, source_target_pairs={{2,4},{6,8},{10,12},{14,16},{18,20},{22,24},{26,28},{4,2},{8,6},{1... | collective-permute-start | bytes 466952 | tf_op jit(solution)/shard_map/ppermute | solution.py:469
  15.3 2.6 %collective-permute-start.2 = (f32[768,128]{1,0:T(8,128)S(1)}, f32[768,128]{1,0:T(8,128)S(1)}, u32[]{:S(2)}, u32[]{:S(2)}) collective-permute-start(f32[768,128]{1,0:T(8,128)S(1)} %pad_maximum_fusion.own), channel_id=1, source_target_pairs={{0,1},{1,0},{2,3},{3,2},{4,5},{5,4},{6,7},{7,6},{8,9},{9,8},{10,11... | collective-permute-start | bytes 1179656 | tf_op jit(solution)/shard_map/ppermute | solution.py:463
  17.9 1.7 %collective-permute-start.3 = (f32[608,128]{1,0:T(8,128)S(1)}, f32[608,128]{1,0:T(8,128)S(1)}, u32[]{:S(2)}, u32[]{:S(2)}) collective-permute-start(f32[608,128]{1,0:T(8,128)S(1)} %pad_maximum_fusion.1), channel_id=1, source_target_pairs={{0,1},{1,0},{2,3},{3,2},{4,5},{5,4},{6,7},{7,6},{8,9},{9,8},{10,11... | collective-permute-start | bytes 933896 | tf_op jit(solution)/shard_map/ppermute | solution.py:463

commit v6 on v5

--- a/solution.py
+++ b/solution.py
@@ -226,6 +226,31 @@
     return t + pltpu.roll(t, 2 if k < 2 else LANES - 2, 1)
 
 
+def coarsen_kernel(bx, bz, devices, alpha, beta, packed, fine, mid, part, tmp, sem):
+    z2 = bz // 4
+    waits = [pltpu.make_async_copy(src, fine.at[q], sem.at[q]) for q, src in enumerate((alpha, beta))]
+    for copy in waits:
+        copy.start()
+    for copy in waits:
+        copy.wait()
+    l0, l1, l2 = Level(fine, bz, 0), Level(mid, bz // 2, 1), Level(part, z2, 2)
+    for q in range(2):
+        restrict_planes(lambda r, n, q=q: l0.get(q, r, n), l0, 0, bx // 2, l1, q, 0, tmp.at[q], 1)
+        restrict_planes(lambda r, n, q=q: l1.get(q, r, n), l1, 0, bx // 4, l2, q, 0, tmp.at[q], 2)
+    lane = lax.broadcasted_iota(jnp.int32, (z2, LANES), 1) % 4
+    for k in range(bx // 8):
+        a0, a1 = l2.get(0, 2 * k * z2, z2), l2.get(0, (2 * k + 1) * z2, z2)
+        b0, b1 = l2.get(1, 2 * k * z2, z2), l2.get(1, (2 * k + 1) * z2, z2)
+        l2.put(2, k * z2, jnp.where(lane == 0, a0, jnp.where(lane == 1, b0, jnp.where(lane == 2, a1, b1))))
+    n = bx // 8 * z2
+    mine = part[2, pl.ds(0, n), :]
+
+    def spread(i):
+        packed[pl.ds(i * n, n), :] = mine
+
+    each(devices, n, spread)
+
+
 def down_kernel(
     bx, bz, n_wide, n_narrow, own, even, odd, other, others, packed, keep0, keep1, lev0, lev1, part, tmp, sem0, sem1
 ):
@@ -283,8 +308,6 @@
     z2 = zw // 4
     n2 = k2 * z2
     l2 = Level(part, z2, 2)
-    restrict_planes(lambda r, n: l1.get(A, r, n), l1, H1, k2, l2, 1, 0, tmp.at[1], 1)
-    restrict_planes(lambda r, n: l1.get(B, r, n), l1, H1, k2, l2, 2, 0, tmp.at[0], 1)
     l1.first_cx(0)
     l1.put(CZ, 0, jnp.zeros((l1.zw, LANES), jnp.float32))
     l1.setup(1, p1 - 2, 1, valid1)
@@ -293,12 +316,8 @@
     waits.append(keep(l1, V, 0, p1, keep1, U, sem1))
     restrict_planes(lambda r, n: l1.residual(V, r, n), l1, H1, k2, l2, 0, 0, tmp.at[2], 1)
     which = lax.broadcasted_iota(jnp.int32, (z2, LANES), 1) % 4
-    fs, as_, bs = [[part[q, pl.ds(k * z2, z2), :] for k in range(4)] for q in range(3)]
-
-    def four(p):
-        return jnp.where(which == 0, p[0], jnp.where(which == 1, p[1], jnp.where(which == 2, p[2], p[3])))
-
-    parts = [four(fs), four((as_[0], bs[0], as_[1], bs[1])), four((as_[2], bs[2], as_[3], bs[3]))]
+    p = [part[0, pl.ds(k * z2, z2), :] for k in range(4)]
+    mine = jnp.where(which == 0, p[0], jnp.where(which == 1, p[1], jnp.where(which == 2, p[2], p[3])))
     z1 = l1.zw
     first = lax.broadcasted_iota(jnp.int32, (z1, LANES), 1) % 2 == 0
 
@@ -307,18 +326,17 @@
         return jnp.where(first, l1.get(V, r, z1), l1.get(V, r + z1, z1))
 
     upper, lower = face(bx // 2 - 3), face(1)
-    slot = 3 * z2 + z1
+    slot = z2 + z1
 
     def spread(i):
-        for k in range(3):
-            packed[pl.ds(i * slot + k * z2, z2), :] = parts[k]
-        packed[pl.ds(i * slot + 3 * z2, z1), :] = upper
+        packed[pl.ds(i * slot, z2), :] = mine
+        packed[pl.ds(i * slot + z2, z1), :] = upper
 
     each(n_wide, slot, spread)
 
     @pl.when(wide > 0)
     def _():
-        packed[pl.ds(pl.multiple_of((wide - 1) * slot + 3 * z2, 8), z1), :] = lower
+        packed[pl.ds(pl.multiple_of((wide - 1) * slot + z2, 8), z1), :] = lower
 
     for copy in waits:
         copy.wait()
@@ -333,7 +351,7 @@
 
 
 def up_kernel(
-    bx, bz, n_wide, n_narrow, gathered, keep0, keep1, out, lev2, lev3, lev4, lev5, lev0, lev1, near2, near3, faces, slots, tmp, sem0, sem1
+    bx, bz, n_wide, n_narrow, gathered, coarse, keep0, keep1, out, lev2, lev3, lev4, lev5, lev0, lev1, near2, near3, faces, slots, tmp, sem0, sem1
 ):
     wide = lax.axis_index("wide")
     narrow = lax.axis_index("narrow")
@@ -359,7 +377,7 @@
     l2, l3, l4, l5 = levels
     planes2 = bx // 4
     z2 = l2.zw
-    slot = 3 * z2 + z1
+    slot = z2 + z1
     lane = lax.broadcasted_iota(jnp.int32, (z2, LANES), 1) % 4
 
     def slot_of(w):
@@ -368,25 +386,39 @@
         pltpu.sync_copy(gathered.at[pl.ds(pl.multiple_of(w * slot, 8), slot)], slots)
         return slots, 0
 
+    zs = bz // 4
+    n = planes2 // 2 * zs
+    lane_ab = lax.broadcasted_iota(jnp.int32, (n, LANES), 1) % 4
+
+    def unpack_ab(i):
+        w, c = i // n_narrow, i % n_narrow
+        if big(n_wide):
+            pltpu.sync_copy(coarse.at[pl.ds(pl.multiple_of(i * n, 8), n)], slots.at[pl.ds(0, n)])
+            p = slots[pl.ds(0, n), :]
+        else:
+            p = coarse[pl.ds(i * n, n), :]
+        r = l2.base + w * planes2 * z2 + c * zs
+        for k, (q, plane) in enumerate(((A, 0), (B, 0), (A, 1), (B, 1))):
+            t = spread4(p, lane_ab, k)
+            for pair in range(planes2 // 2):
+                l2.put(q, r + (2 * pair + plane) * z2, t[pair * zs : (pair + 1) * zs])
+
+    each(n_wide * n_narrow, 32, unpack_ab)
+
     def unpack(w):
         src, at = slot_of(w)
         r = l2.base + w * planes2 * z2
-        for part, wanted in (
-            (0, ((F, 0), (F, 1), (F, 2), (F, 3))),
-            (1, ((A, 0), (B, 0), (A, 1), (B, 1))),
-            (2, ((A, 2), (B, 2), (A, 3), (B, 3))),
-        ):
-            p = src[pl.ds(at + part * z2, z2), :]
-            for k, (q, plane) in enumerate(wanted):
-                l2.put(q, r + plane * z2, spread4(p, lane, k))
-
-    each(n_wide, 12 * z2, unpack)
+        p = src[pl.ds(at, z2), :]
+        for k in range(4):
+            l2.put(F, r + k * z2, spread4(p, lane, k))
+
+    each(n_wide, 4 * z2, unpack)
     first = lax.broadcasted_iota(jnp.int32, (z1, LANES), 1) % 2 == 0
     for k, by in ((0, -1), (1, 1)):
         there = wide + by
         valid = jnp.logical_and(there >= 0, there < n_wide)
         src, at = slot_of(jnp.clip(there, 0, n_wide - 1))
-        p = jnp.where(valid, src[pl.ds(pl.multiple_of(at + 3 * z2, 8), z1), :], 0.0)
+        p = jnp.where(valid, src[pl.ds(pl.multiple_of(at + z2, 8), z1), :], 0.0)
         t = jnp.where(first, p, 0.0)
         faces[k, pl.ds(0, z1), :] = t + pltpu.roll(t, 1, 1)
         t = p - t
@@ -499,18 +531,37 @@
         functools.partial(pack_kernel, bx, bz),
         out_shape=[face, face],
         in_specs=[pl.BlockSpec(memory_space=pltpu.HBM)] * 3,
-        out_specs=[hbm] * 2,
+        out_specs=[vmem] * 2,
         scratch_shapes=[pltpu.SemaphoreType.DMA((6,))],
         compiler_params=pltpu.CompilerParams(vmem_limit_bytes=62 * 2**20),
         name="pack",
     )(flat(rhs), flat(alpha), flat(beta))
     even, odd, rhs, alpha, beta = lax.optimization_barrier((even, odd, rhs, alpha, beta))
+    devices = n_wide * n_narrow
+    n8 = bx // 8 * (bz // 4)
+    coarse = pl.pallas_call(
+        functools.partial(coarsen_kernel, bx, bz, devices),
+        out_shape=jax.ShapeDtypeStruct((devices * n8, lanes), f32),
+        in_specs=[pl.BlockSpec(memory_space=pltpu.HBM)] * 2,
+        out_specs=vmem,
+        scratch_shapes=[
+            pltpu.VMEM((2, bx * bz, lanes), f32),
+            pltpu.VMEM((2, bx * bz // 4, lanes), f32),
+            pltpu.VMEM((3, bx * bz // 16, lanes), f32),
+            pltpu.VMEM((2, bx * bz // 2, lanes), f32),
+            pltpu.SemaphoreType.DMA((2,)),
+        ],
+        compiler_params=pltpu.CompilerParams(vmem_limit_bytes=62 * 2**20),
+        name="coarsen",
+    )(flat(alpha), flat(beta))
+    coarse = lax.all_to_all(coarse, ("wide", "narrow"), 0, 0, tiled=True)
     own = jnp.concatenate([flat(rhs), flat(alpha), flat(beta)])
     even = swap(even, "wide", 0)
     odd = swap_odd(odd)
     other = from_others(own)
+    even, odd, coarse = lax.optimization_barrier((even, odd, coarse))
     others = from_others(jnp.concatenate([even, odd]))
-    slot = 3 * (zw // 4) + zw // 2
+    slot = zw // 4 + zw // 2
     scratch = [
         pltpu.VMEM((9, planes * zw, lanes), f32),
         pltpu.VMEM((9, p1 * (zw // 2), lanes), f32),
@@ -546,12 +597,12 @@
     out = pl.pallas_call(
         functools.partial(up_kernel, bx, bz, n_wide, n_narrow),
         out_shape=jax.ShapeDtypeStruct((bx * bz, lanes), f32),
-        in_specs=[hbm if big(n_wide) else vmem, hbm, hbm],
+        in_specs=[hbm if big(n_wide) else vmem] * 2 + [hbm, hbm],
         out_specs=vmem,
         scratch_shapes=scratch,
-        compiler_params=params(scratch, bx * bz + (0 if big(n_wide) else n_wide * slot)),
+        compiler_params=params(scratch, bx * bz + (0 if big(n_wide) else n_wide * slot + devices * n8)),
         name="up",
-    )(gathered, keep0, keep1)
+    )(gathered, coarse, keep0, keep1)
     return out.reshape(bx, bz, lanes)
 
 

time: 52.2 us -> 48.9 us (0.937)
  Pallas kernels: 21.2 us -> 14 us
  starting transfers between devices: 3.8 us -> 10.1 us
  blocking collectives: 21.9 us -> 17.3 us
  waiting for transfers between devices: 4.01 us -> 5.98 us
    pallas_call x1, Pallas kernels: 10.6 us -> 1.72 us  [shards(): pl.pallas_call(functools.partial(pack_kernel, bx, bz), out_shape=[face, f...]
    all_to_all x0 -> x1, starting transfers between devices: none -> 7.3 us  [shards(): coarse = lax.all_to_all(coarse, ('wide', 'narrow'), 0, 0, tiled=True)]
    all_to_all x1, blocking collectives: 21.9 us -> 17.3 us  [shards(): gathered = lax.all_to_all(packed, 'wide', 0, 0, tiled=True)]
    pallas_call x0 -> x1, Pallas kernels: none -> 1.98 us  [shards(): pl.pallas_call(functools.partial(coarsen_kernel, bx, bz, devices), out_sh...]
    ppermute x3, waiting for transfers between devices: 4.01 us -> 5.72 us  [swap(): return lax.ppermute(array, axis, [(i, i ^ 1 << bit) for i in range(n)])]
    ppermute x3, starting transfers between devices: 3.15 us -> 2.18 us  [swap(): return lax.ppermute(array, axis, [(i, i ^ 1 << bit) for i in range(n)])]
  transfers between devices with their start and end apart: 4 -> 5, of which waited for: 2 -> 3; matrix products, arithmetic and copies ran while one was open for 2% -> 2% of each run, Pallas kernels for 0% -> 0%
where the time goes in v6:
time: 48.9 us; the launch traced here: 48.6 us
  blocking collectives  17.3 us (35%)
  Pallas kernels  14 us (29%)
  starting transfers between devices  10.1 us (21%)
  waiting for transfers between devices  5.98 us (12%)
  other arithmetic  1.08 us (2%)
    all_to_all x1, blocking collectives, shards(): gathered = lax.all_to_all(packed, 'wide', 0, 0, tiled=True)  17.3 us
    all_to_all x1, starting transfers between devices, shards(): coarse = lax.all_to_all(coarse, ('wide', 'narrow'), 0, 0, tiled=True)  7.3 us
    pallas_call x1, Pallas kernels, shards(): pl.pallas_call(functools.partial(up_kernel, bx, bz, n_wide, n_narrow), ou...  5.82 us
    ppermute x3, waiting for transfers between devices, swap(): return lax.ppermute(array, axis, [(i, i ^ 1 << bit) for i in range(n)])  5.72 us
    pallas_call x1, Pallas kernels, shards(): pl.pallas_call(functools.partial(down_kernel, bx, bz, n_wide, n_narrow),...  4.51 us
    ppermute x3, starting transfers between devices, swap(): return lax.ppermute(array, axis, [(i, i ^ 1 << bit) for i in range(n)])  2.18 us
    pallas_call x1, Pallas kernels, shards(): pl.pallas_call(functools.partial(coarsen_kernel, bx, bz, devices), out_sh...  1.98 us
    pallas_call x1, Pallas kernels, shards(): pl.pallas_call(functools.partial(pack_kernel, bx, bz), out_shape=[face, f...  1.72 us
  transfers between devices with their start and end apart: 5, of which 3 were waited for; matrix products, arithmetic and copies ran while one was open for 2% of the time, Pallas kernels for 0%

profile of v6, /device:TPU:0, one launch (start us, length us, event | category | flops | bytes accessed | tf_op | source)
XLA Modules:
  0.0 48.6 jit_solution(9716557467553161928)
XLA Ops:
  0.0 1.7 %pack.1 = (f32[304,128]{1,0:T(8,128)}, f32[304,128]{1,0:T(8,128)}) custom-call(f32[256,128]{1,0:T(8,128)} %bitcast.21, f32[256,128]{1,0:T(8,128)} %bitcast.17, f32[256,128]{1,0:T(8,128)} %bitcast.14), custom_call_target="tpu_custom_call" | custom-call | tf_op jit(solution)/shard_map/pack/pallas_call | solution.py:530
  1.7 2.0 %coarsen.1 = f32[256,128]{1,0:T(8,128)} custom-call(f32[256,128]{1,0:T(8,128)} %bitcast.18, f32[256,128]{1,0:T(8,128)} %bitcast.15), custom_call_target="tpu_custom_call" | custom-call | tf_op jit(solution)/shard_map/coarsen/pallas_call | solution.py:542
  3.7 7.3 %all-to-all-start = ((f32[32,8,128]{2,1,0:T(8,128)}), f32[32,8,128]{2,1,0:T(8,128)S(1)}, u32[]{:S(2)}, u32[]{:S(2)}) async-start(f32[32,8,128]{2,1,0:T(8,128)} %bitcast.20), calls=%async_computation | async-start | bytes 262144 | tf_op jit(solution)/shard_map/all_to_all | solution.py:557
  11.0 1.8 %collective-permute-start = (f32[304,128]{1,0:T(8,128)}, f32[304,128]{1,0:T(8,128)S(1)}, u32[]{:S(2)}, u32[]{:S(2)}) collective-permute-start(f32[304,128]{1,0:T(8,128)} %get-tuple-element.23), channel_id=1, source_target_pairs={{0,2},{2,0},{4,6},{6,4},{8,10},{10,8},{12,14},{14,12},{16,18},{18,... | collective-permute-start | bytes 466952 | tf_op jit(solution)/shard_map/ppermute | solution.py:495
  12.9 0.7 %collective-permute-start.1 = (f32[304,128]{1,0:T(8,128)}, f32[304,128]{1,0:T(8,128)S(1)}, u32[]{:S(2)}, u32[]{:S(2)}) collective-permute-start(f32[304,128]{1,0:T(8,128)} %get-tuple-element.24), channel_id=1, source_target_pairs={{2,4},{6,8},{10,12},{14,16},{18,20},{22,24},{26,28},{4,2},{8,6},{1... | collective-permute-start | bytes 466952 | tf_op jit(solution)/shard_map/ppermute | solution.py:501
  13.5 1.1 %pad_maximum_fusion.own = f32[768,128]{1,0:T(8,128)S(1)} fusion(f32[256,128]{1,0:T(8,128)} %bitcast.16, f32[256,128]{1,0:T(8,128)} %bitcast.19, f32[256,128]{1,0:T(8,128)} %bitcast.22), kind=kLoop, calls=%fused_computation | loop fusion | flops 196608 | bytes 786432 | tf_op jit(solution)/shard_map/concatenate | solution.py:558
  14.6 0.1 collective-permute-start.2
  14.7 4.3 %collective-permute-done.even = f32[304,128]{1,0:T(8,128)S(1)} collective-permute-done((f32[304,128]{1,0:T(8,128)}, f32[304,128]{1,0:T(8,128)S(1)}, u32[]{:S(2)}, u32[]{:S(2)}) %collective-permute-start) | collective-permute-done | bytes 155680 | tf_op jit(solution)/shard_map/ppermute | solution.py:495
  19.0 0.0 collective-permute-done.1.odd
  19.0 0.3 all-to-all-done
  19.3 0.3 collective-permute-start.3
  19.6 0.0 collective-permute-done.2.other
  19.6 1.4 %collective-permute-done.3.others = f32[608,128]{1,0:T(8,128)S(1)} collective-permute-done((f32[608,128]{1,0:T(8,128)S(1)}, f32[608,128]{1,0:T(8,128)S(1)}, u32[]{:S(2)}, u32[]{:S(2)}) %collective-permute-start.3) | collective-permute-done | bytes 311328 | tf_op jit(solution)/shard_map/ppermute | solution.py:495
  21.0 4.5 %down.1 = (f32[384,128]{1,0:T(8,128)S(1)}, f32[6,640,128]{2,1,0:T(8,128)S(1)}, f32[6,224,128]{2,1,0:T(8,128)S(1)}) custom-call(f32[768,128]{1,0:T(8,128)S(1)} %pad_maximum_fusion.own, f32[304,128]{1,0:T(8,128)S(1)} %collective-permute-done.even, f32[304,128]{1,0:T(8,128)S(1)} %collective-permute-done.1.odd, f32[768,128]{1,0:T(8,128)S(1)} %collective-permute-done.2.other, ...), custom_call_target="tpu_custom_call" | custom-call | tf_op jit(solution)/shard_map/down/pallas_call | solution.py:572
  25.5 17.3 %all_to_all.23 = f32[16,24,128]{2,1,0:T(8,128)S(1)} all-to-all(f32[16,24,128]{2,1,0:T(8,128)S(1)} %bitcast.13), channel_id=1, replica_groups=mesh['wide'=16,'narrow'=2] {'wide'}, dimensions={0} | all-to-all | bytes 393216 | tf_op jit(solution)/shard_map/all_to_all | solution.py:581
  42.8 5.8 %up.1 = f32[256,128]{1,0:T(8,128)} custom-call(f32[384,128]{1,0:T(8,128)S(1)} %bitcast.11, f32[256,128]{1,0:T(8,128)S(1)} %bitcast.12, f32[6,640,128]{2,1,0:T(8,128)S(1)} %get-tuple-element.29.keep0, f32[6,224,128]{2,1,0:T(8,128)S(1)} %get-tuple-element.30.keep1), custom_call_target="tpu_custom_call" | custom-call | tf_op jit(solution)/shard_map/up/pallas_call | solution.py:597
  (1 shorter events, 0.0 us)
Async XLA Ops:
  3.7 15.5 %all-to-all-start = ((f32[32,8,128]{2,1,0:T(8,128)}), f32[32,8,128]{2,1,0:T(8,128)S(1)}, u32[]{:S(2)}, u32[]{:S(2)}) async-start(f32[32,8,128]{2,1,0:T(8,128)} %bitcast.20), calls=%async_computation | async-start | bytes 262144 | tf_op jit(solution)/shard_map/all_to_all | solution.py:557
  11.0 8.0 %collective-permute-start = (f32[304,128]{1,0:T(8,128)}, f32[304,128]{1,0:T(8,128)S(1)}, u32[]{:S(2)}, u32[]{:S(2)}) collective-permute-start(f32[304,128]{1,0:T(8,128)} %get-tuple-element.23), channel_id=1, source_target_pairs={{0,2},{2,0},{4,6},{6,4},{8,10},{10,8},{12,14},{14,12},{16,18},{18,... | collective-permute-start | bytes 466952 | tf_op jit(solution)/shard_map/ppermute | solution.py:495
  12.9 6.1 %collective-permute-start.1 = (f32[304,128]{1,0:T(8,128)}, f32[304,128]{1,0:T(8,128)S(1)}, u32[]{:S(2)}, u32[]{:S(2)}) collective-permute-start(f32[304,128]{1,0:T(8,128)} %get-tuple-element.24), channel_id=1, source_target_pairs={{2,4},{6,8},{10,12},{14,16},{18,20},{22,24},{26,28},{4,2},{8,6},{1... | collective-permute-start | bytes 466952 | tf_op jit(solution)/shard_map/ppermute | solution.py:501
  14.6 5.0 %collective-permute-start.2 = (f32[768,128]{1,0:T(8,128)S(1)}, f32[768,128]{1,0:T(8,128)S(1)}, u32[]{:S(2)}, u32[]{:S(2)}) collective-permute-start(f32[768,128]{1,0:T(8,128)S(1)} %pad_maximum_fusion.own), channel_id=1, source_target_pairs={{0,1},{1,0},{2,3},{3,2},{4,5},{5,4},{6,7},{7,6},{8,9},{9,8},{10,11... | collective-permute-start | bytes 1179656 | tf_op jit(solution)/shard_map/ppermute | solution.py:495
  19.3 1.7 %collective-permute-start.3 = (f32[608,128]{1,0:T(8,128)S(1)}, f32[608,128]{1,0:T(8,128)S(1)}, u32[]{:S(2)}, u32[]{:S(2)}) collective-permute-start(f32[608,128]{1,0:T(8,128)S(1)} %pad_maximum_fusion.1), channel_id=1, source_target_pairs={{0,1},{1,0},{2,3},{3,2},{4,5},{5,4},{6,7},{7,6},{8,9},{9,8},{10,11... | collective-permute-start | bytes 933896 | tf_op jit(solution)/shard_map/ppermute | solution.py:495

commit v7 on v3

--- a/solution.py
+++ b/solution.py
@@ -198,23 +198,20 @@
     return copy
 
 
-def pack_kernel(bx, bz, rhs, alpha, beta, even, odd, own, sem):
+def pack_kernel(bx, bz, rhs, alpha, beta, even, odd, sem):
     up = 1 - lax.axis_index("wide") % 2
     waits = []
-    at = [0, 0]
+    at = 0
     for q, (src, size) in enumerate(((rhs, H - 1), (alpha, H - 1), (beta, H))):
         for k, dst in enumerate((even, odd)):
             upper = up if k == 0 else 1 - up
             start = pl.multiple_of(upper * ((bx - size) * bz), 8)
             copy = pltpu.make_async_copy(
-                src.at[pl.ds(start, size * bz)], dst.at[pl.ds(at[k] * bz, size * bz)], sem.at[2 * q + k]
+                src.at[pl.ds(start, size * bz)], dst.at[pl.ds(at * bz, size * bz)], sem.at[2 * q + k]
             )
             copy.start()
             waits.append(copy)
-            at[k] += size
-        copy = pltpu.make_async_copy(src, own.at[pl.ds(q * bx * bz, bx * bz)], sem.at[6 + q])
-        copy.start()
-        waits.append(copy)
+        at += size
     for copy in waits:
         copy.wait()
 
@@ -281,8 +278,8 @@
     l1.first_cx(0)
     l1.put(CZ, 0, jnp.zeros((l1.zw, LANES), jnp.float32))
     l1.setup(1, p1 - 2, 1, valid1)
+    waits += [keep(l1, q, 0, p1, keep1, q, sem1) for q in (F, W, CX, CZ, CY)]
     l1.sweep(U, V, 2, p1 - 4, 1)
-    waits += [keep(l1, q, 0, p1, keep1, q, sem1) for q in (F, W, CX, CZ, CY)]
     waits.append(keep(l1, V, 0, p1, keep1, U, sem1))
     n1 = 2 * l1.zw
     upper, lower = H1 + bx // 2 - 3, H1 + 1
@@ -452,15 +449,17 @@
         return pltpu.CompilerParams(vmem_limit_bytes=min(255 * 2**18, size + size // 8 + 2**21))
 
     face = jax.ShapeDtypeStruct(((3 * H - 2) * bz, lanes), f32)
-    even, odd, own = pl.pallas_call(
+    even, odd = pl.pallas_call(
         functools.partial(pack_kernel, bx, bz),
-        out_shape=[face, face, jax.ShapeDtypeStruct((3 * bx * bz, lanes), f32)],
+        out_shape=[face, face],
         in_specs=[pl.BlockSpec(memory_space=pltpu.HBM)] * 3,
-        out_specs=[vmem] * 3,
-        scratch_shapes=[pltpu.SemaphoreType.DMA((9,))],
+        out_specs=[vmem] * 2,
+        scratch_shapes=[pltpu.SemaphoreType.DMA((6,))],
         compiler_params=pltpu.CompilerParams(vmem_limit_bytes=62 * 2**20),
         name="pack",
     )(flat(rhs), flat(alpha), flat(beta))
+    even, odd, rhs, alpha, beta = lax.optimization_barrier((even, odd, rhs, alpha, beta))
+    own = jnp.concatenate([flat(rhs), flat(alpha), flat(beta)])
     even = swap(even, "wide", 0)
     odd = swap_odd(odd)
     other = from_others(own)

time: 43.7 us -> 42.2 us (0.966)
  waiting for transfers between devices: 13.2 us -> 12.1 us
  other arithmetic: 0.02 us -> 1.08 us
  local copies, waits for them, and re-layouts: 1 us -> 0 us
  Pallas kernels: 13.5 us -> 12.9 us
    ppermute x4, waiting for transfers between devices: 6.52 us -> 5.45 us  [swap(): return lax.ppermute(array, axis, [(i, i ^ 1 << bit) for i in range(n)])]
    concatenate x0 -> x1, other arithmetic: none -> 1.06 us  [shards(): own = jnp.concatenate([flat(rhs), flat(alpha), flat(beta)])]
    unnamed x2 -> x0, local copies, waits for them, and re-layouts: 1 us -> none
  transfers between devices with their start and end apart: 7 -> 7, of which waited for: 4 -> 4; matrix products, arithmetic and copies ran while one was open for 0% -> 3% of each run, Pallas kernels for 0% -> 0%
where the time goes in v7:
time: 42.2 us; the launch traced here: 41.9 us
  starting transfers between devices  15.7 us (37%)
  Pallas kernels  12.9 us (31%)
  waiting for transfers between devices  12.1 us (29%)
  other arithmetic  1.08 us (3%)
    all_to_all x1, starting transfers between devices, shards(): gathered = lax.all_to_all(packed, ('wide', 'narrow'), 0, 0, tiled=True)  9.44 us
    all_to_all x1, waiting for transfers between devices, shards(): gathered = lax.all_to_all(packed, ('wide', 'narrow'), 0, 0, tiled=True)  6.66 us
    pallas_call x1, Pallas kernels, shards(): pl.pallas_call(functools.partial(up_kernel, bx, bz, n_wide, n_narrow), ou...  5.77 us
    pallas_call x1, Pallas kernels, shards(): pl.pallas_call(functools.partial(down_kernel, bx, bz, n_wide, n_narrow),...  5.46 us
    ppermute x4, waiting for transfers between devices, swap(): return lax.ppermute(array, axis, [(i, i ^ 1 << bit) for i in range(n)])  5.45 us
    ppermute x4, starting transfers between devices, swap(): return lax.ppermute(array, axis, [(i, i ^ 1 << bit) for i in range(n)])  4.98 us
    pallas_call x1, Pallas kernels, shards(): pl.pallas_call(functools.partial(pack_kernel, bx, bz), out_shape=[face, f...  1.7 us
    ppermute x2, starting transfers between devices, swap_odd(): return lax.ppermute(array, 'wide', pairs + [(j, i) for i, j in pairs])  1.31 us
  transfers between devices with their start and end apart: 7, of which 4 were waited for; matrix products, arithmetic and copies ran while one was open for 3% of the time, Pallas kernels for 0%

profile of v7, /device:TPU:0, one launch (start us, length us, event | category | flops | bytes accessed | tf_op | source)
XLA Modules:
  0.0 41.9 jit_solution(17053352375678835499)
XLA Ops:
  0.0 1.7 %pack.1 = (f32[304,128]{1,0:T(8,128)}, f32[304,128]{1,0:T(8,128)}) custom-call(f32[256,128]{1,0:T(8,128)} %bitcast.14, f32[256,128]{1,0:T(8,128)} %bitcast.12, f32[256,128]{1,0:T(8,128)} %bitcast.10), custom_call_target="tpu_custom_call" | custom-call | tf_op jit(solution)/shard_map/pack/pallas_call | solution.py:452
  1.7 3.0 %collective-permute-start = (f32[304,128]{1,0:T(8,128)}, f32[304,128]{1,0:T(8,128)S(1)}, u32[]{:S(2)}, u32[]{:S(2)}) collective-permute-start(f32[304,128]{1,0:T(8,128)} %get-tuple-element.22), channel_id=1, source_target_pairs={{0,2},{2,0},{4,6},{6,4},{8,10},{10,8},{12,14},{14,12},{16,18},{18,... | collective-permute-start | bytes 466952 | tf_op jit(solution)/shard_map/ppermute | solution.py:416
  4.7 0.7 %collective-permute-start.1 = (f32[304,128]{1,0:T(8,128)}, f32[304,128]{1,0:T(8,128)S(1)}, u32[]{:S(2)}, u32[]{:S(2)}) collective-permute-start(f32[304,128]{1,0:T(8,128)} %get-tuple-element.23), channel_id=1, source_target_pairs={{2,4},{6,8},{10,12},{14,16},{18,20},{22,24},{26,28},{4,2},{8,6},{1... | collective-permute-start | bytes 466952 | tf_op jit(solution)/shard_map/ppermute | solution.py:422
  5.4 1.1 %pad_maximum_fusion.own = f32[768,128]{1,0:T(8,128)S(1)} fusion(f32[256,128]{1,0:T(8,128)} %bitcast.11, f32[256,128]{1,0:T(8,128)} %bitcast.13, f32[256,128]{1,0:T(8,128)} %bitcast.15), kind=kLoop, calls=%fused_computation | loop fusion | flops 196608 | bytes 786432 | tf_op jit(solution)/shard_map/concatenate | solution.py:462
  6.4 0.1 collective-permute-start.2
  6.5 2.4 %collective-permute-done.even = f32[304,128]{1,0:T(8,128)S(1)} collective-permute-done((f32[304,128]{1,0:T(8,128)}, f32[304,128]{1,0:T(8,128)S(1)}, u32[]{:S(2)}, u32[]{:S(2)}) %collective-permute-start) | collective-permute-done | bytes 155680 | tf_op jit(solution)/shard_map/ppermute | solution.py:416
  8.9 0.0 collective-permute-done.1.odd
  9.0 0.1 collective-permute-start.3
  9.1 0.0 collective-permute-done.2.other
  9.1 1.6 %collective-permute-done.3.others = f32[608,128]{1,0:T(8,128)S(1)} collective-permute-done((f32[608,128]{1,0:T(8,128)S(1)}, f32[608,128]{1,0:T(8,128)S(1)}, u32[]{:S(2)}, u32[]{:S(2)}) %collective-permute-start.3) | collective-permute-done | bytes 311328 | tf_op jit(solution)/shard_map/ppermute | solution.py:416
  10.7 5.5 %down.1 = (f32[512,128]{1,0:T(8,128)}, f32[32,128]{1,0:T(8,128)S(1)}, f32[32,128]{1,0:T(8,128)S(1)}, f32[6,640,128]{2,1,0:T(8,128)S(1)}, f32[6,224,128]{2,1,0:T(8,128)S(1)}) custom-call(f32[768,128]{1,0:T(8,128)S(1)} %pad_maximum_fusion.own, f32[304,128]{1,0:T(8,128)S(1)} %collective-permute-done.even, f32[304,128]{1,0:T(8,128)S(1)} %collective-permute-done.1.odd, ...), custom_call_target="tpu_custom_call" | custom-call | tf_op jit(solution)/shard_map/down/pallas_call | solution.py:474
  16.1 9.4 %all-to-all-start = ((f32[32,16,128]{2,1,0:T(8,128)}), f32[32,16,128]{2,1,0:T(8,128)S(1)}, u32[]{:S(2)}, u32[]{:S(2)}) async-start(f32[32,16,128]{2,1,0:T(8,128)} %bitcast.6), calls=%async_computation | async-start | bytes 524288 | tf_op jit(solution)/shard_map/all_to_all | solution.py:484
  25.6 1.8 %collective-permute-start.4 = (f32[32,128]{1,0:T(8,128)S(1)}, f32[32,128]{1,0:T(8,128)S(1)}, u32[]{:S(2)}, u32[]{:S(2)}) collective-permute-start(f32[32,128]{1,0:T(8,128)S(1)} %get-tuple-element.25), channel_id=1, source_target_pairs={{0,2},{2,0},{4,6},{6,4},{8,10},{10,8},{12,14},{14,12},{16,18},{18,... | collective-permute-start | bytes 49160 | tf_op jit(solution)/shard_map/ppermute | solution.py:416
  27.4 0.7 %collective-permute-start.5 = (f32[32,128]{1,0:T(8,128)S(1)}, f32[32,128]{1,0:T(8,128)S(1)}, u32[]{:S(2)}, u32[]{:S(2)}) collective-permute-start(f32[32,128]{1,0:T(8,128)S(1)} %get-tuple-element.26), channel_id=1, source_target_pairs={{2,4},{6,8},{10,12},{14,16},{18,20},{22,24},{26,28},{4,2},{8,6},{1... | collective-permute-start | bytes 49160 | tf_op jit(solution)/shard_map/ppermute | solution.py:422
  28.1 1.4 %collective-permute-done.4.heven = f32[32,128]{1,0:T(8,128)S(1)} collective-permute-done((f32[32,128]{1,0:T(8,128)S(1)}, f32[32,128]{1,0:T(8,128)S(1)}, u32[]{:S(2)}, u32[]{:S(2)}) %collective-permute-start.4) | collective-permute-done | bytes 16416 | tf_op jit(solution)/shard_map/ppermute | solution.py:416
  29.5 0.0 collective-permute-done.5.hodd
  29.5 6.7 %all-to-all-done = f32[32,16,128]{2,1,0:T(8,128)S(1)} async-done(((f32[32,16,128]{2,1,0:T(8,128)}), f32[32,16,128]{2,1,0:T(8,128)S(1)}, u32[]{:S(2)}, u32[]{:S(2)}) %all-to-all-start) | async-done | bytes 262176 | tf_op jit(solution)/shard_map/all_to_all | solution.py:484
  36.2 5.8 %up.1 = f32[256,128]{1,0:T(8,128)} custom-call(f32[512,128]{1,0:T(8,128)S(1)} %bitcast.9, f32[32,128]{1,0:T(8,128)S(1)} %collective-permute-done.4.heven, f32[32,128]{1,0:T(8,128)S(1)} %collective-permute-done.5.hodd, f32[6,640,128]{2,1,0:T(8,128)S(1)} %get-tuple-element.27.keep0, f32[6,224,128]{2,1,0:T(8,128)S(1)} %get-tuple-element.28.keep1), custom_call_target="tpu_custom_call" | custom-call | tf_op jit(solution)/shard_map/up/pallas_call | solution.py:498
  (1 shorter events, 0.0 us)
Async XLA Ops:
  1.7 7.2 %collective-permute-start = (f32[304,128]{1,0:T(8,128)}, f32[304,128]{1,0:T(8,128)S(1)}, u32[]{:S(2)}, u32[]{:S(2)}) collective-permute-start(f32[304,128]{1,0:T(8,128)} %get-tuple-element.22), channel_id=1, source_target_pairs={{0,2},{2,0},{4,6},{6,4},{8,10},{10,8},{12,14},{14,12},{16,18},{18,... | collective-permute-start | bytes 466952 | tf_op jit(solution)/shard_map/ppermute | solution.py:416
  4.7 4.2 %collective-permute-start.1 = (f32[304,128]{1,0:T(8,128)}, f32[304,128]{1,0:T(8,128)S(1)}, u32[]{:S(2)}, u32[]{:S(2)}) collective-permute-start(f32[304,128]{1,0:T(8,128)} %get-tuple-element.23), channel_id=1, source_target_pairs={{2,4},{6,8},{10,12},{14,16},{18,20},{22,24},{26,28},{4,2},{8,6},{1... | collective-permute-start | bytes 466952 | tf_op jit(solution)/shard_map/ppermute | solution.py:422
  6.4 2.6 %collective-permute-start.2 = (f32[768,128]{1,0:T(8,128)S(1)}, f32[768,128]{1,0:T(8,128)S(1)}, u32[]{:S(2)}, u32[]{:S(2)}) collective-permute-start(f32[768,128]{1,0:T(8,128)S(1)} %pad_maximum_fusion.own), channel_id=1, source_target_pairs={{0,1},{1,0},{2,3},{3,2},{4,5},{5,4},{6,7},{7,6},{8,9},{9,8},{10,11... | collective-permute-start | bytes 1179656 | tf_op jit(solution)/shard_map/ppermute | solution.py:416
  9.0 1.7 %collective-permute-start.3 = (f32[608,128]{1,0:T(8,128)S(1)}, f32[608,128]{1,0:T(8,128)S(1)}, u32[]{:S(2)}, u32[]{:S(2)}) collective-permute-start(f32[608,128]{1,0:T(8,128)S(1)} %pad_maximum_fusion.1), channel_id=1, source_target_pairs={{0,1},{1,0},{2,3},{3,2},{4,5},{5,4},{6,7},{7,6},{8,9},{9,8},{10,11... | collective-permute-start | bytes 933896 | tf_op jit(solution)/shard_map/ppermute | solution.py:416
  16.1 20.0 %all-to-all-start = ((f32[32,16,128]{2,1,0:T(8,128)}), f32[32,16,128]{2,1,0:T(8,128)S(1)}, u32[]{:S(2)}, u32[]{:S(2)}) async-start(f32[32,16,128]{2,1,0:T(8,128)} %bitcast.6), calls=%async_computation | async-start | bytes 524288 | tf_op jit(solution)/shard_map/all_to_all | solution.py:484
  25.6 3.9 %collective-permute-start.4 = (f32[32,128]{1,0:T(8,128)S(1)}, f32[32,128]{1,0:T(8,128)S(1)}, u32[]{:S(2)}, u32[]{:S(2)}) collective-permute-start(f32[32,128]{1,0:T(8,128)S(1)} %get-tuple-element.25), channel_id=1, source_target_pairs={{0,2},{2,0},{4,6},{6,4},{8,10},{10,8},{12,14},{14,12},{16,18},{18,... | collective-permute-start | bytes 49160 | tf_op jit(solution)/shard_map/ppermute | solution.py:416
  27.4 2.1 %collective-permute-start.5 = (f32[32,128]{1,0:T(8,128)S(1)}, f32[32,128]{1,0:T(8,128)S(1)}, u32[]{:S(2)}, u32[]{:S(2)}) collective-permute-start(f32[32,128]{1,0:T(8,128)S(1)} %get-tuple-element.26), channel_id=1, source_target_pairs={{2,4},{6,8},{10,12},{14,16},{18,20},{22,24},{26,28},{4,2},{8,6},{1... | collective-permute-start | bytes 49160 | tf_op jit(solution)/shard_map/ppermute | solution.py:422

commit v8 on v7

--- a/solution.py
+++ b/solution.py
@@ -216,6 +216,12 @@
         copy.wait()
 
 
+def spread4(p, lane, k):
+    t = jnp.where(lane == k, p, 0.0)
+    t = t + pltpu.roll(t, 1 if k % 2 == 0 else LANES - 1, 1)
+    return t + pltpu.roll(t, 2 if k < 2 else LANES - 2, 1)
+
+
 def down_kernel(
     bx, bz, n_wide, n_narrow, own, even, odd, other, others, packed, ueven, uodd, keep0, keep1, lev0, lev1, part, tmp, sem0, sem1
 ):
@@ -283,18 +289,23 @@
     waits.append(keep(l1, V, 0, p1, keep1, U, sem1))
     n1 = 2 * l1.zw
     upper, lower = H1 + bx // 2 - 3, H1 + 1
-    ueven[...] = l1.get(V, pl.multiple_of((up * upper + (1 - up) * lower) * l1.zw, 8), n1)
-    uodd[...] = l1.get(V, pl.multiple_of(((1 - up) * upper + up * lower) * l1.zw, 8), n1)
+    above, below = l1.get(V, upper * l1.zw, n1), l1.get(V, lower * l1.zw, n1)
+    ueven[...] = jnp.where(up == 1, above, below)
+    uodd[...] = jnp.where(up == 1, below, above)
     restrict_planes(lambda r, n: l1.residual(V, r, n), l1, H1, k2, l2, 0, 0, tmp.at[2], 1)
-    which = lax.broadcasted_iota(jnp.int32, (n2, LANES), 1) % 4
-    part[0] = jnp.where(which == 0, part[0], jnp.where(which == 1, part[1], part[2]))
-    share = n2 // n_narrow
-    mine = part[0, pl.ds(pl.multiple_of(narrow * share, 8), share), :]
+    which = lax.broadcasted_iota(jnp.int32, (z2, LANES), 1) % 4
+    fs, as_, bs = [[part[q, pl.ds(k * z2, z2), :] for k in range(4)] for q in range(3)]
+
+    def four(p):
+        return jnp.where(which == 0, p[0], jnp.where(which == 1, p[1], jnp.where(which == 2, p[2], p[3])))
+
+    parts = [four(fs), four((as_[0], bs[0], as_[1], bs[1])), four((as_[2], bs[2], as_[3], bs[3]))]
 
     def spread(i):
-        packed[pl.ds(i * share, share), :] = mine
-
-    each(n_wide * n_narrow, share, spread)
+        for k in range(3):
+            packed[pl.ds((3 * i + k) * z2, z2), :] = parts[k]
+
+    each(n_wide, 3 * z2, spread)
     for copy in waits:
         copy.wait()
 
@@ -329,19 +340,21 @@
             level.put(q, m + level.nx * zl, zero)
     l2, l3, l4, l5 = levels
     planes2 = bx // 4
-    n2 = planes2 * l2.zw
-    n = n2 // n_narrow
-    lane = lax.broadcasted_iota(jnp.int32, (n, LANES), 1) % 4
-
-    def unpack(i):
-        p = gathered[pl.ds(i * n, n), :]
-        for q, k, first, second in ((F, 0, 1, 2), (A, 1, LANES - 1, 2), (B, 2, 1, LANES - 2)):
-            t = jnp.where(lane == k, p, 0.0)
-            t = t + pltpu.roll(t, first, 1)
-            t = t + pltpu.roll(t, second, 1)
-            l2.put(q, l2.base + i * n, t)
-
-    each(n_wide * n_narrow, n, unpack)
+    z2 = l2.zw
+    lane = lax.broadcasted_iota(jnp.int32, (z2, LANES), 1) % 4
+
+    def unpack(w):
+        r = l2.base + w * planes2 * z2
+        for part, wanted in (
+            (0, ((F, 0), (F, 1), (F, 2), (F, 3))),
+            (1, ((A, 0), (B, 0), (A, 1), (B, 1))),
+            (2, ((A, 2), (B, 2), (A, 3), (B, 3))),
+        ):
+            p = gathered[pl.ds((3 * w + part) * z2, z2), :]
+            for k, (q, plane) in enumerate(wanted):
+                l2.put(q, r + plane * z2, spread4(p, lane, k))
+
+    each(n_wide, 12 * z2, unpack)
 
     def chunk_of(level):
         return max(1, min(32 // level.zw, level.nx))
@@ -473,7 +486,7 @@
     ]
     packed, ueven, uodd, keep0, keep1 = pl.pallas_call(
         functools.partial(down_kernel, bx, bz, n_wide, n_narrow),
-        out_shape=[jax.ShapeDtypeStruct((n_wide * n2, lanes), f32), u_face, u_face, keep0, keep1],
+        out_shape=[jax.ShapeDtypeStruct((n_wide * 3 * (zw // 4), lanes), f32), u_face, u_face, keep0, keep1],
         in_specs=[vmem] * 5,
         out_specs=[vmem, vmem, vmem, hbm, hbm],
         scratch_shapes=scratch,
@@ -481,7 +494,7 @@
         name="down",
     )(own, even, odd, other, others)
     heven, hodd = swap(ueven, "wide", 0), swap_odd(uodd)
-    gathered = lax.all_to_all(packed, ("wide", "narrow"), 0, 0, tiled=True)
+    gathered = lax.all_to_all(packed, "wide", 0, 0, tiled=True)
     nx = n_wide * bx
     scratch = []
     for index in range(2, LEVELS):

time: 42.2 us -> 41.6 us (0.986)
  waiting for transfers between devices: 12.1 us -> 10.4 us
  starting transfers between devices: 15.7 us -> 16.8 us
    all_to_all x1, waiting for transfers between devices: 6.66 us -> 4.57 us  [shards(): gathered = lax.all_to_all(packed, 'wide', 0, 0, tiled=True)]
    all_to_all x1, starting transfers between devices: 9.44 us -> 10.5 us  [shards(): gathered = lax.all_to_all(packed, 'wide', 0, 0, tiled=True)]
where the time goes in v8:
time: 41.6 us; the launch traced here: 41.3 us
  starting transfers between devices  16.8 us (40%)
  Pallas kernels  12.9 us (31%)
  waiting for transfers between devices  10.4 us (25%)
  other arithmetic  1.08 us (3%)
    all_to_all x1, starting transfers between devices, shards(): gathered = lax.all_to_all(packed, 'wide', 0, 0, tiled=True)  10.5 us
    ppermute x4, waiting for transfers between devices, swap(): return lax.ppermute(array, axis, [(i, i ^ 1 << bit) for i in range(n)])  5.8 us
    pallas_call x1, Pallas kernels, shards(): pl.pallas_call(functools.partial(up_kernel, bx, bz, n_wide, n_narrow), ou...  5.77 us
    pallas_call x1, Pallas kernels, shards(): pl.pallas_call(functools.partial(down_kernel, bx, bz, n_wide, n_narrow),...  5.42 us
    ppermute x4, starting transfers between devices, swap(): return lax.ppermute(array, axis, [(i, i ^ 1 << bit) for i in range(n)])  5.07 us
    all_to_all x1, waiting for transfers between devices, shards(): gathered = lax.all_to_all(packed, 'wide', 0, 0, tiled=True)  4.57 us
    pallas_call x1, Pallas kernels, shards(): pl.pallas_call(functools.partial(pack_kernel, bx, bz), out_shape=[face, f...  1.7 us
    ppermute x2, starting transfers between devices, swap_odd(): return lax.ppermute(array, 'wide', pairs + [(j, i) for i, j in pairs])  1.31 us
  transfers between devices with their start and end apart: 7, of which 4 were waited for; matrix products, arithmetic and copies ran while one was open for 3% of the time, Pallas kernels for 0%

profile of v8, /device:TPU:0, one launch (start us, length us, event | category | flops | bytes accessed | tf_op | source)
XLA Modules:
  0.0 41.3 jit_solution(7958409023388204294)
XLA Ops:
  0.0 1.7 %pack.1 = (f32[304,128]{1,0:T(8,128)}, f32[304,128]{1,0:T(8,128)}) custom-call(f32[256,128]{1,0:T(8,128)} %bitcast.14, f32[256,128]{1,0:T(8,128)} %bitcast.12, f32[256,128]{1,0:T(8,128)} %bitcast.10), custom_call_target="tpu_custom_call" | custom-call | tf_op jit(solution)/shard_map/pack/pallas_call | solution.py:465
  1.7 3.0 %collective-permute-start = (f32[304,128]{1,0:T(8,128)}, f32[304,128]{1,0:T(8,128)S(1)}, u32[]{:S(2)}, u32[]{:S(2)}) collective-permute-start(f32[304,128]{1,0:T(8,128)} %get-tuple-element.22), channel_id=1, source_target_pairs={{0,2},{2,0},{4,6},{6,4},{8,10},{10,8},{12,14},{14,12},{16,18},{18,... | collective-permute-start | bytes 466952 | tf_op jit(solution)/shard_map/ppermute | solution.py:429
  4.7 0.7 %collective-permute-start.1 = (f32[304,128]{1,0:T(8,128)}, f32[304,128]{1,0:T(8,128)S(1)}, u32[]{:S(2)}, u32[]{:S(2)}) collective-permute-start(f32[304,128]{1,0:T(8,128)} %get-tuple-element.23), channel_id=1, source_target_pairs={{2,4},{6,8},{10,12},{14,16},{18,20},{22,24},{26,28},{4,2},{8,6},{1... | collective-permute-start | bytes 466952 | tf_op jit(solution)/shard_map/ppermute | solution.py:435
  5.4 1.1 %pad_maximum_fusion.own = f32[768,128]{1,0:T(8,128)S(1)} fusion(f32[256,128]{1,0:T(8,128)} %bitcast.11, f32[256,128]{1,0:T(8,128)} %bitcast.13, f32[256,128]{1,0:T(8,128)} %bitcast.15), kind=kLoop, calls=%fused_computation | loop fusion | flops 196608 | bytes 786432 | tf_op jit(solution)/shard_map/concatenate | solution.py:475
  6.4 0.1 collective-permute-start.2
  6.5 2.4 %collective-permute-done.even = f32[304,128]{1,0:T(8,128)S(1)} collective-permute-done((f32[304,128]{1,0:T(8,128)}, f32[304,128]{1,0:T(8,128)S(1)}, u32[]{:S(2)}, u32[]{:S(2)}) %collective-permute-start) | collective-permute-done | bytes 155680 | tf_op jit(solution)/shard_map/ppermute | solution.py:429
  8.9 0.0 collective-permute-done.1.odd
  9.0 0.1 collective-permute-start.3
  9.1 0.0 collective-permute-done.2.other
  9.1 1.6 %collective-permute-done.3.others = f32[608,128]{1,0:T(8,128)S(1)} collective-permute-done((f32[608,128]{1,0:T(8,128)S(1)}, f32[608,128]{1,0:T(8,128)S(1)}, u32[]{:S(2)}, u32[]{:S(2)}) %collective-permute-start.3) | collective-permute-done | bytes 311328 | tf_op jit(solution)/shard_map/ppermute | solution.py:429
  10.7 5.4 %down.1 = (f32[384,128]{1,0:T(8,128)}, f32[32,128]{1,0:T(8,128)S(1)}, f32[32,128]{1,0:T(8,128)S(1)}, f32[6,640,128]{2,1,0:T(8,128)S(1)}, f32[6,224,128]{2,1,0:T(8,128)S(1)}) custom-call(f32[768,128]{1,0:T(8,128)S(1)} %pad_maximum_fusion.own, f32[304,128]{1,0:T(8,128)S(1)} %collective-permute-done.even, f32[304,128]{1,0:T(8,128)S(1)} %collective-permute-done.1.odd, ...), custom_call_target="tpu_custom_call" | custom-call | tf_op jit(solution)/shard_map/down/pallas_call | solution.py:487
  16.1 10.5 %all-to-all-start = ((f32[16,24,128]{2,1,0:T(8,128)}), f32[16,24,128]{2,1,0:T(8,128)S(1)}, u32[]{:S(2)}, u32[]{:S(2)}) async-start(f32[16,24,128]{2,1,0:T(8,128)} %bitcast.6), calls=%async_computation | async-start | bytes 393216 | tf_op jit(solution)/shard_map/all_to_all | solution.py:497
  26.5 1.9 %collective-permute-start.4 = (f32[32,128]{1,0:T(8,128)S(1)}, f32[32,128]{1,0:T(8,128)S(1)}, u32[]{:S(2)}, u32[]{:S(2)}) collective-permute-start(f32[32,128]{1,0:T(8,128)S(1)} %get-tuple-element.25), channel_id=1, source_target_pairs={{0,2},{2,0},{4,6},{6,4},{8,10},{10,8},{12,14},{14,12},{16,18},{18,... | collective-permute-start | bytes 49160 | tf_op jit(solution)/shard_map/ppermute | solution.py:429
  28.5 0.7 %collective-permute-start.5 = (f32[32,128]{1,0:T(8,128)S(1)}, f32[32,128]{1,0:T(8,128)S(1)}, u32[]{:S(2)}, u32[]{:S(2)}) collective-permute-start(f32[32,128]{1,0:T(8,128)S(1)} %get-tuple-element.26), channel_id=1, source_target_pairs={{2,4},{6,8},{10,12},{14,16},{18,20},{22,24},{26,28},{4,2},{8,6},{1... | collective-permute-start | bytes 49160 | tf_op jit(solution)/shard_map/ppermute | solution.py:435
  29.1 1.8 %collective-permute-done.4.heven = f32[32,128]{1,0:T(8,128)S(1)} collective-permute-done((f32[32,128]{1,0:T(8,128)S(1)}, f32[32,128]{1,0:T(8,128)S(1)}, u32[]{:S(2)}, u32[]{:S(2)}) %collective-permute-start.4) | collective-permute-done | bytes 16416 | tf_op jit(solution)/shard_map/ppermute | solution.py:429
  30.9 0.0 collective-permute-done.5.hodd
  30.9 4.6 %all-to-all-done = f32[16,24,128]{2,1,0:T(8,128)S(1)} async-done(((f32[16,24,128]{2,1,0:T(8,128)}), f32[16,24,128]{2,1,0:T(8,128)S(1)}, u32[]{:S(2)}, u32[]{:S(2)}) %all-to-all-start) | async-done | bytes 196640 | tf_op jit(solution)/shard_map/all_to_all | solution.py:497
  35.5 5.8 %up.1 = f32[256,128]{1,0:T(8,128)} custom-call(f32[384,128]{1,0:T(8,128)S(1)} %bitcast.9, f32[32,128]{1,0:T(8,128)S(1)} %collective-permute-done.4.heven, f32[32,128]{1,0:T(8,128)S(1)} %collective-permute-done.5.hodd, f32[6,640,128]{2,1,0:T(8,128)S(1)} %get-tuple-element.27.keep0, f32[6,224,128]{2,1,0:T(8,128)S(1)} %get-tuple-element.28.keep1), custom_call_target="tpu_custom_call" | custom-call | tf_op jit(solution)/shard_map/up/pallas_call | solution.py:511
  (1 shorter events, 0.0 us)
Async XLA Ops:
  1.7 7.2 %collective-permute-start = (f32[304,128]{1,0:T(8,128)}, f32[304,128]{1,0:T(8,128)S(1)}, u32[]{:S(2)}, u32[]{:S(2)}) collective-permute-start(f32[304,128]{1,0:T(8,128)} %get-tuple-element.22), channel_id=1, source_target_pairs={{0,2},{2,0},{4,6},{6,4},{8,10},{10,8},{12,14},{14,12},{16,18},{18,... | collective-permute-start | bytes 466952 | tf_op jit(solution)/shard_map/ppermute | solution.py:429
  4.7 4.2 %collective-permute-start.1 = (f32[304,128]{1,0:T(8,128)}, f32[304,128]{1,0:T(8,128)S(1)}, u32[]{:S(2)}, u32[]{:S(2)}) collective-permute-start(f32[304,128]{1,0:T(8,128)} %get-tuple-element.23), channel_id=1, source_target_pairs={{2,4},{6,8},{10,12},{14,16},{18,20},{22,24},{26,28},{4,2},{8,6},{1... | collective-permute-start | bytes 466952 | tf_op jit(solution)/shard_map/ppermute | solution.py:435
  6.4 2.6 %collective-permute-start.2 = (f32[768,128]{1,0:T(8,128)S(1)}, f32[768,128]{1,0:T(8,128)S(1)}, u32[]{:S(2)}, u32[]{:S(2)}) collective-permute-start(f32[768,128]{1,0:T(8,128)S(1)} %pad_maximum_fusion.own), channel_id=1, source_target_pairs={{0,1},{1,0},{2,3},{3,2},{4,5},{5,4},{6,7},{7,6},{8,9},{9,8},{10,11... | collective-permute-start | bytes 1179656 | tf_op jit(solution)/shard_map/ppermute | solution.py:429
  9.0 1.7 %collective-permute-start.3 = (f32[608,128]{1,0:T(8,128)S(1)}, f32[608,128]{1,0:T(8,128)S(1)}, u32[]{:S(2)}, u32[]{:S(2)}) collective-permute-start(f32[608,128]{1,0:T(8,128)S(1)} %pad_maximum_fusion.1), channel_id=1, source_target_pairs={{0,1},{1,0},{2,3},{3,2},{4,5},{5,4},{6,7},{7,6},{8,9},{9,8},{10,11... | collective-permute-start | bytes 933896 | tf_op jit(solution)/shard_map/ppermute | solution.py:429
  16.1 19.4 %all-to-all-start = ((f32[16,24,128]{2,1,0:T(8,128)}), f32[16,24,128]{2,1,0:T(8,128)S(1)}, u32[]{:S(2)}, u32[]{:S(2)}) async-start(f32[16,24,128]{2,1,0:T(8,128)} %bitcast.6), calls=%async_computation | async-start | bytes 393216 | tf_op jit(solution)/shard_map/all_to_all | solution.py:497
  26.5 4.4 %collective-permute-start.4 = (f32[32,128]{1,0:T(8,128)S(1)}, f32[32,128]{1,0:T(8,128)S(1)}, u32[]{:S(2)}, u32[]{:S(2)}) collective-permute-start(f32[32,128]{1,0:T(8,128)S(1)} %get-tuple-element.25), channel_id=1, source_target_pairs={{0,2},{2,0},{4,6},{6,4},{8,10},{10,8},{12,14},{14,12},{16,18},{18,... | collective-permute-start | bytes 49160 | tf_op jit(solution)/shard_map/ppermute | solution.py:429
  28.5 2.4 %collective-permute-start.5 = (f32[32,128]{1,0:T(8,128)S(1)}, f32[32,128]{1,0:T(8,128)S(1)}, u32[]{:S(2)}, u32[]{:S(2)}) collective-permute-start(f32[32,128]{1,0:T(8,128)S(1)} %get-tuple-element.26), channel_id=1, source_target_pairs={{2,4},{6,8},{10,12},{14,16},{18,20},{22,24},{26,28},{4,2},{8,6},{1... | collective-permute-start | bytes 49160 | tf_op jit(solution)/shard_map/ppermute | solution.py:435
